TPU v7x, 32 devices: a whole 2x2x4 slice. The times are simulated.
32 devices in a mesh: rows: 8 (over z, y), px: 4 (over x, core).
Axes of the slice: x: 2, y: 2, z: 4, core: 2. Of those that a mesh axis runs over, the one named last changes fastest.
Arguments:
- queries: float32 [8, 65536], P(None, 'rows'), may hold values from -6 to 6
- pixel_mean: float32 [65536], P('rows'), may hold values from -3 to 3
- eigenbasis: bfloat16 [65536, 4096], P('rows', 'px'), may hold values from -0.0234375 to 0.0234375
- eigenvalues: float32 [4096], P('px'), may hold values from 0.05 to 5
- level_ids: int32 [5, 8], replicated, may hold values from 0 to 63
- slab: bfloat16 [4096, 65536], P('rows', 'px'), may hold values from -16 to 16
- slab_classes: int32 [4096], P('rows'), may hold values from 0 to 9
- target_categories: int32 [8], replicated, may hold values from 0 to 9
Outputs:
- denoised: float32 [8, 65536], P(None, 'px')
All inputs are finite; a program needn't handle non-finite values.
Results may differ from a plain program's by a relative error of at most 0.0005.
Values sent between devices are 32-bit elements; how exact they have to be, the bound alone decides.
No kernel may reach another device: no remote copies, remote signals or barrier semaphores. Data moves between devices by JAX's collectives and lax.ppermute only.
A program may use at most 128 MiB of HBM per device.

v0:
```python
import math

import jax
import jax.numpy as jnp
from jax import lax
from jax.sharding import PartitionSpec as P

IMAGE_POINTS = 65536
LEVELS = 64


steering_strength = 1.5
rms_epsilon = 1e-06


def merged(x, axis, combine):
    everything = jax.tree.map(lambda part: lax.all_gather(part, axis), x)
    first = jax.tree.map(lambda part: part[0], everything)

    def step(k, so_far):
        return combine(so_far, jax.tree.map(lambda part: part[k], everything))

    return lax.fori_loop(1, lax.axis_size(axis), step, first)


def noise_levels(level_ids):
    fraction = level_ids.astype(jnp.float32) / (LEVELS - 1)
    return 0.6 * jnp.exp2(fraction)


def combine(left_part, right_part):
    overall = jnp.maximum(left_part[0], right_part[0])
    left_scale = jnp.exp(left_part[0] - overall)
    right_scale = jnp.exp(right_part[0] - overall)
    weight_mass = left_part[1] * left_scale + right_part[1] * right_scale
    weighted = left_part[2] * left_scale[:, None] + right_part[2] * right_scale[:, None]
    return (overall, weight_mass, weighted)


def gauss_project(latent, pixel_mean, eigenbasis, eigenvalues, active_sigma_index):
    centered = (latent - pixel_mean[None, :]).astype(jnp.bfloat16)
    coefficients = lax.psum(
        jnp.dot(centered, eigenbasis, preferred_element_type=jnp.float32), "rows"
    )
    shrink = eigenvalues[None, :] / (
        eigenvalues[None, :] + (active_sigma_index * active_sigma_index)[:, None]
    )
    shrunk = (coefficients * shrink).astype(jnp.bfloat16)
    return lax.dot_general(
        shrunk, eigenbasis, (((1,), (1,)), ((), ())), preferred_element_type=jnp.float32
    )


def empirical_estimate(
    current_latent,
    pairwise_similarity,
    training_vector_energies,
    category_reward,
    slab,
    active_sigma_index,
    following_level,
):
    sharpness_factor = 1.0 / (
        2.0 * active_sigma_index * active_sigma_index * math.sqrt(IMAGE_POINTS)
    )
    unnormalized_affinity = (
        sharpness_factor[:, None] * (2.0 * pairwise_similarity - training_vector_energies[None, :])
        + category_reward
    )
    block_peak = jnp.max(unnormalized_affinity, axis=1)
    weights = jnp.exp(unnormalized_affinity - block_peak[:, None]).astype(jnp.bfloat16)
    weight_mass = jnp.sum(weights.astype(jnp.float32), axis=1)
    weighted = jnp.dot(weights, slab, preferred_element_type=jnp.float32)
    overall, weight_mass, weighted = merged((block_peak, weight_mass, weighted), "rows", combine)
    average = weighted / weight_mass[:, None]
    return average + (following_level / active_sigma_index)[:, None] * (current_latent - average)


def shards(
    queries, pixel_mean, eigenbasis, eigenvalues, level_ids, slab, slab_classes, target_categories
):
    noise_sample = noise_levels(level_ids)
    latent = queries
    partial_value = gauss_project(latent, pixel_mean, eigenbasis, eigenvalues, noise_sample[0])
    cleaned = pixel_mean[None, :] + lax.psum(partial_value, "px")
    latent = cleaned + (noise_sample[1] / noise_sample[0])[:, None] * (latent - cleaned)
    partial_value = gauss_project(latent, pixel_mean, eigenbasis, eigenvalues, noise_sample[1])
    step_ratio = (noise_sample[2] / noise_sample[1])[:, None]
    px_count = lax.axis_size("px")
    px_place = lax.axis_index("px")
    cleaned = pixel_mean[None, :] + lax.psum(partial_value, "px")
    latent = cleaned + step_ratio * (latent - cleaned)
    everything = lax.all_gather(latent, "rows", axis=1, tiled=True)
    px_span = everything.shape[1] // px_count
    current_latent = lax.dynamic_slice_in_dim(everything, px_place * px_span, px_span, 1)
    row_norms_part = jnp.einsum("rp,rp->r", slab, slab, preferred_element_type=jnp.float32)
    category_reward = jnp.where(
        slab_classes[None, :] == target_categories[:, None], steering_strength, 0.0
    ).astype(jnp.float32)
    operand = current_latent.astype(jnp.bfloat16)
    products_part = lax.dot_general(
        operand, slab, (((1,), (1,)), ((), ())), preferred_element_type=jnp.float32
    )
    pairwise_similarity, training_vector_energies = lax.psum((products_part, row_norms_part), "px")
    updated_latent = empirical_estimate(
        current_latent,
        pairwise_similarity,
        training_vector_energies,
        category_reward,
        slab,
        noise_sample[2],
        noise_sample[3],
    )
    operand = updated_latent.astype(jnp.bfloat16)
    products_part = lax.dot_general(
        operand, slab, (((1,), (1,)), ((), ())), preferred_element_type=jnp.float32
    )
    squares_part = jnp.sum(updated_latent * updated_latent, axis=1)
    pairwise_similarity, squares = lax.psum((products_part, squares_part), "px")
    magnitude_normalizer = jnp.sqrt(squares / IMAGE_POINTS + rms_epsilon)
    updated_latent = empirical_estimate(
        updated_latent / magnitude_normalizer[:, None],
        pairwise_similarity / magnitude_normalizer[:, None],
        training_vector_energies,
        category_reward,
        slab,
        noise_sample[3],
        noise_sample[4],
    )
    squares = lax.psum(jnp.sum(updated_latent * updated_latent, axis=1), "px")
    return updated_latent / jnp.sqrt(squares / IMAGE_POINTS + rms_epsilon)[:, None]


def solution(mesh):
    in_specs = (
        P(None, "rows"),
        P("rows"),
        P("rows", "px"),
        P("px"),
        P(),
        P("rows", "px"),
        P("rows"),
        P(),
    )
    out_specs = P(None, "px")
    return jax.shard_map(shards, mesh=mesh, in_specs=in_specs, out_specs=out_specs, check_vma=False)
```

profile of v0, /device:TPU:0, one launch (start us, length us, event | category | flops | bytes accessed | tf_op | source)
XLA Modules:
  0.0 470.4 jit_solution(10967206249863583956)
XLA Ops:
  7.3 8.2 %fusion.16 = f32[8,1024]{1,0:T(8,128)S(1)} fusion(bf16[8192,1024]{1,0:T(8,128)(2,1)} %param.14, f32[8,8192]{1,0:T(8,128)} %param.12, f32[8192]{0:T(1024)} %param.13), kind=kOutput, calls=%fused_computation.37 | convolution fusion | flops 134348800 | bytes 17104896 | tf_op jit(solution)/shard_map/dot_general | solution.py:43
  15.5 38.9 %psum.63 = f32[8,1024]{1,0:T(8,128)S(1)} all-reduce(f32[8,1024]{1,0:T(8,128)S(1)} %fusion.16), channel_id=1, replica_groups=mesh['rows'=8,'px'=4] {'rows'}, use_global_device_ids=true, to_apply=%region_0.0 | all-reduce | flops 8192 | bytes 65536 | tf_op jit(solution)/shard_map/psum | solution.py:42
  54.3 10.9 %fusion.20 = f32[8,8192]{1,0:T(8,128)} fusion(bf16[8192,1024]{1,0:T(8,128)(2,1)} %param.14, f32[8,1024]{1,0:T(8,128)S(1)} %psum.63, f32[8]{0:T(128)S(1)} %get-tuple-element.421, f32[1024]{0:T(1024)S(1)} %copy-done.4), kind=kOutput, calls=%fused_computation.45 | convolution fusion | flops 134250496 | bytes 17076256 | tf_op jit(solution)/shard_map/dot_general | solution.py:49
  65.3 29.3 %all-reduce.11.cloned.1.call-done = f32[8,8192]{1,0:T(8,128)} async-done(((f32[8,8192]{1,0:T(8,128)}), f32[8,8192]{1,0:T(8,128)}) %all-reduce.11.cloned.1.call-update) | async-done | bytes 262160 | tf_op jit(solution)/shard_map/psum | solution.py:85
  94.7 8.2 %fusion.17 = f32[8,1024]{1,0:T(8,128)S(1)} fusion(bf16[8192,1024]{1,0:T(8,128)(2,1)} %param.14, f32[8192]{0:T(1024)S(1)} %copy-done.2, f32[8,8192]{1,0:T(8,128)S(1)} %copy-done, f32[8,8192]{1,0:T(8,128)} %all-reduce.11.cloned.1.call-done, f32[8]{0:T(128)S(1)} %get-tuple-element.418), kind=kOutput, calls=%fused_computation.38 | convolution fusion | flops 134610944 | bytes 17367072 | tf_op jit(solution)/shard_map/dot_general | solution.py:43
  102.9 37.1 %psum.65 = f32[8,1024]{1,0:T(8,128)S(1)} all-reduce(f32[8,1024]{1,0:T(8,128)S(1)} %fusion.17), channel_id=1, replica_groups=mesh['rows'=8,'px'=4] {'rows'}, use_global_device_ids=true, to_apply=%region_2.0 | all-reduce | flops 8192 | bytes 65536 | tf_op jit(solution)/shard_map/psum | solution.py:42
  140.0 10.9 %fusion.21 = f32[8,8192]{1,0:T(8,128)} fusion(bf16[8192,1024]{1,0:T(8,128)(2,1)} %param.14, f32[8,1024]{1,0:T(8,128)S(1)} %psum.65, f32[8]{0:T(128)S(1)} %get-tuple-element.417, f32[1024]{0:T(1024)S(1)} %copy-done.4), kind=kOutput, calls=%fused_computation.46 | convolution fusion | flops 134250496 | bytes 17076256 | tf_op jit(solution)/shard_map/dot_general | solution.py:49
  151.0 28.3 %all-reduce.13.cloned.1.call-done = f32[8,8192]{1,0:T(8,128)} async-done(((f32[8,8192]{1,0:T(8,128)}), f32[8,8192]{1,0:T(8,128)}) %all-reduce.13.cloned.1.call-update) | async-done | bytes 262160 | tf_op jit(solution)/shard_map/psum | solution.py:91
  179.3 1.8 multiply_add_fusion.2
  181.1 7.2 %fusion.12 = f32[512]{0:T(512)S(1)} fusion(bf16[512,16384]{1,0:T(8,128)(2,1)} %param.17), kind=kLoop, calls=%fused_computation.23 | loop fusion | flops 25165312 | bytes 16779264 | tf_op jit(solution)/shard_map/rp,rp->r/dot_general | solution.py:96
  188.4 42.4 %all-gather.10.cloned.1.call-done = f32[8,65536]{1,0:T(8,128)} async-done(((f32[8,8192]{1,0:T(8,128)}), f32[8,65536]{1,0:T(8,128)}) %all-gather.10.cloned.1.call-update) | async-done | bytes 2097168 | tf_op jit(solution)/shard_map/all_gather | solution.py:93
  230.7 10.4 %fusion.13 = f32[8,512]{1,0:T(8,128)S(1)} fusion(bf16[512,16384]{1,0:T(8,128)(2,1)} %param.17, f32[8,65536]{1,0:T(8,128)} %all-gather.10.cloned.1.call-done, s32[]{:T(128)S(6)} %select_n.31), kind=kOutput, calls=%fused_computation.29 | convolution fusion | flops 134217728 | bytes 17055748 | tf_op jit(solution)/shard_map/dot_general | solution.py:101
  241.1 10.3 %all-reduce.7 = (f32[8,512]{1,0:T(8,128)S(1)}, f32[512]{0:T(512)S(1)}) all-reduce(f32[8,512]{1,0:T(8,128)S(1)} %fusion.13, f32[512]{0:T(512)S(1)} %fusion.12), channel_id=1, replica_groups=mesh['rows'=8,'px'=4] {'px'}, use_global_device_ids=true, to_apply=%region_4.5 | all-reduce | flops 4608 | bytes 36864 | tf_op jit(solution)/shard_map/psum | solution.py:104
  251.7 8.9 %fusion.36 = f32[8,16384]{1,0:T(8,128)} fusion(bf16[8,512]{1,0:T(8,128)(2,1)S(1)} %get-tuple-element.414, bf16[512,16384]{1,0:T(8,128)(2,1)} %param.17), kind=kOutput, calls=%fused_computation.74 | convolution fusion | flops 134217728 | bytes 17309696 | tf_op jit(solution)/shard_map/dot_general | solution.py:73
  262.6 20.3 %all-reduce.5 = (f32[64]{0:T(128)S(1)}, f32[64]{0:T(128)S(1)}) all-reduce(f32[64]{0:T(128)S(1)} %dynamic-update-slice, f32[64]{0:T(128)S(1)} %dynamic-update-slice.1), channel_id=2, replica_groups=mesh['rows'=8,'px'=4] {'rows'}, use_global_device_ids=true, to_apply=%add | all-reduce | flops 128 | bytes 1024
  283.0 50.0 %all-gather.12.cloned.1.call-done = f32[64,16384]{1,0:T(8,128)} async-done(((f32[8,16384]{1,0:T(8,128)}), f32[64,16384]{1,0:T(8,128)}) %all-gather.12.cloned.1.call-update) | async-done | bytes 4194320 | tf_op jit(solution)/shard_map/all_gather | solution.py:17
  334.1 9.4 %while.38 = (s32[]{:T(128)}, f32[8]{0:T(128)S(1)}, f32[8]{0:T(128)S(1)}, f32[8,16384]{1,0:T(8,128)S(1)}, f32[8,8]{1,0:T(8,128)S(1)}, /*index=5*/f32[8,8]{1,0:T(8...) while((s32[]{:T(128)}, f32[8]{0:T(128)S(1)}, f32[8]{0:T(128)S(1)}, ...), condition=%wide.region_9.10_spmd, body=%wide.region_8.9_spmd.sunk | while | flops 393269 | bytes 1573335 | solution.py:23
  344.9 10.2 %fusion.14 = f32[8,512]{1,0:T(8,128)S(1)} fusion(bf16[512,16384]{1,0:T(8,128)(2,1)} %param.17, f32[8,16384]{1,0:T(8,128)S(1)} %get-tuple-element.412), kind=kOutput, calls=%fused_computation.31 | convolution fusion | flops 134348800 | bytes 17317888 | tf_op jit(solution)/shard_map/dot_general | solution.py:115
  355.0 10.3 %all-reduce.6 = (f32[8,512]{1,0:T(8,128)S(1)}, f32[8]{0:T(128)S(1)}) all-reduce(f32[8,512]{1,0:T(8,128)S(1)} %fusion.14, f32[8]{0:T(128)S(1)} %get-tuple-element.411), channel_id=1, replica_groups=mesh['rows'=8,'px'=4] {'px'}, use_global_device_ids=true, to_apply=%region_10.11 | all-reduce | flops 4104 | bytes 32832 | tf_op jit(solution)/shard_map/psum | solution.py:119
  365.5 8.9 %fusion.32 = f32[8,16384]{1,0:T(8,128)} fusion(bf16[512,16384]{1,0:T(8,128)(2,1)} %param.17, f32[8,512]{1,0:T(8,128)S(1)} %get-tuple-element.410, f32[8]{0:T(128)S(1)} %get-tuple-element.409), kind=kOutput, calls=%fused_computation.72 | convolution fusion | flops 134225920 | bytes 17317920 | tf_op jit(solution)/shard_map/dot_general | solution.py:73
  375.1 20.2 %all-reduce.4 = (f32[64]{0:T(128)S(1)}, f32[64]{0:T(128)S(1)}) all-reduce(f32[64]{0:T(128)S(1)} %dynamic-update-slice.2, f32[64]{0:T(128)S(1)} %dynamic-update-slice.3), channel_id=5, replica_groups=mesh['rows'=8,'px'=4] {'rows'}, use_global_device_ids=true, to_apply=%add.2 | all-reduce | flops 128 | bytes 1024
  395.5 51.0 %all-gather.14.cloned.1.call-done = f32[64,16384]{1,0:T(8,128)} async-done(((f32[8,16384]{1,0:T(8,128)}), f32[64,16384]{1,0:T(8,128)}) %all-gather.14.cloned.1.call-update) | async-done | bytes 4194320 | tf_op jit(solution)/shard_map/all_gather | solution.py:17
  447.6 9.4 %while.39 = (s32[]{:T(128)}, f32[8]{0:T(128)S(1)}, f32[8]{0:T(128)S(1)}, f32[8,16384]{1,0:T(8,128)S(1)}, f32[8,8]{1,0:T(8,128)S(1)}, /*index=5*/f32[8,8]{1,0:T(8...) while((s32[]{:T(128)}, f32[8]{0:T(128)S(1)}, f32[8]{0:T(128)S(1)}, ...), condition=%wide.region_16.17_spmd, body=%wide.region_15.16_spmd.sunk | while | flops 393269 | bytes 1573335 | solution.py:23
  457.3 5.7 %psum.71 = f32[8]{0:T(128)S(1)} all-reduce(f32[8]{0:T(128)S(1)} %get-tuple-element.407), channel_id=1, replica_groups=mesh['rows'=8,'px'=4] {'px'}, use_global_device_ids=true, to_apply=%region_18.19 | all-reduce | flops 8 | bytes 64 | tf_op jit(solution)/shard_map/psum | solution.py:130
  (78 shorter events, 27.1 us)
Async XLA Ops:
  6.5 47.8 %copy-start.4 = (f32[1024]{0:T(1024)S(1)}, f32[1024]{0:T(1024)}, u32[]{:S(2)}) copy-start(f32[1024]{0:T(1024)} %param.15) | copy-start | bytes 12292
  6.5 88.1 %all-reduce.11.cloned.1.call-start = ((), (), s32[]{:S(2)}) async-start(), calls=%async_computation | async-start | bytes 524288 | tf_op jit(solution)/shard_map/psum | solution.py:85
  7.3 87.4 %copy-start = (f32[8,8192]{1,0:T(8,128)S(1)}, f32[8,8192]{1,0:T(8,128)}, u32[]{:S(2)}) copy-start(f32[8,8192]{1,0:T(8,128)} %param.12) | copy-start | bytes 786436
  7.3 87.4 %copy-start.2 = (f32[8192]{0:T(1024)S(1)}, f32[8192]{0:T(1024)}, u32[]{:S(2)}) copy-start(f32[8192]{0:T(1024)} %param.13) | copy-start | bytes 98308
  65.3 114.0 %all-reduce.13.cloned.1.call-start = ((), (), s32[]{:S(2)}) async-start(), calls=%async_computation.1 | async-start | bytes 524288 | tf_op jit(solution)/shard_map/psum | solution.py:91
  94.7 84.6 %copy-start.1 = (f32[8,8192]{1,0:T(8,128)S(1)}, f32[8,8192]{1,0:T(8,128)}, u32[]{:S(2)}) copy-start(f32[8,8192]{1,0:T(8,128)} %all-reduce.11.cloned.1.call-done) | copy-start | bytes 786436
  150.9 79.8 %all-gather.10.cloned.1.call-start = ((), (), s32[]{:S(2)}) async-start(), calls=%async_computation.2 | async-start | bytes 2359296 | tf_op jit(solution)/shard_map/all_gather | solution.py:93
  181.1 151.9 %all-gather.12.cloned.1.call-start = ((), (), s32[]{:S(2)}) async-start(), calls=%async_computation.3 | async-start | bytes 4718592 | tf_op jit(solution)/shard_map/all_gather | solution.py:17
  181.1 70.2 %copy-start.3 = (s32[512]{0:T(512)S(1)}, s32[512]{0:T(512)}, u32[]{:S(2)}) copy-start(s32[512]{0:T(512)} %param.18) | copy-start | bytes 6148
  181.1 70.2 %copy-start.5 = (s32[8]{0:T(128)S(1)}, s32[8]{0:T(128)}, u32[]{:S(2)}) copy-start(s32[8]{0:T(128)} %param.19) | copy-start | bytes 100
  188.4 72.5 %copy-start.6 = (u32[32]{0:T(128)S(1)}, u32[32]{0:T(128)}, u32[]{:S(2)}) copy-start(u32[32]{0:T(128)} %constant.109) | copy-start | bytes 388
  260.6 185.9 %all-gather.14.cloned.1.call-start = ((), (), s32[]{:S(2)}) async-start(), calls=%async_computation.4 | async-start | bytes 4718592 | tf_op jit(solution)/shard_map/all_gather | solution.py:17
Sparse Core Ops, SparseCore 0:
  65.4 29.2 all-reduce.10
  151.1 28.1 all-reduce.12
  181.4 49.2 all-gather.9
  260.7 72.2 all-gather.11
  374.5 71.9 all-gather.13
where the time goes:
time: 472 us; the launch traced here: 470 us
  waiting for transfers between devices  201 us (43%)
  blocking collectives  143 us (30%)
  matrix products  76.5 us (16%)
  other arithmetic  31.6 us (7%)
  between operations  13.9 us (3%)
    all_gather x2, waiting for transfers between devices, merged(): everything = jax.tree.map(lambda part: lax.all_gather(part, axis), x)  101 us
    psum x2, blocking collectives, gauss_project(): lax.psum(jnp.dot(centered, eigenbasis, preferred_element_type=jnp.float32...  76 us
    psum x2, waiting for transfers between devices, shards(): cleaned = pixel_mean[None, :] + lax.psum(partial_value, 'px')  57.6 us
    all_gather x1, waiting for transfers between devices, shards(): everything = lax.all_gather(latent, 'rows', axis=1, tiled=True)  42.4 us
    unnamed x2, blocking collectives  40.5 us
    dot_general x2, matrix products, gauss_project(): lax.dot_general(shrunk, eigenbasis, (((1,), (1,)), ((), ())), preferred_e...  21.8 us
    dot_general x2, matrix products, shards(): lax.dot_general(operand, slab, (((1,), (1,)), ((), ())), preferred_elemen...  20.6 us
    add x14, other arithmetic, combine(): left_part[2] * left_scale[:, None] + right_part[2] * right_scale[:, None]  18.1 us
  transfers between devices with their start and end apart: 5, of which 5 were waited for; matrix products, arithmetic and copies ran while one was open for 2% of the time, Pallas kernels for 0%

commit v1 on v0

v1 whole, which is shorter than its diff:
```python
import functools
import math

import jax
import jax.numpy as jnp
from jax import lax
from jax.experimental import pallas as pl
from jax.experimental.pallas import tpu as pltpu
from jax.sharding import PartitionSpec as P

IMAGE_POINTS = 65536
LEVELS = 64
STEERING = 1.5
RMS_EPSILON = 1e-06
MIB = 1024 * 1024
NT = (((1,), (1,)), ((), ()))
CHUNKS = 8
PAD = 128

f32 = jnp.float32
bf16 = jnp.bfloat16


def vmem():
    return pl.BlockSpec(memory_space=pltpu.VMEM)


def anywhere():
    return pl.BlockSpec(memory_space=pl.ANY)


def in_vmem(x):
    return pltpu.with_memory_space_constraint(x, pltpu.VMEM)


def shape(dims, dtype=f32):
    return jax.ShapeDtypeStruct(dims, dtype)


def call(kernel, out_shape, args, in_specs=None, scratch=(), flops=0, name=None):
    many = isinstance(out_shape, (list, tuple))
    return pl.pallas_call(
        kernel,
        in_specs=in_specs or [vmem()] * len(args),
        out_specs=[vmem()] * len(out_shape) if many else vmem(),
        out_shape=out_shape,
        scratch_shapes=list(scratch),
        compiler_params=pltpu.CompilerParams(vmem_limit_bytes=10 * MIB),
        cost_estimate=pl.CostEstimate(
            flops=flops, bytes_accessed=16 * MIB if flops else MIB, transcendentals=0
        ),
        name=name,
    )(*args)


def rows_at(start, count, unit):
    return pl.ds(pl.multiple_of(start, unit), count)


def load_project_kernel(q_hbm, mean_hbm, e_hbm, copies, offset, e_vmem, q, mean, sems):
    pixels = e_hbm.shape[0]
    chunk = pixels // CHUNKS

    def moves(c):
        at = rows_at(c * chunk, chunk, chunk)
        return (
            pltpu.make_async_copy(q_hbm.at[:, at], q.at[:, at], sems.at[c, 0]),
            pltpu.make_async_copy(mean_hbm.at[:, at], mean.at[:, at], sems.at[c, 1]),
            pltpu.make_async_copy(e_hbm.at[at], e_vmem.at[at], sems.at[c, 2]),
        )

    @pl.loop(0, CHUNKS)
    def _(c):
        for move in moves(c):
            move.start()

    def step(c, total):
        for move in moves(c):
            move.wait()
        at = rows_at(c * chunk, chunk, chunk)
        off = q[:, at] - mean[:, at]
        offset[:, at] = off
        return total + jnp.dot(off.astype(bf16), e_vmem[at, :], preferred_element_type=f32)

    total = lax.fori_loop(0, CHUNKS, step, jnp.zeros((8, e_hbm.shape[1]), f32))
    for k in range(copies.shape[0]):
        copies[k] = total


def load_project(queries, mean, basis, row_count):
    pixels, comps = basis.shape
    basis = pltpu.with_memory_space_constraint(basis, pltpu.HBM)
    return call(
        load_project_kernel,
        [
            shape((row_count, 8, comps)),
            shape((8, pixels)),
            pltpu.VMEM((pixels, comps), bf16),
        ],
        (queries, mean, basis),
        in_specs=[anywhere()] * 3,
        scratch=[
            pltpu.VMEM((8, pixels), f32),
            pltpu.VMEM((1, pixels), f32),
            pltpu.SemaphoreType.DMA((CHUNKS, 3)),
        ],
        flops=16 * pixels * comps,
        name="load_project",
    )


def back_kernel(step, flip, parts, eigenvalues, sigma, e_vmem, image):
    half = image.shape[1]
    core = lax.rem(lax.axis_index("px"), 2)
    which = 1 - core if flip else core
    now = sigma[:, step : step + 1]
    coeff = jnp.sum(parts[...], axis=0)
    ev = eigenvalues[...]
    shrunk = (coeff * (ev / (ev + now * now))).astype(bf16)
    tile = min(1024, half)

    @pl.loop(0, half // tile)
    def _(i):
        at = rows_at(which * half + i * tile, tile, tile)
        image[:, rows_at(i * tile, tile, tile)] = lax.dot_general(
            shrunk, e_vmem[at, :], NT, preferred_element_type=f32
        )


def back(step, flip, parts, eigenvalues, sigma, e_vmem):
    pixels, comps = e_vmem.shape
    return call(
        functools.partial(back_kernel, step, flip),
        shape((8, pixels // 2)),
        (parts, eigenvalues, sigma, in_vmem(e_vmem)),
        flops=8 * pixels * comps,
        name=f"back_{step}_{int(flip)}",
    )


def project_half_kernel(flip, off, e_vmem, out):
    half = off.shape[1]
    core = lax.rem(lax.axis_index("px"), 2)
    which = 1 - core if flip else core
    tile = min(1024, half)

    def step(i, total):
        at = rows_at(which * half + i * tile, tile, tile)
        part = off[:, rows_at(i * tile, tile, tile)].astype(bf16)
        return total + jnp.dot(part, e_vmem[at, :], preferred_element_type=f32)

    out[...] = lax.fori_loop(0, half // tile, step, jnp.zeros(out.shape, f32))


def project_rest_kernel(off, own, e_vmem, copies):
    half = off.shape[1]
    which = 1 - lax.rem(lax.axis_index("px"), 2)
    tile = min(1024, half)

    def step(i, total):
        at = rows_at(which * half + i * tile, tile, tile)
        part = off[:, rows_at(i * tile, tile, tile)].astype(bf16)
        return total + jnp.dot(part, e_vmem[at, :], preferred_element_type=f32)

    total = lax.fori_loop(0, half // tile, step, own[...])
    for k in range(copies.shape[0]):
        copies[k] = total


def first_update_kernel(mine, theirs, offset, sigma, out):
    half = mine.shape[1]
    core = lax.rem(lax.axis_index("px"), 2)
    ratio = sigma[:, 1:2] / sigma[:, 0:1]
    image = mine[...] + theirs[...]
    out[...] = image + ratio * (offset[:, rows_at(core * half, half, half)] - image)


def second_update_kernel(mine, theirs, offset, mean, sigma, out):
    half = mine.shape[1]
    span = half // 2
    place = lax.axis_index("px")
    core = lax.rem(place, 2)
    x = lax.div(place, 2)
    ratio = sigma[:, 2:3] / sigma[:, 1:2]
    image = mine[...] + theirs[...]
    first = jnp.where(x == 0, 1.0, 0.0).astype(f32)
    mean_half = mean[:, rows_at(core * half, half, half)]
    sent = (1.0 - ratio) * image + first * (ratio * offset[...] + mean_half)
    for k in range(2):
        out[lax.rem(k + x, 2)] = sent[:, k * span : (k + 1) * span]


def norms_kernel(slab, out):
    rows, pixels = slab.shape
    tile = 1024

    def step(i, total):
        part = slab[:, rows_at(i * tile, tile, tile)].astype(f32)
        square = part * part
        for k in range(tile // 128):
            total = total + square[:, k * 128 : (k + 1) * 128]
        return total

    total = lax.fori_loop(0, pixels // tile, step, jnp.zeros((rows, 128), f32))
    out[...] = jnp.sum(total, axis=1)[None, :]


def dots_kernel(first, pieces, extra, slab, out):
    count, _, width = pieces.shape
    span = slab.shape[1] // count

    def step(k, total):
        part = pieces[k, :, :span].astype(bf16)
        at = rows_at(k * span, span, span)
        return total + lax.dot_general(part, slab[:, at], NT, preferred_element_type=f32)

    out[:8] = lax.fori_loop(0, count, step, jnp.zeros((8, slab.shape[0]), f32))
    if first:
        out[8:] = jnp.broadcast_to(extra[...], (8, slab.shape[0]))
    else:
        squares = jnp.sum(pieces[:, :, span:], axis=0)[:, :1]
        out[8:] = jnp.broadcast_to(squares, (8, slab.shape[0]))


def weighted_kernel(step, gathered, norms, classes, targets, sigma, slab, out, *aside):
    count, _, width = out.shape
    span = width - PAD
    both = jnp.sum(gathered[...], axis=0)
    dots = both[:8]
    if step == 0:
        norm = both[8:9]
        aside[0][...] = norm
    else:
        norm = norms[...]
        scale = jnp.sqrt(both[8:, :1] / IMAGE_POINTS + RMS_EPSILON)
        dots = dots / scale
        aside[0][...] = jnp.broadcast_to(scale, aside[0].shape)
    now = sigma[:, 2 + step : 3 + step]
    sharp = 1.0 / (2.0 * now * now * math.sqrt(IMAGE_POINTS))
    bonus = jnp.where(classes[...] == targets[...], STEERING, 0.0).astype(f32)
    scores = sharp * (2.0 * dots - norm) + bonus
    peak = jnp.max(scores, axis=1, keepdims=True)
    weights = jnp.exp(scores - peak).astype(bf16)
    mass = jnp.sum(weights.astype(f32), axis=1, keepdims=True)
    lane = lax.broadcasted_iota(jnp.int32, (8, PAD), 1)
    tail = jnp.where(lane < PAD // 2, peak, mass)

    @pl.loop(0, count)
    def _(k):
        at = rows_at(k * span, span, span)
        out[k, :, :span] = jnp.dot(weights, slab[:, at], preferred_element_type=f32)
        out[k, :, span:] = tail


def combine_kernel(step, parts, state, scale, sigma, copies):
    count, _, width = parts.shape
    span = width - PAD
    peaks = [parts[k, :, span : span + 1] for k in range(count)]
    top = functools.reduce(jnp.maximum, peaks)
    total, mass = jnp.zeros((8, span), f32), jnp.zeros((8, 1), f32)
    for k in range(count):
        factor = jnp.exp(peaks[k] - top)
        total = total + factor * parts[k, :, :span]
        mass = mass + factor * parts[k, :, span + PAD // 2 : span + PAD // 2 + 1]
    average = total / mass
    ratio = sigma[:, 3 + step : 4 + step] / sigma[:, 2 + step : 3 + step]
    current = state[...] if step == 0 else state[...] / scale[:, :1]
    update = average + ratio * (current - average)
    square = jnp.broadcast_to(jnp.sum(update * update, axis=1, keepdims=True), (8, PAD))
    for k in range(count):
        copies[k, :, :span] = update
        copies[k, :, span:] = square


def squares_kernel(pieces, out):
    span = pieces.shape[2] - PAD
    out[...] = jnp.sum(pieces[:, :, span:], axis=0)


def finish_kernel(pieces, squares, out):
    count, _, width = pieces.shape
    span = width - PAD
    total = jnp.sum(squares[...], axis=0)[:, :1]
    scale = jnp.sqrt(total / IMAGE_POINTS + RMS_EPSILON)

    @pl.loop(0, count)
    def _(k):
        out[:, rows_at(k * span, span, span)] = pieces[k, :, :span] / scale


def exchange_px(x, flip):
    size = lax.axis_size("px")
    return lax.ppermute(x, "px", [(i, i ^ flip) for i in range(size)])


def swap_rows(x):
    return lax.all_to_all(x, "rows", 0, 0, tiled=True)


def to_slices(x, turn):
    rows, px = lax.axis_size("rows"), lax.axis_size("px")
    pairs = []
    for r in range(rows):
        for p in range(px):
            upper, core = divmod(p, 2)
            piece = r * px + 2 * core + (upper + turn) % 2
            pairs.append((r * px + p, (piece % rows) * px + piece // rows))
    return lax.ppermute(x, ("rows", "px"), pairs)


def shards(
    queries, pixel_mean, eigenbasis, eigenvalues, level_ids, slab, slab_classes, target_categories
):
    rows = lax.axis_size("rows")
    pixels, comps = eigenbasis.shape
    slab_rows, slab_pixels = slab.shape
    span = slab_pixels // rows
    sigma = 0.6 * jnp.exp2(level_ids.T.astype(f32) / (LEVELS - 1))
    mean = pixel_mean[None, :]
    values = eigenvalues[None, :]
    classes = slab_classes[None, :]
    targets = target_categories[:, None]
    gauss_flops = 8 * pixels * comps
    slab_flops = 16 * slab_rows * slab_pixels

    copies, offset, basis = load_project(queries, mean, eigenbasis, rows)
    parts = swap_rows(copies)
    sent = exchange_px(back(0, True, parts, values, sigma, basis), 1)
    image = back(0, False, parts, values, sigma, basis) + sent
    across = exchange_px(image, 2)
    norms = call(
        norms_kernel,
        shape((1, slab_rows)),
        (in_vmem(slab),),
        flops=2 * slab_rows * slab_pixels,
        name="norms",
    )
    offset = call(
        first_update_kernel,
        shape((8, pixels // 2)),
        (image, across, offset, sigma),
        name="first_update",
    )
    other = exchange_px(offset, 1)
    own = call(
        functools.partial(project_half_kernel, False),
        shape((8, comps)),
        (offset, in_vmem(basis)),
        flops=gauss_flops,
        name="project_own",
    )
    copies = call(
        project_rest_kernel,
        shape((rows, 8, comps)),
        (other, own, in_vmem(basis)),
        flops=gauss_flops,
        name="project_rest",
    )
    parts = swap_rows(copies)
    sent = exchange_px(back(1, True, parts, values, sigma, basis), 1)
    mine = back(1, False, parts, values, sigma, basis)
    outgoing = call(
        second_update_kernel,
        shape((2, 8, span)),
        (mine, sent, offset, mean, sigma),
        name="second_update",
    )
    state = to_slices(outgoing[0], 0) + to_slices(outgoing[1], 1)
    pieces = swap_rows(jnp.broadcast_to(state[None], (rows, 8, span)))
    products = call(
        functools.partial(dots_kernel, True),
        shape((16, slab_rows)),
        (pieces, norms, in_vmem(slab)),
        flops=slab_flops,
        name="dots_0",
    )
    scale = None
    for step in range(2):
        gathered = lax.all_gather(products, "px")
        weighted, aside = call(
            functools.partial(weighted_kernel, step),
            [
                shape((rows, 8, span + PAD)),
                shape((1, slab_rows)) if step == 0 else shape((8, PAD)),
            ],
            (gathered, norms, classes, targets, sigma, in_vmem(slab)),
            flops=slab_flops,
            name=f"weighted_{step}",
        )
        if step == 0:
            norms = aside
        else:
            scale = aside
        parts = swap_rows(weighted)
        copies = call(
            functools.partial(combine_kernel, step),
            shape((rows, 8, span + PAD)),
            (parts, state, sigma if scale is None else scale, sigma),
            name=f"combine_{step}",
        )
        state = copies[0, :, :span]
        pieces = swap_rows(copies)
        if step == 0:
            products = call(
                functools.partial(dots_kernel, False),
                shape((16, slab_rows)),
                (pieces, norms, in_vmem(slab)),
                flops=slab_flops,
                name="dots_1",
            )
    squares = call(squares_kernel, shape((8, PAD)), (pieces,), name="squares")
    squares = lax.all_gather(squares, "px")
    return call(finish_kernel, shape((8, slab_pixels)), (pieces, squares), name="finish")


def solution(mesh):
    in_specs = (
        P(None, "rows"),
        P("rows"),
        P("rows", "px"),
        P("px"),
        P(),
        P("rows", "px"),
        P("rows"),
        P(),
    )
    out_specs = P(None, "px")
    return jax.shard_map(shards, mesh=mesh, in_specs=in_specs, out_specs=out_specs, check_vma=False)
```

time: 472 us -> 229 us (0.49)
  waiting for transfers between devices: 201 us -> 34 us
  matrix products: 76.5 us -> 0 us
  blocking collectives: 143 us -> 89.6 us
  Pallas kernels: 0 us -> 49.6 us
  other arithmetic: 31.6 us -> 0.05 us
  local copies, waits for them, and re-layouts: 4.04 us -> 31.6 us
  starting transfers between devices: 0.39 us -> 23.2 us
  between operations: 13.9 us -> 0.21 us
    all_gather x3 -> x0, waiting for transfers between devices: 143 us -> none  [the longest x2 101 us: merged(): everything = jax.tree.map(lambda part: lax.all_gather(part, axis), x)]
    psum x5 -> x0, blocking collectives: 102 us -> none  [the longest x2 76 us: gauss_project(): lax.psum(jnp.dot(centered, eigenbasis, preferred_element_type=jnp.float32...]
    dot_general x8 -> x0, matrix products: 76.5 us -> none  [the longest x2 21.8 us: gauss_project(): lax.dot_general(shrunk, eigenbasis, (((1,), (1,)), ((), ())), preferred_e...]
    all_to_all x0 -> x4, blocking collectives: none -> 73.5 us  [swap_rows(): return lax.all_to_all(x, 'rows', 0, 0, tiled=True)]
    psum x2 -> x0, waiting for transfers between devices: 57.6 us -> none  [shards(): cleaned = pixel_mean[None, :] + lax.psum(partial_value, 'px')]
    pallas_call x0 -> x18, Pallas kernels: none -> 49.6 us  [call(): pl.pallas_call(kernel, in_specs=in_specs or [vmem()] * len(args), out_spe...]
    unnamed x2 -> x0, blocking collectives: 40.5 us -> none
    unnamed x23 -> x41, local copies, waits for them, and re-layouts: 1.58 us -> 30.6 us
  transfers between devices with their start and end apart: 5 -> 9, of which waited for: 5 -> 4; matrix products, arithmetic and copies ran while one was open for 2% -> 0% of each run, Pallas kernels for 0% -> 6%
where the time goes in v1:
time: 229 us; the launch traced here: 228 us
  blocking collectives  89.6 us (39%)
  Pallas kernels  49.6 us (22%)
  waiting for transfers between devices  34 us (15%)
  local copies, waits for them, and re-layouts  31.6 us (14%)
  starting transfers between devices  23.2 us (10%)
    all_to_all x4, blocking collectives, swap_rows(): return lax.all_to_all(x, 'rows', 0, 0, tiled=True)  73.5 us
    pallas_call x18, Pallas kernels, call(): pl.pallas_call(kernel, in_specs=in_specs or [vmem()] * len(args), out_spe...  49.6 us
    unnamed x41, local copies, waits for them, and re-layouts  30.6 us
    all_to_all x3, waiting for transfers between devices, swap_rows(): return lax.all_to_all(x, 'rows', 0, 0, tiled=True)  24.7 us
    all_to_all x3, starting transfers between devices, swap_rows(): return lax.all_to_all(x, 'rows', 0, 0, tiled=True)  17.4 us
    all_gather x2, blocking collectives, shards(): gathered = lax.all_gather(products, 'px')  10.9 us
    all_gather x1, blocking collectives, shards(): squares = lax.all_gather(squares, 'px')  5.17 us
    ppermute x2, waiting for transfers between devices, to_slices(): return lax.ppermute(x, ('rows', 'px'), pairs)  4.89 us
  transfers between devices with their start and end apart: 9, of which 4 were waited for; matrix products, arithmetic and copies ran while one was open for 0% of the time, Pallas kernels for 6%

profile of v1, /device:TPU:0, one launch (start us, length us, event | category | flops | bytes accessed | tf_op | source)
XLA Modules:
  0.0 228.2 jit_solution(6823928594302736346)
XLA Ops:
  1.7 7.3 %load_project.1 = (f32[8,8,1024]{2,1,0:T(8,128)}, f32[8,8192]{1,0:T(8,128)S(1)}, bf16[8192,1024]{1,0:T(8,128)(2,1)S(1)}) custom-call(f32[8,8192]{1,0:T(8,128)S(1)} %copy-done.5, f32[1,8192]{1,0:T(1,128)S(1)} %bitcast.21, bf16[8192,1024]{1,0:T(8,128)(2,1)} %e_hbm.1), custom_call_target="tpu_custom_call" | custom-call | flops 134217728 | bytes 16777216 | tf_op jit(solution)/shard_map/load_project/pallas_call | solution.py:42
  9.0 5.7 %copy-done = bf16[8192,1024]{1,0:T(8,128)(2,1)} copy-done((bf16[8192,1024]{1,0:T(8,128)(2,1)}, bf16[8192,1024]{1,0:T(8,128)(2,1)S(1)}, u32[]{:S(2)}) %copy-start) | copy-done | bytes 16777240
  14.8 7.3 %all-to-all-start = ((f32[8,8,1024]{2,1,0:T(8,128)}), f32[8,8,1024]{2,1,0:T(8,128)S(1)}, u32[]{:S(2)}, u32[]{:S(2)}) async-start(f32[8,8,1024]{2,1,0:T(8,128)} %get-tuple-element.12), calls=%async_computation | async-start | bytes 524288 | tf_op jit(solution)/shard_map/all_to_all | solution.py:297
  22.1 8.8 %all-to-all-done.parts = f32[8,8,1024]{2,1,0:T(8,128)S(1)} async-done(((f32[8,8,1024]{2,1,0:T(8,128)}), f32[8,8,1024]{2,1,0:T(8,128)S(1)}, u32[]{:S(2)}, u32[]{:S(2)}) %all-to-all-start) | async-done | bytes 262176 | tf_op jit(solution)/shard_map/all_to_all | solution.py:297
  31.0 5.8 %copy-done.1 = bf16[8192,1024]{1,0:T(8,128)(2,1)S(1)} copy-done((bf16[8192,1024]{1,0:T(8,128)(2,1)S(1)}, bf16[8192,1024]{1,0:T(8,128)(2,1)}, u32[]{:S(2)}) %copy-start.1) | copy-done | bytes 16777240
  43.8 4.4 %collective-permute-done.1.theirs = f32[8,4096]{1,0:T(8,128)S(1)} collective-permute-done((f32[8,4096]{1,0:T(8,128)S(1)}, f32[8,4096]{1,0:T(8,128)S(1)}, u32[]{:S(2)}, u32[]{:S(2)}) %collective-permute-start.1) | collective-permute-done | bytes 131104 | tf_op jit(solution)/shard_map/ppermute | solution.py:293
  51.6 12.9 %all_to_all.35.parts = f32[8,8,1024]{2,1,0:T(8,128)S(1)} all-to-all(f32[8,8,1024]{2,1,0:T(8,128)S(1)} %project_rest.1), channel_id=1, replica_groups=mesh['rows'=8,'px'=4] {'rows'}, dimensions={0} | all-to-all | bytes 524288 | tf_op jit(solution)/shard_map/all_to_all | solution.py:297
  70.9 3.6 %collective-permute-start.5 = (f32[8,2048]{1,0:T(8,128)S(1)}, f32[8,2048]{1,0:T(8,128)S(1)}, u32[]{:S(2)}, u32[]{:S(2)}) collective-permute-start(f32[8,2048]{1,0:T(8,128)S(1)} %get-tuple-element.19), channel_id=1, source_target_pairs={{0,4},{1,12},{2,0},{3,8},{4,20},{5,28},{6,16},{7,24},{8,5},{9,13},... | collective-permute-start | bytes 196616 | tf_op jit(solution)/shard_map/ppermute | solution.py:308
  74.5 4.9 %collective-permute-done.5 = f32[8,2048]{1,0:T(8,128)S(1)} collective-permute-done((f32[8,2048]{1,0:T(8,128)S(1)}, f32[8,2048]{1,0:T(8,128)S(1)}, u32[]{:S(2)}, u32[]{:S(2)}) %collective-permute-start.5) | collective-permute-done | bytes 65568 | tf_op jit(solution)/shard_map/ppermute | solution.py:308
  80.2 6.5 %all-to-all-start.2 = ((f32[8,8,2048]{2,1,0:T(8,128)}), f32[8,8,2048]{2,1,0:T(8,128)S(1)}, u32[]{:S(2)}, u32[]{:S(2)}) async-start(f32[8,8,2048]{2,1,0:T(8,128)} %broadcast_in_dim.20), calls=%async_computation.2 | async-start | bytes 1048576 | tf_op jit(solution)/shard_map/all_to_all | solution.py:297
  86.8 5.8 %copy-done.2 = bf16[512,16384]{1,0:T(8,128)(2,1)S(1)} copy-done((bf16[512,16384]{1,0:T(8,128)(2,1)S(1)}, bf16[512,16384]{1,0:T(8,128)(2,1)}, u32[]{:S(2)}) %copy-start.2) | copy-done | bytes 16777240
  92.6 7.8 %norms.1.extra = f32[1,512]{1,0:T(1,128)S(1)} custom-call(bf16[512,16384]{1,0:T(8,128)(2,1)S(1)} %copy-done.2), custom_call_target="tpu_custom_call" | custom-call | flops 16777216 | bytes 16777216 | tf_op jit(solution)/shard_map/norms/pallas_call | solution.py:42
  100.4 5.8 %copy-done.3 = bf16[512,16384]{1,0:T(8,128)(2,1)S(1)} copy-done((bf16[512,16384]{1,0:T(8,128)(2,1)S(1)}, bf16[512,16384]{1,0:T(8,128)(2,1)}, u32[]{:S(2)}) %copy-start.3) | copy-done | bytes 16777240
  106.2 5.3 %dots_0.1 = f32[16,512]{1,0:T(8,128)S(1)} custom-call(f32[8,8,2048]{2,1,0:T(8,128)S(1)} %all-to-all-done.2.pieces, f32[1,512]{1,0:T(1,128)S(1)} %norms.1.extra, bf16[512,16384]{1,0:T(8,128)(2,1)S(1)} %copy-done.3), custom_call_target="tpu_custom_call" | custom-call | flops 134217728 | bytes 16777216 | tf_op jit(solution)/shard_map/dots_0/pallas_call | solution.py:42
  111.5 5.4 %all-gather = f32[64,512]{1,0:T(8,128)S(1)} all-gather(f32[16,512]{1,0:T(8,128)S(1)} %dots_0.1), channel_id=2, replica_groups=mesh['rows'=8,'px'=4] {'px'}, dimensions={0}, use_global_device_ids=true | all-gather | bytes 163840 | tf_op jit(solution)/shard_map/all_gather | solution.py:379
  116.9 5.8 %copy-done.4 = bf16[512,16384]{1,0:T(8,128)(2,1)S(1)} copy-done((bf16[512,16384]{1,0:T(8,128)(2,1)S(1)}, bf16[512,16384]{1,0:T(8,128)(2,1)}, u32[]{:S(2)}) %copy-start.4) | copy-done | bytes 16777240
  126.1 22.3 %all_to_all.36.parts = f32[8,8,2176]{2,1,0:T(8,128)S(1)} all-to-all(f32[8,8,2176]{2,1,0:T(8,128)S(1)} %get-tuple-element.15), channel_id=1, replica_groups=mesh['rows'=8,'px'=4] {'rows'}, dimensions={0} | all-to-all | bytes 1114112 | tf_op jit(solution)/shard_map/all_to_all | solution.py:297
  148.6 18.7 %all_to_all.37.pieces = f32[8,8,2176]{2,1,0:T(8,128)S(1)} all-to-all(f32[8,8,2176]{2,1,0:T(8,128)S(1)} %combine_0.1), channel_id=1, replica_groups=mesh['rows'=8,'px'=4] {'rows'}, dimensions={0} | all-to-all | bytes 1114112 | tf_op jit(solution)/shard_map/all_to_all | solution.py:297
  167.3 5.4 %dots_1.1 = f32[16,512]{1,0:T(8,128)S(1)} custom-call(f32[8,8,2176]{2,1,0:T(8,128)S(1)} %all_to_all.37.pieces, f32[1,512]{1,0:T(1,128)S(1)} %get-tuple-element.16.extra.norms, bf16[512,16384]{1,0:T(8,128)(2,1)S(1)} %bitcast.18), custom_call_target="tpu_custom_call" | custom-call | flops 134217728 | bytes 16777216 | tf_op jit(solution)/shard_map/dots_1/pallas_call | solution.py:42
  172.7 5.4 %all-gather.1 = f32[64,512]{1,0:T(8,128)S(1)} all-gather(f32[16,512]{1,0:T(8,128)S(1)} %dots_1.1), channel_id=3, replica_groups=mesh['rows'=8,'px'=4] {'px'}, dimensions={0}, use_global_device_ids=true | all-gather | bytes 163840 | tf_op jit(solution)/shard_map/all_gather | solution.py:379
  178.1 4.2 %weighted_1.1 = (f32[8,8,2176]{2,1,0:T(8,128)}, f32[8,128]{1,0:T(8,128)S(1)}) custom-call(f32[4,16,512]{2,1,0:T(8,128)S(1)} %bitcast.19, f32[1,512]{1,0:T(1,128)S(1)} %get-tuple-element.16.extra.norms, s32[1,512]{1,0:T(1,128)S(1)} %bitcast.29, s32[8,1]{1,0:T(8,128)S(1)} %copy.10.targets, f32[8,5]{1,0:T(8,128)S(1)} %multiply_bitcast_fusion.sigma.scale, ...), custom_call_target="tpu_custom_call" | custom-call | flops 134217728 | bytes 16777216 | tf_op jit(solution)/shard_map/weighted_1/pallas_call | solution.py:42
  185.8 15.9 %all-to-all-done.5.parts = f32[8,8,2176]{2,1,0:T(8,128)S(1)} async-done(((f32[8,8,2176]{2,1,0:T(8,128)}), f32[8,8,2176]{2,1,0:T(8,128)S(1)}, u32[]{:S(2)}, u32[]{:S(2)}) %all-to-all-start.5) | async-done | bytes 557088 | tf_op jit(solution)/shard_map/all_to_all | solution.py:297
  202.0 19.6 %all_to_all.38.pieces = f32[8,8,2176]{2,1,0:T(8,128)S(1)} all-to-all(f32[8,8,2176]{2,1,0:T(8,128)S(1)} %combine_1.1), channel_id=1, replica_groups=mesh['rows'=8,'px'=4] {'rows'}, dimensions={0} | all-to-all | bytes 1114112 | tf_op jit(solution)/shard_map/all_to_all | solution.py:297
  221.6 5.2 %all-gather.2 = f32[32,128]{1,0:T(8,128)S(1)} all-gather(f32[8,128]{1,0:T(8,128)S(1)} %squares.1), channel_id=4, replica_groups=mesh['rows'=8,'px'=4] {'px'}, dimensions={0}, use_global_device_ids=true | all-gather | bytes 20480 | tf_op jit(solution)/shard_map/all_gather | solution.py:412
  (69 shorter events, 28.3 us)
Async XLA Ops:
  1.7 20.3 %copy-start.10 = (s32[5,8]{1,0:T(8,128)S(1)}, s32[5,8]{1,0:T(8,128)}, u32[]{:S(2)}) copy-start(s32[5,8]{1,0:T(8,128)} %param.12) | copy-start | bytes 484
  1.7 29.3 %copy-start.8 = (f32[1024]{0:T(1024)S(1)}, f32[1024]{0:T(1024)}, u32[]{:S(2)}) copy-start(f32[1024]{0:T(1024)} %param.11) | copy-start | bytes 12292
  14.8 16.2 %all-to-all-start = ((f32[8,8,1024]{2,1,0:T(8,128)}), f32[8,8,1024]{2,1,0:T(8,128)S(1)}, u32[]{:S(2)}, u32[]{:S(2)}) async-start(f32[8,8,1024]{2,1,0:T(8,128)} %get-tuple-element.12), calls=%async_computation | async-start | bytes 524288 | tf_op jit(solution)/shard_map/all_to_all | solution.py:297
  31.0 5.8 %copy-start.1 = (bf16[8192,1024]{1,0:T(8,128)(2,1)S(1)}, bf16[8192,1024]{1,0:T(8,128)(2,1)}, u32[]{:S(2)}) copy-start(bf16[8192,1024]{1,0:T(8,128)(2,1)} %copy-done) | copy-start | bytes 50331652
  36.7 11.7 %slice-start = ((s8[16777216]{0:T(1024)(128)(4,1)}), s8[4194304]{0:T(1024)(128)(4,1)S(1)}, s32[]{:S(2)}) async-start(s8[16777216]{0:T(1024)(128)(4,1)} %bitcast.15), calls=%async_computation.7 | async-start | bytes 8388608
  36.7 11.7 %slice-start.1 = ((s8[16777216]{0:T(1024)(128)(4,1)}), s8[4194304]{0:T(1024)(128)(4,1)S(1)}, s32[]{:S(2)}) async-start(s8[16777216]{0:T(1024)(128)(4,1)} %bitcast.15), calls=%async_computation.8 | async-start | bytes 8388608
  39.4 9.0 %slice-start.2 = ((s8[16777216]{0:T(1024)(128)(4,1)}), s8[4194304]{0:T(1024)(128)(4,1)S(1)}, s32[]{:S(2)}) async-start(s8[16777216]{0:T(1024)(128)(4,1)} %bitcast.15), calls=%async_computation.9 | async-start | bytes 8388608
  39.5 9.0 %slice-start.3 = ((s8[16777216]{0:T(1024)(128)(4,1)}), s8[4194304]{0:T(1024)(128)(4,1)S(1)}, s32[]{:S(2)}) async-start(s8[16777216]{0:T(1024)(128)(4,1)} %bitcast.15), calls=%async_computation.10 | async-start | bytes 8388608
  39.5 2.7 %collective-permute-start = (f32[8,4096]{1,0:T(8,128)S(1)}, f32[8,4096]{1,0:T(8,128)S(1)}, u32[]{:S(2)}, u32[]{:S(2)}) collective-permute-start(f32[8,4096]{1,0:T(8,128)S(1)} %back_0_1.1), channel_id=1, source_target_pairs={{0,1},{1,0},{2,3},{3,2},{4,5},{5,4},{6,7},{7,6},{8,9},{9,8},{10,11... | collective-permute-start | bytes 393224 | tf_op jit(solution)/shard_map/ppermute | solution.py:293
  42.2 6.0 %collective-permute-start.1 = (f32[8,4096]{1,0:T(8,128)S(1)}, f32[8,4096]{1,0:T(8,128)S(1)}, u32[]{:S(2)}, u32[]{:S(2)}) collective-permute-start(f32[8,4096]{1,0:T(8,128)S(1)} %add.6.mine), channel_id=1, source_target_pairs={{0,2},{1,3},{2,0},{3,1},{4,6},{5,7},{6,4},{7,5},{8,10},{9,11},{10,... | collective-permute-start | bytes 393224 | tf_op jit(solution)/shard_map/ppermute | solution.py:293
  48.3 1.7 collective-permute-start.2
  64.6 22.1 %copy-start.11 = (s32[8]{0:T(128)S(1)}, s32[8]{0:T(128)}, u32[]{:S(2)}) copy-start(s32[8]{0:T(128)} %param.15) | copy-start | bytes 100
  67.3 2.7 %collective-permute-start.3 = (f32[8,4096]{1,0:T(8,128)S(1)}, f32[8,4096]{1,0:T(8,128)S(1)}, u32[]{:S(2)}, u32[]{:S(2)}) collective-permute-start(f32[8,4096]{1,0:T(8,128)S(1)} %back_1_1.1), channel_id=1, source_target_pairs={{0,1},{1,0},{2,3},{3,2},{4,5},{5,4},{6,7},{7,6},{8,9},{9,8},{10,11... | collective-permute-start | bytes 393224 | tf_op jit(solution)/shard_map/ppermute | solution.py:293
  70.2 4.2 %collective-permute-start.4 = (f32[8,2048]{1,0:T(8,128)S(1)}, f32[8,2048]{1,0:T(8,128)S(1)}, u32[]{:S(2)}, u32[]{:S(2)}) collective-permute-start(f32[8,2048]{1,0:T(8,128)S(1)} %get-tuple-element.20), channel_id=1, source_target_pairs={{0,0},{1,8},{2,4},{3,12},{4,16},{5,24},{6,20},{7,28},{8,1},{9,9},{... | collective-permute-start | bytes 196616 | tf_op jit(solution)/shard_map/ppermute | solution.py:308
  70.9 8.4 %collective-permute-start.5 = (f32[8,2048]{1,0:T(8,128)S(1)}, f32[8,2048]{1,0:T(8,128)S(1)}, u32[]{:S(2)}, u32[]{:S(2)}) collective-permute-start(f32[8,2048]{1,0:T(8,128)S(1)} %get-tuple-element.19), channel_id=1, source_target_pairs={{0,4},{1,12},{2,0},{3,8},{4,20},{5,28},{6,16},{7,24},{8,5},{9,13},... | collective-permute-start | bytes 196616 | tf_op jit(solution)/shard_map/ppermute | solution.py:308
  80.2 20.2 %all-to-all-start.2 = ((f32[8,8,2048]{2,1,0:T(8,128)}), f32[8,8,2048]{2,1,0:T(8,128)S(1)}, u32[]{:S(2)}, u32[]{:S(2)}) async-start(f32[8,8,2048]{2,1,0:T(8,128)} %broadcast_in_dim.20), calls=%async_computation.2 | async-start | bytes 1048576 | tf_op jit(solution)/shard_map/all_to_all | solution.py:297
  86.8 5.8 %copy-start.2 = (bf16[512,16384]{1,0:T(8,128)(2,1)S(1)}, bf16[512,16384]{1,0:T(8,128)(2,1)}, u32[]{:S(2)}) copy-start(bf16[512,16384]{1,0:T(8,128)(2,1)} %slab.9) | copy-start | bytes 50331652
  92.6 24.4 %copy-start.9 = (s32[512]{0:T(512)S(1)}, s32[512]{0:T(512)}, u32[]{:S(2)}) copy-start(s32[512]{0:T(512)} %param.14) | copy-start | bytes 6148
  100.4 5.8 %copy-start.3 = (bf16[512,16384]{1,0:T(8,128)(2,1)S(1)}, bf16[512,16384]{1,0:T(8,128)(2,1)}, u32[]{:S(2)}) copy-start(bf16[512,16384]{1,0:T(8,128)(2,1)} %slab.9) | copy-start | bytes 50331652
  106.2 61.1 %slice-start.4 = ((s8[16777216]{0:T(1024)(128)(4,1)}), s8[4194304]{0:T(1024)(128)(4,1)S(1)}, s32[]{:S(2)}) async-start(s8[16777216]{0:T(1024)(128)(4,1)} %bitcast.17), calls=%async_computation.11 | async-start | bytes 8388608
  106.2 61.1 %slice-start.5 = ((s8[16777216]{0:T(1024)(128)(4,1)}), s8[4194304]{0:T(1024)(128)(4,1)S(1)}, s32[]{:S(2)}) async-start(s8[16777216]{0:T(1024)(128)(4,1)} %bitcast.17), calls=%async_computation.12 | async-start | bytes 8388608
  122.7 44.6 %slice-start.6 = ((s8[16777216]{0:T(1024)(128)(4,1)}), s8[4194304]{0:T(1024)(128)(4,1)S(1)}, s32[]{:S(2)}) async-start(s8[16777216]{0:T(1024)(128)(4,1)} %bitcast.17), calls=%async_computation.13 | async-start | bytes 8388608
  122.7 44.6 %slice-start.7 = ((s8[16777216]{0:T(1024)(128)(4,1)}), s8[4194304]{0:T(1024)(128)(4,1)S(1)}, s32[]{:S(2)}) async-start(s8[16777216]{0:T(1024)(128)(4,1)} %bitcast.17), calls=%async_computation.14 | async-start | bytes 8388608
  182.3 19.4 %all-to-all-start.5 = ((f32[8,8,2176]{2,1,0:T(8,128)}), f32[8,8,2176]{2,1,0:T(8,128)S(1)}, u32[]{:S(2)}, u32[]{:S(2)}) async-start(f32[8,8,2176]{2,1,0:T(8,128)} %get-tuple-element.17), calls=%async_computation.5 | async-start | bytes 1114112 | tf_op jit(solution)/shard_map/all_to_all | solution.py:297
  (5 other events, 18.7 us)

commit v2 on v1

--- a/solution.py
+++ b/solution.py
@@ -57,7 +57,16 @@
     return pl.ds(pl.multiple_of(start, unit), count)
 
 
-def load_project_kernel(q_hbm, mean_hbm, e_hbm, copies, offset, e_vmem, q, mean, sems):
+def column(row):
+    count = row.shape[1]
+    down = lax.broadcasted_iota(jnp.int32, (count, count), 0)
+    across = lax.broadcasted_iota(jnp.int32, (count, count), 1)
+    return jnp.sum(jnp.where(down == across, row, 0.0), axis=1, keepdims=True)
+
+
+def load_project_kernel(
+    q_hbm, mean_hbm, e_hbm, levels, copies, offset, e_vmem, sigma, mean, q, sems
+):
     pixels = e_hbm.shape[0]
     chunk = pixels // CHUNKS
 
@@ -74,6 +83,13 @@
         for move in moves(c):
             move.start()
 
+    lane = lax.broadcasted_iota(jnp.int32, sigma.shape, 1)
+    table = jnp.zeros(sigma.shape, f32)
+    for t in range(levels.shape[0]):
+        fraction = column(levels[t : t + 1, :].astype(f32)) / (LEVELS - 1)
+        table = jnp.where(lane == t, 0.6 * jnp.exp2(fraction), table)
+    sigma[...] = table
+
     def step(c, total):
         for move in moves(c):
             move.wait()
@@ -87,21 +103,24 @@
         copies[k] = total
 
 
-def load_project(queries, mean, basis, row_count):
+def load_project(queries, mean, basis, levels, row_count):
     pixels, comps = basis.shape
-    basis = pltpu.with_memory_space_constraint(basis, pltpu.HBM)
+    queries, mean, basis = [
+        pltpu.with_memory_space_constraint(x, pltpu.HBM) for x in (queries, mean, basis)
+    ]
     return call(
         load_project_kernel,
         [
             shape((row_count, 8, comps)),
             shape((8, pixels)),
             pltpu.VMEM((pixels, comps), bf16),
+            shape((8, PAD)),
+            shape((1, pixels)),
         ],
-        (queries, mean, basis),
-        in_specs=[anywhere()] * 3,
+        (queries, mean, basis, levels),
+        in_specs=[anywhere()] * 3 + [vmem()],
         scratch=[
             pltpu.VMEM((8, pixels), f32),
-            pltpu.VMEM((1, pixels), f32),
             pltpu.SemaphoreType.DMA((CHUNKS, 3)),
         ],
         flops=16 * pixels * comps,
@@ -190,19 +209,24 @@
         out[lax.rem(k + x, 2)] = sent[:, k * span : (k + 1) * span]
 
 
-def norms_kernel(slab, out):
+def norms_kernel(slab, out, folded):
     rows, pixels = slab.shape
-    tile = 1024
-
-    def step(i, total):
-        part = slab[:, rows_at(i * tile, tile, tile)].astype(f32)
-        square = part * part
-        for k in range(tile // 128):
-            total = total + square[:, k * 128 : (k + 1) * 128]
-        return total
-
-    total = lax.fori_loop(0, pixels // tile, step, jnp.zeros((rows, 128), f32))
-    out[...] = jnp.sum(total, axis=1)[None, :]
+    height, tile = 64, 512
+
+    @pl.loop(0, rows // height)
+    def _(b):
+        at = rows_at(b * height, height, height)
+
+        def step(i, total):
+            part = slab[at, rows_at(i * tile, tile, tile)].astype(f32)
+            for k in range(tile // 128):
+                piece = part[:, k * 128 : (k + 1) * 128]
+                total = total + piece * piece
+            return total
+
+        folded[at, :] = lax.fori_loop(0, pixels // tile, step, jnp.zeros((height, 128), f32))
+
+    out[...] = jnp.sum(folded[...], axis=1)[None, :]
 
 
 def dots_kernel(first, pieces, extra, slab, out):
@@ -237,7 +261,7 @@
         aside[0][...] = jnp.broadcast_to(scale, aside[0].shape)
     now = sigma[:, 2 + step : 3 + step]
     sharp = 1.0 / (2.0 * now * now * math.sqrt(IMAGE_POINTS))
-    bonus = jnp.where(classes[...] == targets[...], STEERING, 0.0).astype(f32)
+    bonus = jnp.where(classes[...].astype(f32) == column(targets[...].astype(f32)), STEERING, 0.0).astype(f32)
     scores = sharp * (2.0 * dots - norm) + bonus
     peak = jnp.max(scores, axis=1, keepdims=True)
     weights = jnp.exp(scores - peak).astype(bf16)
@@ -252,7 +276,7 @@
         out[k, :, span:] = tail
 
 
-def combine_kernel(step, parts, state, scale, sigma, copies):
+def combine_kernel(step, parts, state, scale, sigma, copies, *new_state):
     count, _, width = parts.shape
     span = width - PAD
     peaks = [parts[k, :, span : span + 1] for k in range(count)]
@@ -267,6 +291,8 @@
     current = state[...] if step == 0 else state[...] / scale[:, :1]
     update = average + ratio * (current - average)
     square = jnp.broadcast_to(jnp.sum(update * update, axis=1, keepdims=True), (8, PAD))
+    if new_state:
+        new_state[0][...] = update
     for k in range(count):
         copies[k, :, :span] = update
         copies[k, :, span:] = square
@@ -315,15 +341,15 @@
     pixels, comps = eigenbasis.shape
     slab_rows, slab_pixels = slab.shape
     span = slab_pixels // rows
-    sigma = 0.6 * jnp.exp2(level_ids.T.astype(f32) / (LEVELS - 1))
-    mean = pixel_mean[None, :]
     values = eigenvalues[None, :]
     classes = slab_classes[None, :]
-    targets = target_categories[:, None]
+    targets = target_categories[None, :]
     gauss_flops = 8 * pixels * comps
     slab_flops = 16 * slab_rows * slab_pixels
 
-    copies, offset, basis = load_project(queries, mean, eigenbasis, rows)
+    copies, offset, basis, sigma, mean = load_project(
+        queries, pixel_mean[None, :], eigenbasis, level_ids, rows
+    )
     parts = swap_rows(copies)
     sent = exchange_px(back(0, True, parts, values, sigma, basis), 1)
     image = back(0, False, parts, values, sigma, basis) + sent
@@ -332,9 +358,11 @@
         norms_kernel,
         shape((1, slab_rows)),
         (in_vmem(slab),),
+        scratch=[pltpu.VMEM((slab_rows, 128), f32)],
         flops=2 * slab_rows * slab_pixels,
         name="norms",
     )
+    across, norms = lax.optimization_barrier((across, norms))
     offset = call(
         first_update_kernel,
         shape((8, pixels // 2)),
@@ -365,8 +393,8 @@
         (mine, sent, offset, mean, sigma),
         name="second_update",
     )
-    state = to_slices(outgoing[0], 0) + to_slices(outgoing[1], 1)
-    pieces = swap_rows(jnp.broadcast_to(state[None], (rows, 8, span)))
+    state = [to_slices(outgoing[0], 0) + to_slices(outgoing[1], 1)]
+    pieces = swap_rows(jnp.broadcast_to(state[0][None], (rows, 8, span)))
     products = call(
         functools.partial(dots_kernel, True),
         shape((16, slab_rows)),
@@ -392,13 +420,12 @@
         else:
             scale = aside
         parts = swap_rows(weighted)
-        copies = call(
+        copies, *state = call(
             functools.partial(combine_kernel, step),
-            shape((rows, 8, span + PAD)),
-            (parts, state, sigma if scale is None else scale, sigma),
+            [shape((rows, 8, span + PAD)), shape((8, span))][: 2 - step],
+            (parts, *state, sigma if scale is None else scale, sigma),
             name=f"combine_{step}",
         )
-        state = copies[0, :, :span]
         pieces = swap_rows(copies)
         if step == 0:
             products = call(

time: 229 us -> 198 us (0.86)
  blocking collectives: 89.6 us -> 141 us
  local copies, waits for them, and re-layouts: 31.6 us -> 0.77 us
  waiting for transfers between devices: 34 us -> 4.7 us
  starting transfers between devices: 23.2 us -> 6.26 us
  Pallas kernels: 49.6 us -> 44.9 us
    all_to_all x4 -> x7, blocking collectives: 73.5 us -> 125 us  [swap_rows(): return lax.all_to_all(x, 'rows', 0, 0, tiled=True)]
    unnamed x41 -> x16, local copies, waits for them, and re-layouts: 30.6 us -> 0.73 us
    all_to_all x3 -> x0, waiting for transfers between devices: 24.7 us -> none  [swap_rows(): return lax.all_to_all(x, 'rows', 0, 0, tiled=True)]
    all_to_all x3 -> x0, starting transfers between devices: 17.4 us -> none  [swap_rows(): return lax.all_to_all(x, 'rows', 0, 0, tiled=True)]
    pallas_call x18, Pallas kernels: 49.6 us -> 44.9 us  [call(): pl.pallas_call(kernel, in_specs=in_specs or [vmem()] * len(args), out_spe...]
    ppermute x4, waiting for transfers between devices: 4.42 us -> 0.01 us  [exchange_px(): return lax.ppermute(x, 'px', [(i, i ^ flip) for i in range(size)])]
  transfers between devices with their start and end apart: 9 -> 6, of which waited for: 4 -> 1; matrix products, arithmetic and copies ran while one was open for 0% -> 0% of each run, Pallas kernels for 6% -> 6%
where the time goes in v2:
time: 198 us
  blocking collectives  141 us (71%)
  Pallas kernels  44.9 us (23%)
  starting transfers between devices  6.26 us (3%)
  waiting for transfers between devices  4.7 us (2%)
    all_to_all x7, blocking collectives, swap_rows(): return lax.all_to_all(x, 'rows', 0, 0, tiled=True)  125 us
    pallas_call x18, Pallas kernels, call(): pl.pallas_call(kernel, in_specs=in_specs or [vmem()] * len(args), out_spe...  44.9 us
    all_gather x2, blocking collectives, shards(): gathered = lax.all_gather(products, 'px')  10.9 us
    all_gather x1, blocking collectives, shards(): squares = lax.all_gather(squares, 'px')  5.17 us
    ppermute x2, waiting for transfers between devices, to_slices(): return lax.ppermute(x, ('rows', 'px'), pairs)  4.69 us
    ppermute x2, starting transfers between devices, to_slices(): return lax.ppermute(x, ('rows', 'px'), pairs)  4.39 us
  transfers between devices with their start and end apart: 6, of which 1 were waited for; matrix products, arithmetic and copies ran while one was open for 0% of the time, Pallas kernels for 6%

profile of v2, /device:TPU:0, one launch (start us, length us, event | category | flops | bytes accessed | tf_op | source)
XLA Modules:
  0.0 197.7 jit_solution(7654722197092053126)
XLA Ops:
  0.7 6.6 %load_project.1 = (f32[8,8,1024]{2,1,0:T(8,128)S(1)}, f32[8,8192]{1,0:T(8,128)S(1)}, bf16[8192,1024]{1,0:T(8,128)(2,1)S(1)}, f32[8,128]{1,0:T(8,128)S(1)}, f32[1,8192]{1,0:T(1,128)S(1)}) custom-call(f32[8,8192]{1,0:T(8,128)} %q_hbm.1, f32[1,8192]{1,0:T(1,128)} %bitcast.24, bf16[8192,1024]{1,0:T(8,128)(2,1)} %e_hbm.1, s32[5,8]{1,0:T(8,128)S(1)} %copy-done.2), custom_call_target="tpu_custom_call" | custom-call | flops 134217728 | bytes 16777216 | tf_op jit(solution)/shard_map/load_project/pallas_call | solution.py:42
  7.3 16.0 %all_to_all.35.parts = f32[8,8,1024]{2,1,0:T(8,128)S(1)} all-to-all(f32[8,8,1024]{2,1,0:T(8,128)S(1)} %get-tuple-element.18), channel_id=1, replica_groups=mesh['rows'=8,'px'=4] {'rows'}, dimensions={0} | all-to-all | bytes 524288 | tf_op jit(solution)/shard_map/all_to_all | solution.py:323
  23.3 2.7 %back_0_1.1 = f32[8,4096]{1,0:T(8,128)S(1)} custom-call(f32[8,8,1024]{2,1,0:T(8,128)S(1)} %all_to_all.35.parts, f32[1,1024]{1,0:T(1,128)S(1)} %bitcast.16, f32[8,128]{1,0:T(8,128)S(1)} %get-tuple-element.19.sigma.scale, bf16[8192,1024]{1,0:T(8,128)(2,1)S(1)} %get-tuple-element.20.e_vmem), custom_call_target="tpu_custom_call" | custom-call | flops 67108864 | bytes 16777216 | tf_op jit(solution)/shard_map/back_0_1/pallas_call | solution.py:42
  26.1 2.7 %back_0_0.1 = f32[8,4096]{1,0:T(8,128)S(1)} custom-call(f32[8,8,1024]{2,1,0:T(8,128)S(1)} %all_to_all.35.parts, f32[1,1024]{1,0:T(1,128)S(1)} %bitcast.17, f32[8,128]{1,0:T(8,128)S(1)} %get-tuple-element.19.sigma.scale, bf16[8192,1024]{1,0:T(8,128)(2,1)S(1)} %get-tuple-element.20.e_vmem), custom_call_target="tpu_custom_call" | custom-call | flops 67108864 | bytes 16777216 | tf_op jit(solution)/shard_map/back_0_0/pallas_call | solution.py:42
  30.4 4.6 %norms.1.extra = f32[1,512]{1,0:T(1,128)S(1)} custom-call(bf16[512,16384]{1,0:T(8,128)(2,1)S(1)} %bitcast.12), custom_call_target="tpu_custom_call" | custom-call | flops 16777216 | bytes 16777216 | tf_op jit(solution)/shard_map/norms/pallas_call | solution.py:42
  35.5 1.6 project_own.1.own
  37.0 1.6 project_rest.1
  38.6 12.8 %all_to_all.36.parts = f32[8,8,1024]{2,1,0:T(8,128)S(1)} all-to-all(f32[8,8,1024]{2,1,0:T(8,128)S(1)} %project_rest.1), channel_id=1, replica_groups=mesh['rows'=8,'px'=4] {'rows'}, dimensions={0} | all-to-all | bytes 524288 | tf_op jit(solution)/shard_map/all_to_all | solution.py:323
  51.4 2.7 %back_1_1.1 = f32[8,4096]{1,0:T(8,128)S(1)} custom-call(f32[8,8,1024]{2,1,0:T(8,128)S(1)} %all_to_all.36.parts, f32[1,1024]{1,0:T(1,128)S(1)} %bitcast.18, f32[8,128]{1,0:T(8,128)S(1)} %get-tuple-element.19.sigma.scale, bf16[8192,1024]{1,0:T(8,128)(2,1)S(1)} %get-tuple-element.20.e_vmem), custom_call_target="tpu_custom_call" | custom-call | flops 67108864 | bytes 16777216 | tf_op jit(solution)/shard_map/back_1_1/pallas_call | solution.py:42
  54.1 2.7 %back_1_0.1.mine = f32[8,4096]{1,0:T(8,128)S(1)} custom-call(f32[8,8,1024]{2,1,0:T(8,128)S(1)} %all_to_all.36.parts, f32[1,1024]{1,0:T(1,128)S(1)} %bitcast.19, f32[8,128]{1,0:T(8,128)S(1)} %get-tuple-element.19.sigma.scale, bf16[8192,1024]{1,0:T(8,128)(2,1)S(1)} %get-tuple-element.20.e_vmem), custom_call_target="tpu_custom_call" | custom-call | flops 67108864 | bytes 16777216 | tf_op jit(solution)/shard_map/back_1_0/pallas_call | solution.py:42
  57.7 3.7 %collective-permute-start.5 = (f32[8,2048]{1,0:T(8,128)S(1)}, f32[8,2048]{1,0:T(8,128)S(1)}, u32[]{:S(2)}, u32[]{:S(2)}) collective-permute-start(f32[8,2048]{1,0:T(8,128)S(1)} %get-tuple-element.31), channel_id=1, source_target_pairs={{0,4},{1,12},{2,0},{3,8},{4,20},{5,28},{6,16},{7,24},{8,5},{9,13},... | collective-permute-start | bytes 196616 | tf_op jit(solution)/shard_map/ppermute | solution.py:334
  61.4 4.7 %collective-permute-done.5 = f32[8,2048]{1,0:T(8,128)S(1)} collective-permute-done((f32[8,2048]{1,0:T(8,128)S(1)}, f32[8,2048]{1,0:T(8,128)S(1)}, u32[]{:S(2)}, u32[]{:S(2)}) %collective-permute-start.5) | collective-permute-done | bytes 65568 | tf_op jit(solution)/shard_map/ppermute | solution.py:334
  66.2 19.7 %all_to_all.37.pieces = f32[8,8,2048]{2,1,0:T(8,128)S(1)} all-to-all(f32[8,8,2048]{2,1,0:T(8,128)S(1)} %broadcast_in_dim.20), channel_id=1, replica_groups=mesh['rows'=8,'px'=4] {'rows'}, dimensions={0} | all-to-all | bytes 1048576 | tf_op jit(solution)/shard_map/all_to_all | solution.py:323
  85.9 5.3 %dots_0.1 = f32[16,512]{1,0:T(8,128)S(1)} custom-call(f32[8,8,2048]{2,1,0:T(8,128)S(1)} %all_to_all.37.pieces, f32[1,512]{1,0:T(1,128)S(1)} %norms.1.extra, bf16[512,16384]{1,0:T(8,128)(2,1)S(1)} %bitcast.12), custom_call_target="tpu_custom_call" | custom-call | flops 134217728 | bytes 16777216 | tf_op jit(solution)/shard_map/dots_0/pallas_call | solution.py:42
  91.2 5.4 %all-gather = f32[64,512]{1,0:T(8,128)S(1)} all-gather(f32[16,512]{1,0:T(8,128)S(1)} %dots_0.1), channel_id=2, replica_groups=mesh['rows'=8,'px'=4] {'px'}, dimensions={0}, use_global_device_ids=true | all-gather | bytes 163840 | tf_op jit(solution)/shard_map/all_gather | solution.py:407
  96.6 3.4 %weighted_0.1 = (f32[8,8,2176]{2,1,0:T(8,128)S(1)}, f32[1,512]{1,0:T(1,128)S(1)}) custom-call(f32[4,16,512]{2,1,0:T(8,128)S(1)} %bitcast.13, f32[1,512]{1,0:T(1,128)S(1)} %norms.1.extra, s32[1,512]{1,0:T(1,128)S(1)} %bitcast.20, s32[1,8]{1,0:T(1,128)S(1)} %bitcast.22, f32[8,128]{1,0:T(8,128)S(1)} %get-tuple-element.19.sigma.scale, ...), custom_call_target="tpu_custom_call" | custom-call | flops 134217728 | bytes 16777216 | tf_op jit(solution)/shard_map/weighted_0/pallas_call | solution.py:42
  100.0 19.9 %all_to_all.38.parts = f32[8,8,2176]{2,1,0:T(8,128)S(1)} all-to-all(f32[8,8,2176]{2,1,0:T(8,128)S(1)} %get-tuple-element.25), channel_id=1, replica_groups=mesh['rows'=8,'px'=4] {'rows'}, dimensions={0} | all-to-all | bytes 1114112 | tf_op jit(solution)/shard_map/all_to_all | solution.py:323
  120.1 18.7 %all_to_all.39.pieces = f32[8,8,2176]{2,1,0:T(8,128)S(1)} all-to-all(f32[8,8,2176]{2,1,0:T(8,128)S(1)} %get-tuple-element.26), channel_id=1, replica_groups=mesh['rows'=8,'px'=4] {'rows'}, dimensions={0} | all-to-all | bytes 1114112 | tf_op jit(solution)/shard_map/all_to_all | solution.py:323
  138.8 5.4 %dots_1.1 = f32[16,512]{1,0:T(8,128)S(1)} custom-call(f32[8,8,2176]{2,1,0:T(8,128)S(1)} %all_to_all.39.pieces, f32[1,512]{1,0:T(1,128)S(1)} %get-tuple-element.27.extra.norms, bf16[512,16384]{1,0:T(8,128)(2,1)S(1)} %bitcast.12), custom_call_target="tpu_custom_call" | custom-call | flops 134217728 | bytes 16777216 | tf_op jit(solution)/shard_map/dots_1/pallas_call | solution.py:42
  144.2 5.4 %all-gather.1 = f32[64,512]{1,0:T(8,128)S(1)} all-gather(f32[16,512]{1,0:T(8,128)S(1)} %dots_1.1), channel_id=3, replica_groups=mesh['rows'=8,'px'=4] {'px'}, dimensions={0}, use_global_device_ids=true | all-gather | bytes 163840 | tf_op jit(solution)/shard_map/all_gather | solution.py:407
  149.6 3.4 %weighted_1.1 = (f32[8,8,2176]{2,1,0:T(8,128)S(1)}, f32[8,128]{1,0:T(8,128)S(1)}) custom-call(f32[4,16,512]{2,1,0:T(8,128)S(1)} %bitcast.14, f32[1,512]{1,0:T(1,128)S(1)} %get-tuple-element.27.extra.norms, s32[1,512]{1,0:T(1,128)S(1)} %bitcast.21, s32[1,8]{1,0:T(1,128)S(1)} %bitcast.23, f32[8,128]{1,0:T(8,128)S(1)} %get-tuple-element.19.sigma.scale, ...), custom_call_target="tpu_custom_call" | custom-call | flops 134217728 | bytes 16777216 | tf_op jit(solution)/shard_map/weighted_1/pallas_call | solution.py:42
  153.0 19.1 %all_to_all.40.parts = f32[8,8,2176]{2,1,0:T(8,128)S(1)} all-to-all(f32[8,8,2176]{2,1,0:T(8,128)S(1)} %get-tuple-element.28), channel_id=1, replica_groups=mesh['rows'=8,'px'=4] {'rows'}, dimensions={0} | all-to-all | bytes 1114112 | tf_op jit(solution)/shard_map/all_to_all | solution.py:323
  172.4 18.7 %all_to_all.41.pieces = f32[8,8,2176]{2,1,0:T(8,128)S(1)} all-to-all(f32[8,8,2176]{2,1,0:T(8,128)S(1)} %combine_1.1), channel_id=1, replica_groups=mesh['rows'=8,'px'=4] {'rows'}, dimensions={0} | all-to-all | bytes 1114112 | tf_op jit(solution)/shard_map/all_to_all | solution.py:323
  191.1 5.2 %all-gather.2 = f32[32,128]{1,0:T(8,128)S(1)} all-gather(f32[8,128]{1,0:T(8,128)S(1)} %squares.1), channel_id=4, replica_groups=mesh['rows'=8,'px'=4] {'px'}, dimensions={0}, use_global_device_ids=true | all-gather | bytes 20480 | tf_op jit(solution)/shard_map/all_gather | solution.py:439
  (37 shorter events, 5.7 us)
Async XLA Ops:
  0.0 23.3 %copy-start = (f32[1024]{0:T(1024)S(1)}, f32[1024]{0:T(1024)}, u32[]{:S(2)}) copy-start(f32[1024]{0:T(1024)} %param.11) | copy-start | bytes 12292
  0.0 0.7 copy-start.2
  23.3 7.0 %slice-start = ((s8[16777216]{0:T(1024)(128)(4,1)}), s8[4194304]{0:T(1024)(128)(4,1)S(1)}, s32[]{:S(2)}) async-start(s8[16777216]{0:T(1024)(128)(4,1)} %bitcast.11), calls=%async_computation.7 | async-start | bytes 8388608
  23.3 7.0 %slice-start.1 = ((s8[16777216]{0:T(1024)(128)(4,1)}), s8[4194304]{0:T(1024)(128)(4,1)S(1)}, s32[]{:S(2)}) async-start(s8[16777216]{0:T(1024)(128)(4,1)} %bitcast.11), calls=%async_computation.8 | async-start | bytes 8388608
  26.0 4.3 %slice-start.2 = ((s8[16777216]{0:T(1024)(128)(4,1)}), s8[4194304]{0:T(1024)(128)(4,1)S(1)}, s32[]{:S(2)}) async-start(s8[16777216]{0:T(1024)(128)(4,1)} %bitcast.11), calls=%async_computation.9 | async-start | bytes 8388608
  26.0 4.3 %slice-start.3 = ((s8[16777216]{0:T(1024)(128)(4,1)}), s8[4194304]{0:T(1024)(128)(4,1)S(1)}, s32[]{:S(2)}) async-start(s8[16777216]{0:T(1024)(128)(4,1)} %bitcast.11), calls=%async_computation.10 | async-start | bytes 8388608
  26.0 2.7 %collective-permute-start = (f32[8,4096]{1,0:T(8,128)S(1)}, f32[8,4096]{1,0:T(8,128)S(1)}, u32[]{:S(2)}, u32[]{:S(2)}) collective-permute-start(f32[8,4096]{1,0:T(8,128)S(1)} %back_0_1.1), channel_id=1, source_target_pairs={{0,1},{1,0},{2,3},{3,2},{4,5},{5,4},{6,7},{7,6},{8,9},{9,8},{10,11... | collective-permute-start | bytes 393224 | tf_op jit(solution)/shard_map/ppermute | solution.py:319
  28.8 6.2 %collective-permute-start.1 = (f32[8,4096]{1,0:T(8,128)S(1)}, f32[8,4096]{1,0:T(8,128)S(1)}, u32[]{:S(2)}, u32[]{:S(2)}) collective-permute-start(f32[8,4096]{1,0:T(8,128)S(1)} %add.6.mine), channel_id=1, source_target_pairs={{0,2},{1,3},{2,0},{3,1},{4,6},{5,7},{6,4},{7,5},{8,10},{9,11},{10,... | collective-permute-start | bytes 393224 | tf_op jit(solution)/shard_map/ppermute | solution.py:319
  35.2 1.9 collective-permute-start.2
  54.1 42.5 %copy-start.1 = (s32[512]{0:T(512)S(1)}, s32[512]{0:T(512)}, u32[]{:S(2)}) copy-start(s32[512]{0:T(512)} %param.14) | copy-start | bytes 6148
  54.1 42.5 %copy-start.3 = (s32[8]{0:T(128)S(1)}, s32[8]{0:T(128)}, u32[]{:S(2)}) copy-start(s32[8]{0:T(128)} %param.15) | copy-start | bytes 100
  54.1 2.7 %collective-permute-start.3 = (f32[8,4096]{1,0:T(8,128)S(1)}, f32[8,4096]{1,0:T(8,128)S(1)}, u32[]{:S(2)}, u32[]{:S(2)}) collective-permute-start(f32[8,4096]{1,0:T(8,128)S(1)} %back_1_1.1), channel_id=1, source_target_pairs={{0,1},{1,0},{2,3},{3,2},{4,5},{5,4},{6,7},{7,6},{8,9},{9,8},{10,11... | collective-permute-start | bytes 393224 | tf_op jit(solution)/shard_map/ppermute | solution.py:319
  57.0 4.4 %collective-permute-start.4 = (f32[8,2048]{1,0:T(8,128)S(1)}, f32[8,2048]{1,0:T(8,128)S(1)}, u32[]{:S(2)}, u32[]{:S(2)}) collective-permute-start(f32[8,2048]{1,0:T(8,128)S(1)} %get-tuple-element.32), channel_id=1, source_target_pairs={{0,0},{1,8},{2,4},{3,12},{4,16},{5,24},{6,20},{7,28},{8,1},{9,9},{... | collective-permute-start | bytes 196616 | tf_op jit(solution)/shard_map/ppermute | solution.py:334
  57.7 8.4 %collective-permute-start.5 = (f32[8,2048]{1,0:T(8,128)S(1)}, f32[8,2048]{1,0:T(8,128)S(1)}, u32[]{:S(2)}, u32[]{:S(2)}) collective-permute-start(f32[8,2048]{1,0:T(8,128)S(1)} %get-tuple-element.31), channel_id=1, source_target_pairs={{0,4},{1,12},{2,0},{3,8},{4,20},{5,28},{6,16},{7,24},{8,5},{9,13},... | collective-permute-start | bytes 196616 | tf_op jit(solution)/shard_map/ppermute | solution.py:334

commit v3 on v2

--- a/solution.py
+++ b/solution.py
@@ -229,94 +229,217 @@
     out[...] = jnp.sum(folded[...], axis=1)[None, :]
 
 
-def dots_kernel(first, pieces, extra, slab, out):
-    count, _, width = pieces.shape
-    span = slab.shape[1] // count
-
-    def step(k, total):
-        part = pieces[k, :, :span].astype(bf16)
-        at = rows_at(k * span, span, span)
-        return total + lax.dot_general(part, slab[:, at], NT, preferred_element_type=f32)
-
-    out[:8] = lax.fori_loop(0, count, step, jnp.zeros((8, slab.shape[0]), f32))
-    if first:
-        out[8:] = jnp.broadcast_to(extra[...], (8, slab.shape[0]))
-    else:
-        squares = jnp.sum(pieces[:, :, span:], axis=0)[:, :1]
-        out[8:] = jnp.broadcast_to(squares, (8, slab.shape[0]))
-
-
-def weighted_kernel(step, gathered, norms, classes, targets, sigma, slab, out, *aside):
-    count, _, width = out.shape
-    span = width - PAD
+def block_at(k, span):
+    block = lax.bitwise_xor(lax.axis_index("rows"), k)
+    return rows_at(block * span, span, span)
+
+
+def dots_kernel(offsets, *refs):
+    *inputs, slab, out = refs
+    pieces, before = inputs[: len(offsets)], inputs[len(offsets) :]
+    span = slab.shape[1] // lax.axis_size("rows")
+    total = before[0][:8] if before else jnp.zeros((8, slab.shape[0]), f32)
+    rest = before[0][8:] if before else jnp.zeros((8, slab.shape[0]), f32)
+    for piece, ks in zip(pieces, offsets):
+        for i, k in enumerate(ks):
+            block = piece if len(piece.shape) == 2 else piece.at[i]
+            total = total + lax.dot_general(
+                block[:, :span].astype(bf16),
+                slab[:, block_at(k, span)],
+                NT,
+                preferred_element_type=f32,
+            )
+            if block.shape[1] > span:
+                lane = lax.broadcasted_iota(jnp.int32, rest.shape, 1)
+                rest = rest + jnp.where(lane >= 0, block[:, span : span + 1], 0.0)
+    out[:8] = total
+    out[8:] = rest
+
+
+def dots(pieces, offsets, before, slab, name):
+    rows = lax.axis_size("rows")
+    count = sum(len(ks) for ks in offsets)
+    return call(
+        functools.partial(dots_kernel, offsets),
+        shape((16, slab.shape[0])),
+        (*pieces, *before, in_vmem(slab)),
+        flops=16 * count * slab.shape[0] * (slab.shape[1] // rows),
+        name=name,
+    )
+
+
+def put_chunks(weights, tail, ks, slab, out):
+    span = slab.shape[1] // lax.axis_size("rows")
+    for i, k in enumerate(ks):
+        out[i, :, :span] = jnp.dot(
+            weights, slab[:, block_at(k, span)], preferred_element_type=f32
+        )
+        out[i, :, span:] = tail
+
+
+def scores_kernel(step, ks, gathered, norms, classes, targets, sigma, slab, out, kept, tails, aside):
     both = jnp.sum(gathered[...], axis=0)
-    dots = both[:8]
+    inner = both[:8]
     if step == 0:
         norm = both[8:9]
-        aside[0][...] = norm
+        aside[...] = jnp.broadcast_to(norm, aside.shape)
     else:
-        norm = norms[...]
+        norm = norms[:1]
         scale = jnp.sqrt(both[8:, :1] / IMAGE_POINTS + RMS_EPSILON)
-        dots = dots / scale
-        aside[0][...] = jnp.broadcast_to(scale, aside[0].shape)
+        inner = inner / scale
+        aside[...] = jnp.broadcast_to(scale, aside.shape)
     now = sigma[:, 2 + step : 3 + step]
     sharp = 1.0 / (2.0 * now * now * math.sqrt(IMAGE_POINTS))
-    bonus = jnp.where(classes[...].astype(f32) == column(targets[...].astype(f32)), STEERING, 0.0).astype(f32)
-    scores = sharp * (2.0 * dots - norm) + bonus
+    wanted = column(targets[...].astype(f32))
+    bonus = jnp.where(classes[...].astype(f32) == wanted, STEERING, 0.0).astype(f32)
+    scores = sharp * (2.0 * inner - norm) + bonus
     peak = jnp.max(scores, axis=1, keepdims=True)
     weights = jnp.exp(scores - peak).astype(bf16)
+    kept[...] = weights.astype(f32)
     mass = jnp.sum(weights.astype(f32), axis=1, keepdims=True)
     lane = lax.broadcasted_iota(jnp.int32, (8, PAD), 1)
     tail = jnp.where(lane < PAD // 2, peak, mass)
-
-    @pl.loop(0, count)
-    def _(k):
-        at = rows_at(k * span, span, span)
-        out[k, :, :span] = jnp.dot(weights, slab[:, at], preferred_element_type=f32)
-        out[k, :, span:] = tail
-
-
-def combine_kernel(step, parts, state, scale, sigma, copies, *new_state):
-    count, _, width = parts.shape
-    span = width - PAD
-    peaks = [parts[k, :, span : span + 1] for k in range(count)]
+    tails[...] = tail
+    put_chunks(weights, tail, ks, slab, out)
+
+
+def chunks_kernel(ks, kept, tails, slab, out):
+    put_chunks(kept[...].astype(bf16), tails[...], ks, slab, out)
+
+
+def merge(parts, span):
+    peaks = [part[:, span : span + 1] for part in parts]
+    masses = [part[:, span + PAD // 2 : span + PAD // 2 + 1] for part in parts]
     top = functools.reduce(jnp.maximum, peaks)
-    total, mass = jnp.zeros((8, span), f32), jnp.zeros((8, 1), f32)
-    for k in range(count):
-        factor = jnp.exp(peaks[k] - top)
-        total = total + factor * parts[k, :, :span]
-        mass = mass + factor * parts[k, :, span + PAD // 2 : span + PAD // 2 + 1]
+    total, mass = 0.0, 0.0
+    for part, peak, part_mass in zip(parts, peaks, masses):
+        factor = jnp.exp(peak - top)
+        total = total + factor * part[:, :span]
+        mass = mass + factor * part_mass
+    return top, mass, total
+
+
+def merge_kernel(mine, theirs, *outs):
+    span = mine.shape[2] - PAD
+    lane = lax.broadcasted_iota(jnp.int32, (8, PAD), 1)
+    for i, out in enumerate(outs):
+        top, mass, total = merge([mine.at[i], theirs.at[i]], span)
+        out[:, :span] = total
+        out[:, span:] = jnp.where(lane < PAD // 2, top, mass)
+
+
+def combine_kernel(step, count, *refs):
+    parts = refs[:count]
+    state, scale, sigma, out = refs[count:]
+    span = out.shape[1] - PAD
+    _, mass, total = merge(parts, span)
     average = total / mass
     ratio = sigma[:, 3 + step : 4 + step] / sigma[:, 2 + step : 3 + step]
-    current = state[...] if step == 0 else state[...] / scale[:, :1]
+    current = state[:, :span]
+    if step:
+        current = current / scale[:, :1]
     update = average + ratio * (current - average)
-    square = jnp.broadcast_to(jnp.sum(update * update, axis=1, keepdims=True), (8, PAD))
-    if new_state:
-        new_state[0][...] = update
-    for k in range(count):
-        copies[k, :, :span] = update
-        copies[k, :, span:] = square
-
-
-def squares_kernel(pieces, out):
-    span = pieces.shape[2] - PAD
-    out[...] = jnp.sum(pieces[:, :, span:], axis=0)
-
-
-def finish_kernel(pieces, squares, out):
-    count, _, width = pieces.shape
-    span = width - PAD
+    out[:, :span] = update
+    out[:, span:] = jnp.broadcast_to(jnp.sum(update * update, axis=1, keepdims=True), (8, PAD))
+
+
+def spread(flat):
+    evens = list(range(0, flat, 2))
+    near, far = evens[: len(evens) // 2], evens[len(evens) // 2 :]
+    return near, far
+
+
+def gather_rows(state):
+    rows = lax.axis_size("rows")
+    near, far = spread(rows)
+    got = {k: exchange("rows", state, k) if k else state for k in near + far}
+    first = exchange("rows", jnp.stack([got[k] for k in near]), 1)
+    second = exchange("rows", jnp.stack([got[k] for k in far]), 1)
+    pieces = [got[k] for k in near + far] + [first, second]
+    offsets = [(k,) for k in near + far]
+    offsets += [tuple(k ^ 1 for k in near), tuple(k ^ 1 for k in far)]
+    return pieces, offsets
+
+
+def gather_dots(state, slab, name):
+    pieces, offsets = gather_rows(state)
+    evens = len(offsets) - 2
+    total = dots(pieces[:1], offsets[:1], (), slab, name + "_own")
+    for i, (lo, hi) in enumerate(
+        ((1, evens // 2), (evens // 2, evens), (evens, evens + 1), (evens + 1, evens + 2))
+    ):
+        if hi > lo:
+            total = dots(pieces[lo:hi], offsets[lo:hi], (total,), slab, f"{name}_{i}")
+    return total
+
+
+def reduce_rows(step, gathered, norms, classes, targets, sigma, slab):
+    rows = lax.axis_size("rows")
+    slab_rows, slab_pixels = slab.shape
+    span = slab_pixels // rows
+    near, far = spread(rows)
+    unit = 16 * slab_rows * span
+
+    def chunks(ks, name):
+        return call(
+            functools.partial(chunks_kernel, ks),
+            shape((len(ks), 8, span + PAD)),
+            (kept, tails, in_vmem(slab)),
+            flops=unit * len(ks),
+            name=f"{name}_{step}",
+        )
+
+    def merged(mine, theirs, name):
+        outs = [shape((8, span + PAD))] * mine.shape[0]
+        return call(merge_kernel, outs, (mine, theirs), name=f"{name}_{step}")
+
+    ks = tuple(k ^ 1 for k in far)
+    across, kept, tails, aside = call(
+        functools.partial(scores_kernel, step, ks),
+        [
+            shape((len(ks), 8, span + PAD)),
+            shape((8, slab_rows)),
+            shape((8, PAD)),
+            shape((8, slab_rows)),
+        ],
+        (gathered, norms, classes, targets, sigma, in_vmem(slab)),
+        flops=unit * len(ks),
+        name=f"scores_{step}",
+    )
+    across = exchange("rows", across, 1)
+    beside = exchange("rows", chunks(tuple(k ^ 1 for k in near), "near_across"), 1)
+    sent = merged(chunks(tuple(near), "near_own"), beside, "near_merge")
+    parts = [exchange("rows", x, k) if k else x for x, k in zip(sent, near)]
+    sent = merged(chunks(tuple(far), "far_own"), across, "far_merge")
+    parts += [exchange("rows", x, k) for x, k in zip(sent, far)]
+    return parts, aside
+
+
+def squares_kernel(*refs):
+    *pieces, out = refs
+    total = jnp.zeros(out.shape, f32)
+    for piece in pieces:
+        span = piece.shape[-1] - PAD
+        if len(piece.shape) == 2:
+            total = total + piece[:, span:]
+        else:
+            total = total + jnp.sum(piece[:, :, span:], axis=0)
+    out[...] = total
+
+
+def finish_kernel(offsets, *refs):
+    *pieces, squares, out = refs
     total = jnp.sum(squares[...], axis=0)[:, :1]
-    scale = jnp.sqrt(total / IMAGE_POINTS + RMS_EPSILON)
-
-    @pl.loop(0, count)
-    def _(k):
-        out[:, rows_at(k * span, span, span)] = pieces[k, :, :span] / scale
-
-
-def exchange_px(x, flip):
-    size = lax.axis_size("px")
-    return lax.ppermute(x, "px", [(i, i ^ flip) for i in range(size)])
+    scale = 1.0 / jnp.sqrt(total / IMAGE_POINTS + RMS_EPSILON)
+    for piece, ks in zip(pieces, offsets):
+        span = piece.shape[-1] - PAD
+        for i, k in enumerate(ks):
+            block = piece if len(piece.shape) == 2 else piece.at[i]
+            out[:, block_at(k, span)] = block[:, :span] * scale
+
+
+def exchange(axis, x, flip):
+    return lax.ppermute(x, axis, [(i, i ^ flip) for i in range(lax.axis_size(axis))])
 
 
 def swap_rows(x):
@@ -345,15 +468,14 @@
     classes = slab_classes[None, :]
     targets = target_categories[None, :]
     gauss_flops = 8 * pixels * comps
-    slab_flops = 16 * slab_rows * slab_pixels
 
     copies, offset, basis, sigma, mean = load_project(
         queries, pixel_mean[None, :], eigenbasis, level_ids, rows
     )
     parts = swap_rows(copies)
-    sent = exchange_px(back(0, True, parts, values, sigma, basis), 1)
+    sent = exchange("px", back(0, True, parts, values, sigma, basis), 1)
     image = back(0, False, parts, values, sigma, basis) + sent
-    across = exchange_px(image, 2)
+    across = exchange("px", image, 2)
     norms = call(
         norms_kernel,
         shape((1, slab_rows)),
@@ -369,7 +491,7 @@
         (image, across, offset, sigma),
         name="first_update",
     )
-    other = exchange_px(offset, 1)
+    other = exchange("px", offset, 1)
     own = call(
         functools.partial(project_half_kernel, False),
         shape((8, comps)),
@@ -385,7 +507,7 @@
         name="project_rest",
     )
     parts = swap_rows(copies)
-    sent = exchange_px(back(1, True, parts, values, sigma, basis), 1)
+    sent = exchange("px", back(1, True, parts, values, sigma, basis), 1)
     mine = back(1, False, parts, values, sigma, basis)
     outgoing = call(
         second_update_kernel,
@@ -393,51 +515,34 @@
         (mine, sent, offset, mean, sigma),
         name="second_update",
     )
-    state = [to_slices(outgoing[0], 0) + to_slices(outgoing[1], 1)]
-    pieces = swap_rows(jnp.broadcast_to(state[0][None], (rows, 8, span)))
-    products = call(
-        functools.partial(dots_kernel, True),
-        shape((16, slab_rows)),
-        (pieces, norms, in_vmem(slab)),
-        flops=slab_flops,
-        name="dots_0",
-    )
-    scale = None
+    state = to_slices(outgoing[0], 0) + to_slices(outgoing[1], 1)
+    products = gather_dots(state, slab, "dots_0")
+    products = jnp.concatenate([products[:8], jnp.broadcast_to(norms, (8, slab_rows))])
+    scale = norms
     for step in range(2):
         gathered = lax.all_gather(products, "px")
-        weighted, aside = call(
-            functools.partial(weighted_kernel, step),
-            [
-                shape((rows, 8, span + PAD)),
-                shape((1, slab_rows)) if step == 0 else shape((8, PAD)),
-            ],
-            (gathered, norms, classes, targets, sigma, in_vmem(slab)),
-            flops=slab_flops,
-            name=f"weighted_{step}",
-        )
+        parts, aside = reduce_rows(step, gathered, norms, classes, targets, sigma, slab)
         if step == 0:
             norms = aside
         else:
             scale = aside
-        parts = swap_rows(weighted)
-        copies, *state = call(
-            functools.partial(combine_kernel, step),
-            [shape((rows, 8, span + PAD)), shape((8, span))][: 2 - step],
-            (parts, *state, sigma if scale is None else scale, sigma),
+        state = call(
+            functools.partial(combine_kernel, step, len(parts)),
+            shape((8, span + PAD)),
+            (*parts, state, scale, sigma),
             name=f"combine_{step}",
         )
-        pieces = swap_rows(copies)
         if step == 0:
-            products = call(
-                functools.partial(dots_kernel, False),
-                shape((16, slab_rows)),
-                (pieces, norms, in_vmem(slab)),
-                flops=slab_flops,
-                name="dots_1",
-            )
-    squares = call(squares_kernel, shape((8, PAD)), (pieces,), name="squares")
+            products = gather_dots(state, slab, "dots_1")
+    pieces, offsets = gather_rows(state)
+    squares = call(squares_kernel, shape((8, PAD)), pieces, name="squares")
     squares = lax.all_gather(squares, "px")
-    return call(finish_kernel, shape((8, slab_pixels)), (pieces, squares), name="finish")
+    return call(
+        functools.partial(finish_kernel, offsets),
+        shape((8, slab_pixels)),
+        (*pieces, squares),
+        name="finish",
+    )
 
 
 def solution(mesh):

time: 198 us -> 162 us (0.82)
  blocking collectives: 141 us -> 45 us
  waiting for transfers between devices: 4.7 us -> 37.1 us
  starting transfers between devices: 6.26 us -> 36.1 us
  Pallas kernels: 44.9 us -> 42.9 us
    all_to_all x7 -> x2, blocking collectives: 125 us -> 28.8 us  [swap_rows(): return lax.all_to_all(x, 'rows', 0, 0, tiled=True)]
    ppermute x4 -> x29, waiting for transfers between devices: 0.01 us -> 32.4 us  [exchange(): lax.ppermute(x, axis, [(i, i ^ flip) for i in range(lax.axis_size(axis))])]
    ppermute x4 -> x29, starting transfers between devices: 1.87 us -> 31.7 us  [exchange(): lax.ppermute(x, axis, [(i, i ^ flip) for i in range(lax.axis_size(axis))])]
    pallas_call x18 -> x36, Pallas kernels: 44.9 us -> 42.9 us  [call(): pl.pallas_call(kernel, in_specs=in_specs or [vmem()] * len(args), out_spe...]
  transfers between devices with their start and end apart: 6 -> 31, of which waited for: 1 -> 18; matrix products, arithmetic and copies ran while one was open for 0% -> 0% of each run, Pallas kernels for 6% -> 15%
where the time goes in v3:
time: 162 us
  blocking collectives  45 us (28%)
  Pallas kernels  42.9 us (26%)
  waiting for transfers between devices  37.1 us (23%)
  starting transfers between devices  36.1 us (22%)
    pallas_call x36, Pallas kernels, call(): pl.pallas_call(kernel, in_specs=in_specs or [vmem()] * len(args), out_spe...  42.9 us
    ppermute x29, waiting for transfers between devices, exchange(): lax.ppermute(x, axis, [(i, i ^ flip) for i in range(lax.axis_size(axis))])  32.4 us
    ppermute x29, starting transfers between devices, exchange(): lax.ppermute(x, axis, [(i, i ^ flip) for i in range(lax.axis_size(axis))])  31.7 us
    all_to_all x2, blocking collectives, swap_rows(): return lax.all_to_all(x, 'rows', 0, 0, tiled=True)  28.8 us
    all_gather x2, blocking collectives, shards(): gathered = lax.all_gather(products, 'px')  11 us
    all_gather x1, blocking collectives, shards(): squares = lax.all_gather(squares, 'px')  5.17 us
    ppermute x2, waiting for transfers between devices, to_slices(): return lax.ppermute(x, ('rows', 'px'), pairs)  4.68 us
    ppermute x2, starting transfers between devices, to_slices(): return lax.ppermute(x, ('rows', 'px'), pairs)  4.39 us
  transfers between devices with their start and end apart: 31, of which 18 were waited for; matrix products, arithmetic and copies ran while one was open for 0% of the time, Pallas kernels for 15%

profile of v3, /device:TPU:0, one launch (start us, length us, event | category | flops | bytes accessed | tf_op | source)
XLA Modules:
  0.0 162.1 jit_solution(6453838014603718879)
XLA Ops:
  0.7 6.6 %load_project.1 = (f32[8,8,1024]{2,1,0:T(8,128)S(1)}, f32[8,8192]{1,0:T(8,128)S(1)}, bf16[8192,1024]{1,0:T(8,128)(2,1)S(1)}, f32[8,128]{1,0:T(8,128)S(1)}, f32[1,8192]{1,0:T(1,128)S(1)}) custom-call(f32[8,8192]{1,0:T(8,128)} %q_hbm.1, f32[1,8192]{1,0:T(1,128)} %bitcast.50, bf16[8192,1024]{1,0:T(8,128)(2,1)} %e_hbm.1, s32[5,8]{1,0:T(8,128)S(1)} %copy-done.2), custom_call_target="tpu_custom_call" | custom-call | flops 134217728 | bytes 16777216 | tf_op jit(solution)/shard_map/load_project/pallas_call | solution.py:42
  7.3 16.0 %all_to_all.10.parts = f32[8,8,1024]{2,1,0:T(8,128)S(1)} all-to-all(f32[8,8,1024]{2,1,0:T(8,128)S(1)} %get-tuple-element.28), channel_id=1, replica_groups=mesh['rows'=8,'px'=4] {'rows'}, dimensions={0} | all-to-all | bytes 524288 | tf_op jit(solution)/shard_map/all_to_all | solution.py:446
  23.3 2.7 %back_0_1.1 = f32[8,4096]{1,0:T(8,128)S(1)} custom-call(f32[8,8,1024]{2,1,0:T(8,128)S(1)} %all_to_all.10.parts, f32[1,1024]{1,0:T(1,128)S(1)} %bitcast.41, f32[8,128]{1,0:T(8,128)S(1)} %get-tuple-element.29.sigma.refs_6_, bf16[8192,1024]{1,0:T(8,128)(2,1)S(1)} %get-tuple-element.30.e_vmem), custom_call_target="tpu_custom_call" | custom-call | flops 67108864 | bytes 16777216 | tf_op jit(solution)/shard_map/back_0_1/pallas_call | solution.py:42
  26.1 2.7 %back_0_0.1 = f32[8,4096]{1,0:T(8,128)S(1)} custom-call(f32[8,8,1024]{2,1,0:T(8,128)S(1)} %all_to_all.10.parts, f32[1,1024]{1,0:T(1,128)S(1)} %bitcast.42, f32[8,128]{1,0:T(8,128)S(1)} %get-tuple-element.29.sigma.refs_6_, bf16[8192,1024]{1,0:T(8,128)(2,1)S(1)} %get-tuple-element.30.e_vmem), custom_call_target="tpu_custom_call" | custom-call | flops 67108864 | bytes 16777216 | tf_op jit(solution)/shard_map/back_0_0/pallas_call | solution.py:42
  30.4 4.6 %norms.1.refs_5_ = f32[1,512]{1,0:T(1,128)S(1)} custom-call(bf16[512,16384]{1,0:T(8,128)(2,1)S(1)} %bitcast.25), custom_call_target="tpu_custom_call" | custom-call | flops 16777216 | bytes 16777216 | tf_op jit(solution)/shard_map/norms/pallas_call | solution.py:42
  38.6 12.8 %all_to_all.11.parts = f32[8,8,1024]{2,1,0:T(8,128)S(1)} all-to-all(f32[8,8,1024]{2,1,0:T(8,128)S(1)} %project_rest.1), channel_id=1, replica_groups=mesh['rows'=8,'px'=4] {'rows'}, dimensions={0} | all-to-all | bytes 524288 | tf_op jit(solution)/shard_map/all_to_all | solution.py:446
  51.4 2.7 %back_1_1.1 = f32[8,4096]{1,0:T(8,128)S(1)} custom-call(f32[8,8,1024]{2,1,0:T(8,128)S(1)} %all_to_all.11.parts, f32[1,1024]{1,0:T(1,128)S(1)} %bitcast.43, f32[8,128]{1,0:T(8,128)S(1)} %get-tuple-element.29.sigma.refs_6_, bf16[8192,1024]{1,0:T(8,128)(2,1)S(1)} %get-tuple-element.30.e_vmem), custom_call_target="tpu_custom_call" | custom-call | flops 67108864 | bytes 16777216 | tf_op jit(solution)/shard_map/back_1_1/pallas_call | solution.py:42
  54.1 2.7 %back_1_0.1.mine = f32[8,4096]{1,0:T(8,128)S(1)} custom-call(f32[8,8,1024]{2,1,0:T(8,128)S(1)} %all_to_all.11.parts, f32[1,1024]{1,0:T(1,128)S(1)} %bitcast.44, f32[8,128]{1,0:T(8,128)S(1)} %get-tuple-element.29.sigma.refs_6_, bf16[8192,1024]{1,0:T(8,128)(2,1)S(1)} %get-tuple-element.30.e_vmem), custom_call_target="tpu_custom_call" | custom-call | flops 67108864 | bytes 16777216 | tf_op jit(solution)/shard_map/back_1_0/pallas_call | solution.py:42
  57.7 3.7 %collective-permute-start.5 = (f32[8,2048]{1,0:T(8,128)S(1)}, f32[8,2048]{1,0:T(8,128)S(1)}, u32[]{:S(2)}, u32[]{:S(2)}) collective-permute-start(f32[8,2048]{1,0:T(8,128)S(1)} %get-tuple-element.51), channel_id=1, source_target_pairs={{0,4},{1,12},{2,0},{3,8},{4,20},{5,28},{6,16},{7,24},{8,5},{9,13},... | collective-permute-start | bytes 196616 | tf_op jit(solution)/shard_map/ppermute | solution.py:457
  61.4 4.7 %collective-permute-done.5 = f32[8,2048]{1,0:T(8,128)S(1)} collective-permute-done((f32[8,2048]{1,0:T(8,128)S(1)}, f32[8,2048]{1,0:T(8,128)S(1)}, u32[]{:S(2)}, u32[]{:S(2)}) %collective-permute-start.5) | collective-permute-done | bytes 65568 | tf_op jit(solution)/shard_map/ppermute | solution.py:457
  66.2 5.6 %collective-permute-start.6 = (f32[8,2048]{1,0:T(8,128)S(1)}, f32[8,2048]{1,0:T(8,128)S(1)}, u32[]{:S(2)}, u32[]{:S(2)}) collective-permute-start(f32[8,2048]{1,0:T(8,128)S(1)} %add.7.refs_0_.refs_4_), channel_id=1, source_target_pairs={{0,16},{4,20},{8,24},{12,28},{16,0},{20,4},{24,8},{28,12},{1,17},{... | collective-permute-start | bytes 196616 | tf_op jit(solution)/shard_map/ppermute | solution.py:442
  72.7 2.8 %collective-permute-done.6.refs_0_ = f32[8,2048]{1,0:T(8,128)S(1)} collective-permute-done((f32[8,2048]{1,0:T(8,128)S(1)}, f32[8,2048]{1,0:T(8,128)S(1)}, u32[]{:S(2)}, u32[]{:S(2)}) %collective-permute-start.6) | collective-permute-done | bytes 65568 | tf_op jit(solution)/shard_map/ppermute | solution.py:442
  75.5 2.4 %collective-permute-done.7.refs_1_ = f32[8,2048]{1,0:T(8,128)S(1)} collective-permute-done((f32[8,2048]{1,0:T(8,128)S(1)}, f32[8,2048]{1,0:T(8,128)S(1)}, u32[]{:S(2)}, u32[]{:S(2)}) %collective-permute-start.7) | collective-permute-done | bytes 65568 | tf_op jit(solution)/shard_map/ppermute | solution.py:442
  84.2 5.6 %all-gather = f32[64,512]{1,0:T(8,128)S(1)} all-gather(f32[16,512]{1,0:T(8,128)S(1)} %pad_maximum_fusion.6), channel_id=2, replica_groups=mesh['rows'=8,'px'=4] {'px'}, dimensions={0}, use_global_device_ids=true | all-gather | bytes 163840 | tf_op jit(solution)/shard_map/all_gather | solution.py:523
  94.6 2.5 %collective-permute-done.13.theirs = f32[2,8,2176]{2,1,0:T(8,128)S(1)} collective-permute-done((f32[2,8,2176]{2,1,0:T(8,128)S(1)}, f32[2,8,2176]{2,1,0:T(8,128)S(1)}, u32[]{:S(2)}, u32[]{:S(2)}) %collective-permute-start.13) | collective-permute-done | bytes 139296 | tf_op jit(solution)/shard_map/ppermute | solution.py:442
  97.7 1.6 collective-permute-start.15
  100.9 3.4 %collective-permute-done.14.refs_2_ = f32[8,2176]{1,0:T(8,128)S(1)} collective-permute-done((f32[8,2176]{1,0:T(8,128)S(1)}, f32[8,2176]{1,0:T(8,128)S(1)}, u32[]{:S(2)}, u32[]{:S(2)}) %collective-permute-start.14) | collective-permute-done | bytes 69664 | tf_op jit(solution)/shard_map/ppermute | solution.py:442
  107.4 2.3 %collective-permute-start.17 = (f32[8,2176]{1,0:T(8,128)S(1)}, f32[8,2176]{1,0:T(8,128)S(1)}, u32[]{:S(2)}, u32[]{:S(2)}) collective-permute-start(f32[8,2176]{1,0:T(8,128)S(1)} %combine_0.1.refs_0_.refs_4_), channel_id=1, source_target_pairs={{0,24},{4,28},{8,16},{12,20},{16,8},{20,12},{24,0},{28,4},{1,25},{... | collective-permute-start | bytes 208904 | tf_op jit(solution)/shard_map/ppermute | solution.py:442
  119.9 5.4 %all-gather.1 = f32[64,512]{1,0:T(8,128)S(1)} all-gather(f32[16,512]{1,0:T(8,128)S(1)} %dots_1_3.1), channel_id=3, replica_groups=mesh['rows'=8,'px'=4] {'px'}, dimensions={0}, use_global_device_ids=true | all-gather | bytes 163840 | tf_op jit(solution)/shard_map/all_gather | solution.py:523
  130.2 2.5 %collective-permute-done.23.theirs = f32[2,8,2176]{2,1,0:T(8,128)S(1)} collective-permute-done((f32[2,8,2176]{2,1,0:T(8,128)S(1)}, f32[2,8,2176]{2,1,0:T(8,128)S(1)}, u32[]{:S(2)}, u32[]{:S(2)}) %collective-permute-start.23) | collective-permute-done | bytes 139296 | tf_op jit(solution)/shard_map/ppermute | solution.py:442
  136.5 4.1 %collective-permute-done.24.refs_2_ = f32[8,2176]{1,0:T(8,128)S(1)} collective-permute-done((f32[8,2176]{1,0:T(8,128)S(1)}, f32[8,2176]{1,0:T(8,128)S(1)}, u32[]{:S(2)}, u32[]{:S(2)}) %collective-permute-start.24) | collective-permute-done | bytes 69664 | tf_op jit(solution)/shard_map/ppermute | solution.py:442
  145.0 3.2 %collective-permute-done.27.refs_2_ = f32[8,2176]{1,0:T(8,128)S(1)} collective-permute-done((f32[8,2176]{1,0:T(8,128)S(1)}, f32[8,2176]{1,0:T(8,128)S(1)}, u32[]{:S(2)}, u32[]{:S(2)}) %collective-permute-start.27) | collective-permute-done | bytes 69664 | tf_op jit(solution)/shard_map/ppermute | solution.py:442
  151.4 3.2 %collective-permute-done.30.refs_5_ = f32[2,8,2176]{2,1,0:T(8,128)S(1)} collective-permute-done((f32[2,8,2176]{2,1,0:T(8,128)S(1)}, f32[2,8,2176]{2,1,0:T(8,128)S(1)}, u32[]{:S(2)}, u32[]{:S(2)}) %collective-permute-start.30) | collective-permute-done | bytes 139296 | tf_op jit(solution)/shard_map/ppermute | solution.py:442
  156.0 5.2 %all-gather.2 = f32[32,128]{1,0:T(8,128)S(1)} all-gather(f32[8,128]{1,0:T(8,128)S(1)} %squares.1), channel_id=4, replica_groups=mesh['rows'=8,'px'=4] {'px'}, dimensions={0}, use_global_device_ids=true | all-gather | bytes 20480 | tf_op jit(solution)/shard_map/all_gather | solution.py:539
  (108 shorter events, 52.9 us)
Async XLA Ops:
  28.8 6.2 %collective-permute-start.1 = (f32[8,4096]{1,0:T(8,128)S(1)}, f32[8,4096]{1,0:T(8,128)S(1)}, u32[]{:S(2)}, u32[]{:S(2)}) collective-permute-start(f32[8,4096]{1,0:T(8,128)S(1)} %add.6.mine), channel_id=1, source_target_pairs={{0,2},{1,3},{2,0},{3,1},{4,6},{5,7},{6,4},{7,5},{8,10},{9,11},{10,... | collective-permute-start | bytes 393224 | tf_op jit(solution)/shard_map/ppermute | solution.py:442
  57.7 8.4 %collective-permute-start.5 = (f32[8,2048]{1,0:T(8,128)S(1)}, f32[8,2048]{1,0:T(8,128)S(1)}, u32[]{:S(2)}, u32[]{:S(2)}) collective-permute-start(f32[8,2048]{1,0:T(8,128)S(1)} %get-tuple-element.51), channel_id=1, source_target_pairs={{0,4},{1,12},{2,0},{3,8},{4,20},{5,28},{6,16},{7,24},{8,5},{9,13},... | collective-permute-start | bytes 196616 | tf_op jit(solution)/shard_map/ppermute | solution.py:457
  66.1 5.7 %collective-permute-start.9 = (f32[8,2048]{1,0:T(8,128)S(1)}, f32[8,2048]{1,0:T(8,128)S(1)}, u32[]{:S(2)}, u32[]{:S(2)}) collective-permute-start(f32[8,2048]{1,0:T(8,128)S(1)} %add.7.refs_0_.refs_4_), channel_id=1, source_target_pairs={{0,8},{4,12},{8,0},{12,4},{16,24},{20,28},{24,16},{28,20},{1,9},{5... | collective-permute-start | bytes 196616 | tf_op jit(solution)/shard_map/ppermute | solution.py:442
  66.2 9.3 %collective-permute-start.6 = (f32[8,2048]{1,0:T(8,128)S(1)}, f32[8,2048]{1,0:T(8,128)S(1)}, u32[]{:S(2)}, u32[]{:S(2)}) collective-permute-start(f32[8,2048]{1,0:T(8,128)S(1)} %add.7.refs_0_.refs_4_), channel_id=1, source_target_pairs={{0,16},{4,20},{8,24},{12,28},{16,0},{20,4},{24,8},{28,12},{1,17},{... | collective-permute-start | bytes 196616 | tf_op jit(solution)/shard_map/ppermute | solution.py:442
  71.8 6.1 %collective-permute-start.7 = (f32[8,2048]{1,0:T(8,128)S(1)}, f32[8,2048]{1,0:T(8,128)S(1)}, u32[]{:S(2)}, u32[]{:S(2)}) collective-permute-start(f32[8,2048]{1,0:T(8,128)S(1)} %add.7.refs_0_.refs_4_), channel_id=1, source_target_pairs={{0,24},{4,28},{8,16},{12,20},{16,8},{20,12},{24,0},{28,4},{1,25},{... | collective-permute-start | bytes 196616 | tf_op jit(solution)/shard_map/ppermute | solution.py:442
  71.9 8.7 %collective-permute-start.10 = (f32[2,8,2048]{2,1,0:T(8,128)S(1)}, f32[2,8,2048]{2,1,0:T(8,128)S(1)}, u32[]{:S(2)}, u32[]{:S(2)}) collective-permute-start(f32[2,8,2048]{2,1,0:T(8,128)S(1)} %pad_maximum_fusion.5), channel_id=1, source_target_pairs={{0,4},{4,0},{8,12},{12,8},{16,20},{20,16},{24,28},{28,24},{1,5},{5... | collective-permute-start | bytes 393224 | tf_op jit(solution)/shard_map/ppermute | solution.py:442
  90.6 6.5 %collective-permute-start.13 = (f32[2,8,2176]{2,1,0:T(8,128)S(1)}, f32[2,8,2176]{2,1,0:T(8,128)S(1)}, u32[]{:S(2)}, u32[]{:S(2)}) collective-permute-start(f32[2,8,2176]{2,1,0:T(8,128)S(1)} %get-tuple-element.39), channel_id=1, source_target_pairs={{0,4},{4,0},{8,12},{12,8},{16,20},{20,16},{24,28},{28,24},{1,5},{5... | collective-permute-start | bytes 417800 | tf_op jit(solution)/shard_map/ppermute | solution.py:442
  92.1 7.4 %collective-permute-start.11 = (f32[2,8,2176]{2,1,0:T(8,128)S(1)}, f32[2,8,2176]{2,1,0:T(8,128)S(1)}, u32[]{:S(2)}, u32[]{:S(2)}) collective-permute-start(f32[2,8,2176]{2,1,0:T(8,128)S(1)} %near_across_0.1), channel_id=1, source_target_pairs={{0,4},{4,0},{8,12},{12,8},{16,20},{20,16},{24,28},{28,24},{1,5},{5... | collective-permute-start | bytes 417800 | tf_op jit(solution)/shard_map/ppermute | solution.py:442
  97.2 7.1 %collective-permute-start.14 = (f32[8,2176]{1,0:T(8,128)S(1)}, f32[8,2176]{1,0:T(8,128)S(1)}, u32[]{:S(2)}, u32[]{:S(2)}) collective-permute-start(f32[8,2176]{1,0:T(8,128)S(1)} %get-tuple-element.40), channel_id=1, source_target_pairs={{0,16},{4,20},{8,24},{12,28},{16,0},{20,4},{24,8},{28,12},{1,17},{... | collective-permute-start | bytes 208904 | tf_op jit(solution)/shard_map/ppermute | solution.py:442
  97.7 6.6 %collective-permute-start.15 = (f32[8,2176]{1,0:T(8,128)S(1)}, f32[8,2176]{1,0:T(8,128)S(1)}, u32[]{:S(2)}, u32[]{:S(2)}) collective-permute-start(f32[8,2176]{1,0:T(8,128)S(1)} %get-tuple-element.41), channel_id=1, source_target_pairs={{0,24},{4,28},{8,16},{12,20},{16,8},{20,12},{24,0},{28,4},{1,25},{... | collective-permute-start | bytes 208904 | tf_op jit(solution)/shard_map/ppermute | solution.py:442
  99.6 5.4 %collective-permute-start.12 = (f32[8,2176]{1,0:T(8,128)S(1)}, f32[8,2176]{1,0:T(8,128)S(1)}, u32[]{:S(2)}, u32[]{:S(2)}) collective-permute-start(f32[8,2176]{1,0:T(8,128)S(1)} %get-tuple-element.38), channel_id=1, source_target_pairs={{0,8},{4,12},{8,0},{12,4},{16,24},{20,28},{24,16},{28,20},{1,9},{5... | collective-permute-start | bytes 208904 | tf_op jit(solution)/shard_map/ppermute | solution.py:442
  105.8 6.4 %collective-permute-start.16 = (f32[8,2176]{1,0:T(8,128)S(1)}, f32[8,2176]{1,0:T(8,128)S(1)}, u32[]{:S(2)}, u32[]{:S(2)}) collective-permute-start(f32[8,2176]{1,0:T(8,128)S(1)} %combine_0.1.refs_0_.refs_4_), channel_id=1, source_target_pairs={{0,16},{4,20},{8,24},{12,28},{16,0},{20,4},{24,8},{28,12},{1,17},{... | collective-permute-start | bytes 208904 | tf_op jit(solution)/shard_map/ppermute | solution.py:442
  107.4 6.2 %collective-permute-start.17 = (f32[8,2176]{1,0:T(8,128)S(1)}, f32[8,2176]{1,0:T(8,128)S(1)}, u32[]{:S(2)}, u32[]{:S(2)}) collective-permute-start(f32[8,2176]{1,0:T(8,128)S(1)} %combine_0.1.refs_0_.refs_4_), channel_id=1, source_target_pairs={{0,24},{4,28},{8,16},{12,20},{16,8},{20,12},{24,0},{28,4},{1,25},{... | collective-permute-start | bytes 208904 | tf_op jit(solution)/shard_map/ppermute | solution.py:442
  109.7 7.6 %collective-permute-start.20 = (f32[2,8,2176]{2,1,0:T(8,128)S(1)}, f32[2,8,2176]{2,1,0:T(8,128)S(1)}, u32[]{:S(2)}, u32[]{:S(2)}) collective-permute-start(f32[2,8,2176]{2,1,0:T(8,128)S(1)} %pad_maximum_fusion.1), channel_id=1, source_target_pairs={{0,4},{4,0},{8,12},{12,8},{16,20},{20,16},{24,28},{28,24},{1,5},{5... | collective-permute-start | bytes 417800 | tf_op jit(solution)/shard_map/ppermute | solution.py:442
  126.2 6.5 %collective-permute-start.23 = (f32[2,8,2176]{2,1,0:T(8,128)S(1)}, f32[2,8,2176]{2,1,0:T(8,128)S(1)}, u32[]{:S(2)}, u32[]{:S(2)}) collective-permute-start(f32[2,8,2176]{2,1,0:T(8,128)S(1)} %get-tuple-element.47), channel_id=1, source_target_pairs={{0,4},{4,0},{8,12},{12,8},{16,20},{20,16},{24,28},{28,24},{1,5},{5... | collective-permute-start | bytes 417800 | tf_op jit(solution)/shard_map/ppermute | solution.py:442
  127.9 7.9 %collective-permute-start.21 = (f32[2,8,2176]{2,1,0:T(8,128)S(1)}, f32[2,8,2176]{2,1,0:T(8,128)S(1)}, u32[]{:S(2)}, u32[]{:S(2)}) collective-permute-start(f32[2,8,2176]{2,1,0:T(8,128)S(1)} %near_across_1.1), channel_id=1, source_target_pairs={{0,4},{4,0},{8,12},{12,8},{16,20},{20,16},{24,28},{28,24},{1,5},{5... | collective-permute-start | bytes 417800 | tf_op jit(solution)/shard_map/ppermute | solution.py:442
  132.8 7.8 %collective-permute-start.24 = (f32[8,2176]{1,0:T(8,128)S(1)}, f32[8,2176]{1,0:T(8,128)S(1)}, u32[]{:S(2)}, u32[]{:S(2)}) collective-permute-start(f32[8,2176]{1,0:T(8,128)S(1)} %get-tuple-element.48), channel_id=1, source_target_pairs={{0,16},{4,20},{8,24},{12,28},{16,0},{20,4},{24,8},{28,12},{1,17},{... | collective-permute-start | bytes 208904 | tf_op jit(solution)/shard_map/ppermute | solution.py:442
  134.2 6.3 %collective-permute-start.25 = (f32[8,2176]{1,0:T(8,128)S(1)}, f32[8,2176]{1,0:T(8,128)S(1)}, u32[]{:S(2)}, u32[]{:S(2)}) collective-permute-start(f32[8,2176]{1,0:T(8,128)S(1)} %get-tuple-element.49), channel_id=1, source_target_pairs={{0,24},{4,28},{8,16},{12,20},{16,8},{20,12},{24,0},{28,4},{1,25},{... | collective-permute-start | bytes 208904 | tf_op jit(solution)/shard_map/ppermute | solution.py:442
  136.0 5.3 %collective-permute-start.22 = (f32[8,2176]{1,0:T(8,128)S(1)}, f32[8,2176]{1,0:T(8,128)S(1)}, u32[]{:S(2)}, u32[]{:S(2)}) collective-permute-start(f32[8,2176]{1,0:T(8,128)S(1)} %get-tuple-element.46), channel_id=1, source_target_pairs={{0,8},{4,12},{8,0},{12,4},{16,24},{20,28},{24,16},{28,20},{1,9},{5... | collective-permute-start | bytes 208904 | tf_op jit(solution)/shard_map/ppermute | solution.py:442
  141.5 6.7 %collective-permute-start.27 = (f32[8,2176]{1,0:T(8,128)S(1)}, f32[8,2176]{1,0:T(8,128)S(1)}, u32[]{:S(2)}, u32[]{:S(2)}) collective-permute-start(f32[8,2176]{1,0:T(8,128)S(1)} %combine_1.1.refs_0_), channel_id=1, source_target_pairs={{0,16},{4,20},{8,24},{12,28},{16,0},{20,4},{24,8},{28,12},{1,17},{... | collective-permute-start | bytes 208904 | tf_op jit(solution)/shard_map/ppermute | solution.py:442
  142.9 6.3 %collective-permute-start.28 = (f32[8,2176]{1,0:T(8,128)S(1)}, f32[8,2176]{1,0:T(8,128)S(1)}, u32[]{:S(2)}, u32[]{:S(2)}) collective-permute-start(f32[8,2176]{1,0:T(8,128)S(1)} %combine_1.1.refs_0_), channel_id=1, source_target_pairs={{0,24},{4,28},{8,16},{12,20},{16,8},{20,12},{24,0},{28,4},{1,25},{... | collective-permute-start | bytes 208904 | tf_op jit(solution)/shard_map/ppermute | solution.py:442
  144.4 5.8 %collective-permute-start.26 = (f32[8,2176]{1,0:T(8,128)S(1)}, f32[8,2176]{1,0:T(8,128)S(1)}, u32[]{:S(2)}, u32[]{:S(2)}) collective-permute-start(f32[8,2176]{1,0:T(8,128)S(1)} %combine_1.1.refs_0_), channel_id=1, source_target_pairs={{0,8},{4,12},{8,0},{12,4},{16,24},{20,28},{24,16},{28,20},{1,9},{5... | collective-permute-start | bytes 208904 | tf_op jit(solution)/shard_map/ppermute | solution.py:442
  149.2 5.3 %collective-permute-start.30 = (f32[2,8,2176]{2,1,0:T(8,128)S(1)}, f32[2,8,2176]{2,1,0:T(8,128)S(1)}, u32[]{:S(2)}, u32[]{:S(2)}) collective-permute-start(f32[2,8,2176]{2,1,0:T(8,128)S(1)} %pad_maximum_fusion.3), channel_id=1, source_target_pairs={{0,4},{4,0},{8,12},{12,8},{16,20},{20,16},{24,28},{28,24},{1,5},{5... | collective-permute-start | bytes 417800 | tf_op jit(solution)/shard_map/ppermute | solution.py:442
  150.2 5.8 %collective-permute-start.29 = (f32[2,8,2176]{2,1,0:T(8,128)S(1)}, f32[2,8,2176]{2,1,0:T(8,128)S(1)}, u32[]{:S(2)}, u32[]{:S(2)}) collective-permute-start(f32[2,8,2176]{2,1,0:T(8,128)S(1)} %pad_maximum_fusion.2), channel_id=1, source_target_pairs={{0,4},{4,0},{8,12},{12,8},{16,20},{20,16},{24,28},{28,24},{1,5},{5... | collective-permute-start | bytes 417800 | tf_op jit(solution)/shard_map/ppermute | solution.py:442
  (15 other events, 91.5 us)

commit v4 on v3

--- a/solution.py
+++ b/solution.py
@@ -14,7 +14,7 @@
 RMS_EPSILON = 1e-06
 MIB = 1024 * 1024
 NT = (((1,), (1,)), ((), ()))
-CHUNKS = 8
+CHUNKS = 16
 PAD = 128
 
 f32 = jnp.float32
@@ -65,7 +65,7 @@
 
 
 def load_project_kernel(
-    q_hbm, mean_hbm, e_hbm, levels, copies, offset, e_vmem, sigma, mean, q, sems
+    q_hbm, mean_hbm, e_hbm, levels_hbm, copies, offset, e_vmem, sigma, mean, q, levels, sems
 ):
     pixels = e_hbm.shape[0]
     chunk = pixels // CHUNKS
@@ -78,11 +78,15 @@
             pltpu.make_async_copy(e_hbm.at[at], e_vmem.at[at], sems.at[c, 2]),
         )
 
+    tables = pltpu.make_async_copy(levels_hbm, levels, sems.at[CHUNKS, 0])
+    tables.start()
+
     @pl.loop(0, CHUNKS)
     def _(c):
         for move in moves(c):
             move.start()
 
+    tables.wait()
     lane = lax.broadcasted_iota(jnp.int32, sigma.shape, 1)
     table = jnp.zeros(sigma.shape, f32)
     for t in range(levels.shape[0]):
@@ -105,8 +109,8 @@
 
 def load_project(queries, mean, basis, levels, row_count):
     pixels, comps = basis.shape
-    queries, mean, basis = [
-        pltpu.with_memory_space_constraint(x, pltpu.HBM) for x in (queries, mean, basis)
+    queries, mean, basis, levels = [
+        pltpu.with_memory_space_constraint(x, pltpu.HBM) for x in (queries, mean, basis, levels)
     ]
     return call(
         load_project_kernel,
@@ -118,42 +122,50 @@
             shape((1, pixels)),
         ],
         (queries, mean, basis, levels),
-        in_specs=[anywhere()] * 3 + [vmem()],
+        in_specs=[anywhere()] * 4,
         scratch=[
             pltpu.VMEM((8, pixels), f32),
-            pltpu.SemaphoreType.DMA((CHUNKS, 3)),
+            pltpu.VMEM(levels.shape, jnp.int32),
+            pltpu.SemaphoreType.DMA((CHUNKS + 1, 3)),
         ],
         flops=16 * pixels * comps,
         name="load_project",
     )
 
 
-def back_kernel(step, flip, parts, eigenvalues, sigma, e_vmem, image):
-    half = image.shape[1]
-    core = lax.rem(lax.axis_index("px"), 2)
-    which = 1 - core if flip else core
+def back_kernel(step, part, parts, eigenvalues, sigma, e_vmem, image):
+    span = image.shape[1]
+    place = lax.axis_index("px")
+    core, upper = lax.rem(place, 2), lax.div(place, 2)
+    if part == "mine":
+        start = core * span
+    elif part == "theirs":
+        start = (1 - core) * span
+    else:
+        start = (2 * core + (upper if part == "keep" else 1 - upper)) * span
     now = sigma[:, step : step + 1]
     coeff = jnp.sum(parts[...], axis=0)
     ev = eigenvalues[...]
     shrunk = (coeff * (ev / (ev + now * now))).astype(bf16)
-    tile = min(1024, half)
-
-    @pl.loop(0, half // tile)
+    tile = min(4096, span)
+
+    @pl.loop(0, span // tile)
     def _(i):
-        at = rows_at(which * half + i * tile, tile, tile)
+        at = rows_at(start + i * tile, tile, tile)
         image[:, rows_at(i * tile, tile, tile)] = lax.dot_general(
             shrunk, e_vmem[at, :], NT, preferred_element_type=f32
         )
 
 
-def back(step, flip, parts, eigenvalues, sigma, e_vmem):
+def back(step, part, parts, eigenvalues, sigma, e_vmem):
     pixels, comps = e_vmem.shape
+    span = pixels // (2 if part in ("mine", "theirs") else 4)
     return call(
-        functools.partial(back_kernel, step, flip),
-        shape((8, pixels // 2)),
+        functools.partial(back_kernel, step, part),
+        shape((8, span)),
         (parts, eigenvalues, sigma, in_vmem(e_vmem)),
-        flops=8 * pixels * comps,
-        name=f"back_{step}_{int(flip)}",
+        flops=16 * span * comps,
+        name=f"back_{step}_{part}",
     )
 
 
@@ -161,7 +173,7 @@
     half = off.shape[1]
     core = lax.rem(lax.axis_index("px"), 2)
     which = 1 - core if flip else core
-    tile = min(1024, half)
+    tile = min(4096, half)
 
     def step(i, total):
         at = rows_at(which * half + i * tile, tile, tile)
@@ -174,7 +186,7 @@
 def project_rest_kernel(off, own, e_vmem, copies):
     half = off.shape[1]
     which = 1 - lax.rem(lax.axis_index("px"), 2)
-    tile = min(1024, half)
+    tile = min(4096, half)
 
     def step(i, total):
         at = rows_at(which * half + i * tile, tile, tile)
@@ -194,19 +206,21 @@
     out[...] = image + ratio * (offset[:, rows_at(core * half, half, half)] - image)
 
 
-def second_update_kernel(mine, theirs, offset, mean, sigma, out):
-    half = mine.shape[1]
-    span = half // 2
+def give_kernel(image, other, out):
+    span = image.shape[1]
+    upper = lax.div(lax.axis_index("px"), 2)
+    out[...] = image[...] + other[:, rows_at((1 - upper) * span, span, span)]
+
+
+def second_update_kernel(image, other, given, offset, mean, sigma, out):
+    span = image.shape[1]
     place = lax.axis_index("px")
-    core = lax.rem(place, 2)
-    x = lax.div(place, 2)
+    core, upper = lax.rem(place, 2), lax.div(place, 2)
     ratio = sigma[:, 2:3] / sigma[:, 1:2]
-    image = mine[...] + theirs[...]
-    first = jnp.where(x == 0, 1.0, 0.0).astype(f32)
-    mean_half = mean[:, rows_at(core * half, half, half)]
-    sent = (1.0 - ratio) * image + first * (ratio * offset[...] + mean_half)
-    for k in range(2):
-        out[lax.rem(k + x, 2)] = sent[:, k * span : (k + 1) * span]
+    at = rows_at(upper * span, span, span)
+    total = image[...] + other[:, at] + given[...]
+    average = mean[:, rows_at((2 * core + upper) * span, span, span)]
+    out[...] = average + total + ratio * (offset[:, at] - total)
 
 
 def norms_kernel(slab, out, folded):
@@ -230,15 +244,17 @@
 
 
 def block_at(k, span):
-    block = lax.bitwise_xor(lax.axis_index("rows"), k)
-    return rows_at(block * span, span, span)
-
-
-def dots_kernel(offsets, *refs):
+    px = lax.axis_size("px")
+    per = lax.axis_size("rows") // px
+    other = lax.bitwise_xor(lax.axis_index("rows"), k)
+    return rows_at((lax.rem(other, per) * px + lax.div(other, per)) * span, span, span)
+
+
+def dots_kernel(offsets, fresh, *refs):
     *inputs, slab, out = refs
     pieces, before = inputs[: len(offsets)], inputs[len(offsets) :]
     span = slab.shape[1] // lax.axis_size("rows")
-    total = before[0][:8] if before else jnp.zeros((8, slab.shape[0]), f32)
+    total = before[0][:8] if before and not fresh else jnp.zeros((8, slab.shape[0]), f32)
     rest = before[0][8:] if before else jnp.zeros((8, slab.shape[0]), f32)
     for piece, ks in zip(pieces, offsets):
         for i, k in enumerate(ks):
@@ -256,16 +272,32 @@
     out[8:] = rest
 
 
-def dots(pieces, offsets, before, slab, name):
+def dots(pieces, offsets, before, slab, name, fresh=False):
     rows = lax.axis_size("rows")
     count = sum(len(ks) for ks in offsets)
     return call(
-        functools.partial(dots_kernel, offsets),
+        functools.partial(dots_kernel, offsets, fresh),
         shape((16, slab.shape[0])),
         (*pieces, *before, in_vmem(slab)),
         flops=16 * count * slab.shape[0] * (slab.shape[1] // rows),
         name=name,
     )
+
+
+def read_slices(piece, norms, slab):
+    rows, px = lax.axis_size("rows"), lax.axis_size("px")
+    per = rows // px
+    got = [to_readers(piece, turn) for turn in range(px)]
+    halves = [range(px // 2), range(px // 2, px)]
+    packs = [jnp.stack([got[t] for t in half]) for half in halves]
+    groups = [([got[t] for t in half], [(t * per,) for t in half]) for half in halves]
+    for k in range(1, per):
+        for pack, half in zip(packs, halves):
+            groups.append(([exchange("rows", pack, k)], [tuple(t * per ^ k for t in half)]))
+    total = (jnp.broadcast_to(norms, (16, slab.shape[0])),)
+    for i, (pieces, offsets) in enumerate(groups):
+        total = (dots(pieces, offsets, total, slab, f"dots_0_{i}", i == 0),)
+    return got[0], total[0]
 
 
 def put_chunks(weights, tail, ks, slab, out):
@@ -446,14 +478,15 @@
     return lax.all_to_all(x, "rows", 0, 0, tiled=True)
 
 
-def to_slices(x, turn):
+def to_readers(x, turn):
     rows, px = lax.axis_size("rows"), lax.axis_size("px")
+    per = rows // px
     pairs = []
     for r in range(rows):
         for p in range(px):
             upper, core = divmod(p, 2)
-            piece = r * px + 2 * core + (upper + turn) % 2
-            pairs.append((r * px + p, (piece % rows) * px + piece // rows))
+            place = (2 * core + upper) ^ turn
+            pairs.append((r * px + p, (place * per + r % per) * px + r // per))
     return lax.ppermute(x, ("rows", "px"), pairs)
 
 
@@ -473,8 +506,8 @@
         queries, pixel_mean[None, :], eigenbasis, level_ids, rows
     )
     parts = swap_rows(copies)
-    sent = exchange("px", back(0, True, parts, values, sigma, basis), 1)
-    image = back(0, False, parts, values, sigma, basis) + sent
+    sent = exchange("px", back(0, "theirs", parts, values, sigma, basis), 1)
+    image = back(0, "mine", parts, values, sigma, basis) + sent
     across = exchange("px", image, 2)
     norms = call(
         norms_kernel,
@@ -507,17 +540,21 @@
         name="project_rest",
     )
     parts = swap_rows(copies)
-    sent = exchange("px", back(1, True, parts, values, sigma, basis), 1)
-    mine = back(1, False, parts, values, sigma, basis)
-    outgoing = call(
+    sent = exchange("px", back(1, "theirs", parts, values, sigma, basis), 1)
+    given = call(
+        give_kernel,
+        shape((8, pixels // 4)),
+        (back(1, "give", parts, values, sigma, basis), sent),
+        name="give",
+    )
+    given = exchange("px", given, 2)
+    piece = call(
         second_update_kernel,
-        shape((2, 8, span)),
-        (mine, sent, offset, mean, sigma),
+        shape((8, pixels // 4)),
+        (back(1, "keep", parts, values, sigma, basis), sent, given, offset, mean, sigma),
         name="second_update",
     )
-    state = to_slices(outgoing[0], 0) + to_slices(outgoing[1], 1)
-    products = gather_dots(state, slab, "dots_0")
-    products = jnp.concatenate([products[:8], jnp.broadcast_to(norms, (8, slab_rows))])
+    state, products = read_slices(piece, norms, slab)
     scale = norms
     for step in range(2):
         gathered = lax.all_gather(products, "px")

time: 162 us -> 156 us (0.963)
  waiting for transfers between devices: 37.1 us -> 30.6 us
  Pallas kernels: 42.9 us -> 40.5 us
  starting transfers between devices: 36.1 us -> 38.3 us
    ppermute x2 -> x4, starting transfers between devices: 4.39 us -> 8.93 us  [to_readers(): return lax.ppermute(x, ('rows', 'px'), pairs)]
    ppermute x29 -> x27, waiting for transfers between devices: 32.4 us -> 29 us  [exchange(): lax.ppermute(x, axis, [(i, i ^ flip) for i in range(lax.axis_size(axis))])]
    ppermute x2 -> x4, waiting for transfers between devices: 4.68 us -> 1.6 us  [to_readers(): return lax.ppermute(x, ('rows', 'px'), pairs)]
    pallas_call x36 -> x37, Pallas kernels: 42.9 us -> 40.5 us  [call(): pl.pallas_call(kernel, in_specs=in_specs or [vmem()] * len(args), out_spe...]
    ppermute x29 -> x27, starting transfers between devices: 31.7 us -> 29.4 us  [exchange(): lax.ppermute(x, axis, [(i, i ^ flip) for i in range(lax.axis_size(axis))])]
  transfers between devices with their start and end apart: 31 -> 31, of which waited for: 18 -> 17; matrix products, arithmetic and copies ran while one was open for 0% -> 0% of each run, Pallas kernels for 15% -> 14%
where the time goes in v4:
time: 156 us; the launch traced here: 155 us
  blocking collectives  45.7 us (29%)
  Pallas kernels  40.5 us (26%)
  starting transfers between devices  38.3 us (25%)
  waiting for transfers between devices  30.6 us (20%)
    pallas_call x37, Pallas kernels, call(): pl.pallas_call(kernel, in_specs=in_specs or [vmem()] * len(args), out_spe...  40.5 us
    ppermute x27, starting transfers between devices, exchange(): lax.ppermute(x, axis, [(i, i ^ flip) for i in range(lax.axis_size(axis))])  29.4 us
    ppermute x27, waiting for transfers between devices, exchange(): lax.ppermute(x, axis, [(i, i ^ flip) for i in range(lax.axis_size(axis))])  29 us
    all_to_all x2, blocking collectives, swap_rows(): return lax.all_to_all(x, 'rows', 0, 0, tiled=True)  28.8 us
    all_gather x2, blocking collectives, shards(): gathered = lax.all_gather(products, 'px')  11.8 us
    ppermute x4, starting transfers between devices, to_readers(): return lax.ppermute(x, ('rows', 'px'), pairs)  8.93 us
    all_gather x1, blocking collectives, shards(): squares = lax.all_gather(squares, 'px')  5.17 us
  transfers between devices with their start and end apart: 31, of which 17 were waited for; matrix products, arithmetic and copies ran while one was open for 0% of the time, Pallas kernels for 14%

profile of v4, /device:TPU:0, one launch (start us, length us, event | category | flops | bytes accessed | tf_op | source)
XLA Modules:
  0.0 155.4 jit_solution(9967991877570302430)
XLA Ops:
  0.0 6.7 %load_project.1 = (f32[8,8,1024]{2,1,0:T(8,128)S(1)}, f32[8,8192]{1,0:T(8,128)S(1)}, bf16[8192,1024]{1,0:T(8,128)(2,1)S(1)}, f32[8,128]{1,0:T(8,128)S(1)}, f32[1,8192]{1,0:T(1,128)S(1)}) custom-call(f32[8,8192]{1,0:T(8,128)} %q_hbm.1, f32[1,8192]{1,0:T(1,128)} %bitcast.47, bf16[8192,1024]{1,0:T(8,128)(2,1)} %e_hbm.1, s32[5,8]{1,0:T(8,128)} %levels_hbm.1), custom_call_target="tpu_custom_call" | custom-call | flops 134217728 | bytes 16777216 | tf_op jit(solution)/shard_map/load_project/pallas_call | solution.py:42
  6.7 16.0 %all_to_all.10.parts = f32[8,8,1024]{2,1,0:T(8,128)S(1)} all-to-all(f32[8,8,1024]{2,1,0:T(8,128)S(1)} %get-tuple-element.28), channel_id=1, replica_groups=mesh['rows'=8,'px'=4] {'rows'}, dimensions={0} | all-to-all | bytes 524288 | tf_op jit(solution)/shard_map/all_to_all | solution.py:478
  22.7 2.3 %back_0_theirs.1 = f32[8,4096]{1,0:T(8,128)S(1)} custom-call(f32[8,8,1024]{2,1,0:T(8,128)S(1)} %all_to_all.10.parts, f32[1,1024]{1,0:T(1,128)S(1)} %bitcast.36, f32[8,128]{1,0:T(8,128)S(1)} %get-tuple-element.29.sigma.refs_6_, bf16[8192,1024]{1,0:T(8,128)(2,1)S(1)} %get-tuple-element.30.e_vmem), custom_call_target="tpu_custom_call" | custom-call | flops 67108864 | bytes 16777216 | tf_op jit(solution)/shard_map/back_0_theirs/pallas_call | solution.py:42
  25.1 2.3 %back_0_mine.1 = f32[8,4096]{1,0:T(8,128)S(1)} custom-call(f32[8,8,1024]{2,1,0:T(8,128)S(1)} %all_to_all.10.parts, f32[1,1024]{1,0:T(1,128)S(1)} %bitcast.37, f32[8,128]{1,0:T(8,128)S(1)} %get-tuple-element.29.sigma.refs_6_, bf16[8192,1024]{1,0:T(8,128)(2,1)S(1)} %get-tuple-element.30.e_vmem), custom_call_target="tpu_custom_call" | custom-call | flops 67108864 | bytes 16777216 | tf_op jit(solution)/shard_map/back_0_mine/pallas_call | solution.py:42
  29.0 4.6 %norms.1.refs_5_ = f32[1,512]{1,0:T(1,128)S(1)} custom-call(bf16[512,16384]{1,0:T(8,128)(2,1)S(1)} %bitcast.21), custom_call_target="tpu_custom_call" | custom-call | flops 16777216 | bytes 16777216 | tf_op jit(solution)/shard_map/norms/pallas_call | solution.py:42
  36.5 12.8 %all_to_all.11.parts = f32[8,8,1024]{2,1,0:T(8,128)S(1)} all-to-all(f32[8,8,1024]{2,1,0:T(8,128)S(1)} %project_rest.1), channel_id=1, replica_groups=mesh['rows'=8,'px'=4] {'rows'}, dimensions={0} | all-to-all | bytes 524288 | tf_op jit(solution)/shard_map/all_to_all | solution.py:478
  49.2 2.3 %back_1_theirs.1 = f32[8,4096]{1,0:T(8,128)S(1)} custom-call(f32[8,8,1024]{2,1,0:T(8,128)S(1)} %all_to_all.11.parts, f32[1,1024]{1,0:T(1,128)S(1)} %bitcast.38, f32[8,128]{1,0:T(8,128)S(1)} %get-tuple-element.29.sigma.refs_6_, bf16[8192,1024]{1,0:T(8,128)(2,1)S(1)} %get-tuple-element.30.e_vmem), custom_call_target="tpu_custom_call" | custom-call | flops 67108864 | bytes 16777216 | tf_op jit(solution)/shard_map/back_1_theirs/pallas_call | solution.py:42
  58.1 2.5 %collective-permute-start.9 = (f32[8,2048]{1,0:T(8,128)S(1)}, f32[8,2048]{1,0:T(8,128)S(1)}, u32[]{:S(2)}, u32[]{:S(2)}) collective-permute-start(f32[8,2048]{1,0:T(8,128)S(1)} %second_update.1), channel_id=1, source_target_pairs={{0,8},{1,24},{2,0},{3,16},{4,12},{5,28},{6,4},{7,20},{8,9},{9,25},... | collective-permute-start | bytes 196616 | tf_op jit(solution)/shard_map/ppermute | solution.py:490
  60.6 2.6 %collective-permute-start.5 = (f32[8,2048]{1,0:T(8,128)S(1)}, f32[8,2048]{1,0:T(8,128)S(1)}, u32[]{:S(2)}, u32[]{:S(2)}) collective-permute-start(f32[8,2048]{1,0:T(8,128)S(1)} %second_update.1), channel_id=1, source_target_pairs={{0,16},{1,0},{2,24},{3,8},{4,20},{5,4},{6,28},{7,12},{8,17},{9,1},... | collective-permute-start | bytes 196616 | tf_op jit(solution)/shard_map/ppermute | solution.py:490
  63.2 3.2 %collective-permute-start.6 = (f32[8,2048]{1,0:T(8,128)S(1)}, f32[8,2048]{1,0:T(8,128)S(1)}, u32[]{:S(2)}, u32[]{:S(2)}) collective-permute-start(f32[8,2048]{1,0:T(8,128)S(1)} %second_update.1), channel_id=1, source_target_pairs={{0,24},{1,8},{2,16},{3,0},{4,28},{5,12},{6,20},{7,4},{8,25},{9,9},... | collective-permute-start | bytes 196616 | tf_op jit(solution)/shard_map/ppermute | solution.py:490
  76.0 6.1 %all-gather = f32[64,512]{1,0:T(8,128)S(1)} all-gather(f32[16,512]{1,0:T(8,128)S(1)} %dots_0_3.1), channel_id=2, replica_groups=mesh['rows'=8,'px'=4] {'px'}, dimensions={0}, use_global_device_ids=true | all-gather | bytes 163840 | tf_op jit(solution)/shard_map/all_gather | solution.py:560
  86.9 2.5 %collective-permute-done.13.theirs = f32[2,8,2176]{2,1,0:T(8,128)S(1)} collective-permute-done((f32[2,8,2176]{2,1,0:T(8,128)S(1)}, f32[2,8,2176]{2,1,0:T(8,128)S(1)}, u32[]{:S(2)}, u32[]{:S(2)}) %collective-permute-start.13) | collective-permute-done | bytes 139296 | tf_op jit(solution)/shard_map/ppermute | solution.py:474
  89.6 2.4 %collective-permute-start.14 = (f32[8,2176]{1,0:T(8,128)S(1)}, f32[8,2176]{1,0:T(8,128)S(1)}, u32[]{:S(2)}, u32[]{:S(2)}) collective-permute-start(f32[8,2176]{1,0:T(8,128)S(1)} %get-tuple-element.40), channel_id=1, source_target_pairs={{0,16},{4,20},{8,24},{12,28},{16,0},{20,4},{24,8},{28,12},{1,17},{... | collective-permute-start | bytes 208904 | tf_op jit(solution)/shard_map/ppermute | solution.py:474
  94.1 2.9 %collective-permute-done.14.refs_2_ = f32[8,2176]{1,0:T(8,128)S(1)} collective-permute-done((f32[8,2176]{1,0:T(8,128)S(1)}, f32[8,2176]{1,0:T(8,128)S(1)}, u32[]{:S(2)}, u32[]{:S(2)}) %collective-permute-start.14) | collective-permute-done | bytes 69664 | tf_op jit(solution)/shard_map/ppermute | solution.py:474
  99.3 2.2 %collective-permute-start.16 = (f32[8,2176]{1,0:T(8,128)S(1)}, f32[8,2176]{1,0:T(8,128)S(1)}, u32[]{:S(2)}, u32[]{:S(2)}) collective-permute-start(f32[8,2176]{1,0:T(8,128)S(1)} %combine_0.1.refs_0_.refs_4_), channel_id=1, source_target_pairs={{0,16},{4,20},{8,24},{12,28},{16,0},{20,4},{24,8},{28,12},{1,17},{... | collective-permute-start | bytes 208904 | tf_op jit(solution)/shard_map/ppermute | solution.py:474
  105.1 2.6 %collective-permute-done.17.refs_1_ = f32[8,2176]{1,0:T(8,128)S(1)} collective-permute-done((f32[8,2176]{1,0:T(8,128)S(1)}, f32[8,2176]{1,0:T(8,128)S(1)}, u32[]{:S(2)}, u32[]{:S(2)}) %collective-permute-start.17) | collective-permute-done | bytes 69664 | tf_op jit(solution)/shard_map/ppermute | solution.py:474
  114.0 5.6 %all-gather.1 = f32[64,512]{1,0:T(8,128)S(1)} all-gather(f32[16,512]{1,0:T(8,128)S(1)} %dots_1_3.1), channel_id=3, replica_groups=mesh['rows'=8,'px'=4] {'px'}, dimensions={0}, use_global_device_ids=true | all-gather | bytes 163840 | tf_op jit(solution)/shard_map/all_gather | solution.py:560
  124.5 2.5 %collective-permute-done.23.theirs = f32[2,8,2176]{2,1,0:T(8,128)S(1)} collective-permute-done((f32[2,8,2176]{2,1,0:T(8,128)S(1)}, f32[2,8,2176]{2,1,0:T(8,128)S(1)}, u32[]{:S(2)}, u32[]{:S(2)}) %collective-permute-start.23) | collective-permute-done | bytes 139296 | tf_op jit(solution)/shard_map/ppermute | solution.py:474
  127.1 2.5 %collective-permute-start.25 = (f32[8,2176]{1,0:T(8,128)S(1)}, f32[8,2176]{1,0:T(8,128)S(1)}, u32[]{:S(2)}, u32[]{:S(2)}) collective-permute-start(f32[8,2176]{1,0:T(8,128)S(1)} %get-tuple-element.49), channel_id=1, source_target_pairs={{0,24},{4,28},{8,16},{12,20},{16,8},{20,12},{24,0},{28,4},{1,25},{... | collective-permute-start | bytes 208904 | tf_op jit(solution)/shard_map/ppermute | solution.py:474
  130.8 3.6 %collective-permute-done.24.refs_2_ = f32[8,2176]{1,0:T(8,128)S(1)} collective-permute-done((f32[8,2176]{1,0:T(8,128)S(1)}, f32[8,2176]{1,0:T(8,128)S(1)}, u32[]{:S(2)}, u32[]{:S(2)}) %collective-permute-start.24) | collective-permute-done | bytes 69664 | tf_op jit(solution)/shard_map/ppermute | solution.py:474
  136.1 2.2 %collective-permute-start.28 = (f32[8,2176]{1,0:T(8,128)S(1)}, f32[8,2176]{1,0:T(8,128)S(1)}, u32[]{:S(2)}, u32[]{:S(2)}) collective-permute-start(f32[8,2176]{1,0:T(8,128)S(1)} %combine_1.1.refs_0_), channel_id=1, source_target_pairs={{0,24},{4,28},{8,16},{12,20},{16,8},{20,12},{24,0},{28,4},{1,25},{... | collective-permute-start | bytes 208904 | tf_op jit(solution)/shard_map/ppermute | solution.py:474
  138.5 4.1 %collective-permute-done.27.refs_2_ = f32[8,2176]{1,0:T(8,128)S(1)} collective-permute-done((f32[8,2176]{1,0:T(8,128)S(1)}, f32[8,2176]{1,0:T(8,128)S(1)}, u32[]{:S(2)}, u32[]{:S(2)}) %collective-permute-start.27) | collective-permute-done | bytes 69664 | tf_op jit(solution)/shard_map/ppermute | solution.py:474
  144.8 2.9 %collective-permute-done.30.refs_5_ = f32[2,8,2176]{2,1,0:T(8,128)S(1)} collective-permute-done((f32[2,8,2176]{2,1,0:T(8,128)S(1)}, f32[2,8,2176]{2,1,0:T(8,128)S(1)}, u32[]{:S(2)}, u32[]{:S(2)}) %collective-permute-start.30) | collective-permute-done | bytes 139296 | tf_op jit(solution)/shard_map/ppermute | solution.py:474
  149.4 5.2 %all-gather.2 = f32[32,128]{1,0:T(8,128)S(1)} all-gather(f32[8,128]{1,0:T(8,128)S(1)} %squares.1), channel_id=4, replica_groups=mesh['rows'=8,'px'=4] {'px'}, dimensions={0}, use_global_device_ids=true | all-gather | bytes 20480 | tf_op jit(solution)/shard_map/all_gather | solution.py:576
  (103 shorter events, 52.5 us)
Async XLA Ops:
  27.4 6.2 %collective-permute-start.1 = (f32[8,4096]{1,0:T(8,128)S(1)}, f32[8,4096]{1,0:T(8,128)S(1)}, u32[]{:S(2)}, u32[]{:S(2)}) collective-permute-start(f32[8,4096]{1,0:T(8,128)S(1)} %add.3.mine), channel_id=1, source_target_pairs={{0,2},{1,3},{2,0},{3,1},{4,6},{5,7},{6,4},{7,5},{8,10},{9,11},{10,... | collective-permute-start | bytes 393224 | tf_op jit(solution)/shard_map/ppermute | solution.py:474
  57.5 8.9 %collective-permute-start.8 = (f32[8,2048]{1,0:T(8,128)S(1)}, f32[8,2048]{1,0:T(8,128)S(1)}, u32[]{:S(2)}, u32[]{:S(2)}) collective-permute-start(f32[8,2048]{1,0:T(8,128)S(1)} %second_update.1), channel_id=1, source_target_pairs={{0,0},{1,16},{2,8},{3,24},{4,4},{5,20},{6,12},{7,28},{8,1},{9,17},... | collective-permute-start | bytes 196616 | tf_op jit(solution)/shard_map/ppermute | solution.py:490
  58.1 8.3 %collective-permute-start.9 = (f32[8,2048]{1,0:T(8,128)S(1)}, f32[8,2048]{1,0:T(8,128)S(1)}, u32[]{:S(2)}, u32[]{:S(2)}) collective-permute-start(f32[8,2048]{1,0:T(8,128)S(1)} %second_update.1), channel_id=1, source_target_pairs={{0,8},{1,24},{2,0},{3,16},{4,12},{5,28},{6,4},{7,20},{8,9},{9,25},... | collective-permute-start | bytes 196616 | tf_op jit(solution)/shard_map/ppermute | solution.py:490
  60.6 6.6 %collective-permute-start.5 = (f32[8,2048]{1,0:T(8,128)S(1)}, f32[8,2048]{1,0:T(8,128)S(1)}, u32[]{:S(2)}, u32[]{:S(2)}) collective-permute-start(f32[8,2048]{1,0:T(8,128)S(1)} %second_update.1), channel_id=1, source_target_pairs={{0,16},{1,0},{2,24},{3,8},{4,20},{5,4},{6,28},{7,12},{8,17},{9,1},... | collective-permute-start | bytes 196616 | tf_op jit(solution)/shard_map/ppermute | solution.py:490
  63.2 5.6 %collective-permute-start.6 = (f32[8,2048]{1,0:T(8,128)S(1)}, f32[8,2048]{1,0:T(8,128)S(1)}, u32[]{:S(2)}, u32[]{:S(2)}) collective-permute-start(f32[8,2048]{1,0:T(8,128)S(1)} %second_update.1), channel_id=1, source_target_pairs={{0,24},{1,8},{2,16},{3,0},{4,28},{5,12},{6,20},{7,4},{8,25},{9,9},... | collective-permute-start | bytes 196616 | tf_op jit(solution)/shard_map/ppermute | solution.py:490
  66.5 6.3 %collective-permute-start.10 = (f32[2,8,2048]{2,1,0:T(8,128)S(1)}, f32[2,8,2048]{2,1,0:T(8,128)S(1)}, u32[]{:S(2)}, u32[]{:S(2)}) collective-permute-start(f32[2,8,2048]{2,1,0:T(8,128)S(1)} %pad_maximum_fusion.5), channel_id=1, source_target_pairs={{0,4},{4,0},{8,12},{12,8},{16,20},{20,16},{24,28},{28,24},{1,5},{5... | collective-permute-start | bytes 393224 | tf_op jit(solution)/shard_map/ppermute | solution.py:474
  68.8 6.0 %collective-permute-start.7 = (f32[2,8,2048]{2,1,0:T(8,128)S(1)}, f32[2,8,2048]{2,1,0:T(8,128)S(1)}, u32[]{:S(2)}, u32[]{:S(2)}) collective-permute-start(f32[2,8,2048]{2,1,0:T(8,128)S(1)} %pad_maximum_fusion.4), channel_id=1, source_target_pairs={{0,4},{4,0},{8,12},{12,8},{16,20},{20,16},{24,28},{28,24},{1,5},{5... | collective-permute-start | bytes 393224 | tf_op jit(solution)/shard_map/ppermute | solution.py:474
  82.9 6.5 %collective-permute-start.13 = (f32[2,8,2176]{2,1,0:T(8,128)S(1)}, f32[2,8,2176]{2,1,0:T(8,128)S(1)}, u32[]{:S(2)}, u32[]{:S(2)}) collective-permute-start(f32[2,8,2176]{2,1,0:T(8,128)S(1)} %get-tuple-element.39), channel_id=1, source_target_pairs={{0,4},{4,0},{8,12},{12,8},{16,20},{20,16},{24,28},{28,24},{1,5},{5... | collective-permute-start | bytes 417800 | tf_op jit(solution)/shard_map/ppermute | solution.py:474
  84.9 9.0 %collective-permute-start.11 = (f32[2,8,2176]{2,1,0:T(8,128)S(1)}, f32[2,8,2176]{2,1,0:T(8,128)S(1)}, u32[]{:S(2)}, u32[]{:S(2)}) collective-permute-start(f32[2,8,2176]{2,1,0:T(8,128)S(1)} %near_across_0.1), channel_id=1, source_target_pairs={{0,4},{4,0},{8,12},{12,8},{16,20},{20,16},{24,28},{28,24},{1,5},{5... | collective-permute-start | bytes 417800 | tf_op jit(solution)/shard_map/ppermute | solution.py:474
  89.6 7.4 %collective-permute-start.14 = (f32[8,2176]{1,0:T(8,128)S(1)}, f32[8,2176]{1,0:T(8,128)S(1)}, u32[]{:S(2)}, u32[]{:S(2)}) collective-permute-start(f32[8,2176]{1,0:T(8,128)S(1)} %get-tuple-element.40), channel_id=1, source_target_pairs={{0,16},{4,20},{8,24},{12,28},{16,0},{20,4},{24,8},{28,12},{1,17},{... | collective-permute-start | bytes 208904 | tf_op jit(solution)/shard_map/ppermute | solution.py:474
  92.0 6.2 %collective-permute-start.15 = (f32[8,2176]{1,0:T(8,128)S(1)}, f32[8,2176]{1,0:T(8,128)S(1)}, u32[]{:S(2)}, u32[]{:S(2)}) collective-permute-start(f32[8,2176]{1,0:T(8,128)S(1)} %get-tuple-element.41), channel_id=1, source_target_pairs={{0,24},{4,28},{8,16},{12,20},{16,8},{20,12},{24,0},{28,4},{1,25},{... | collective-permute-start | bytes 208904 | tf_op jit(solution)/shard_map/ppermute | solution.py:474
  99.3 5.7 %collective-permute-start.16 = (f32[8,2176]{1,0:T(8,128)S(1)}, f32[8,2176]{1,0:T(8,128)S(1)}, u32[]{:S(2)}, u32[]{:S(2)}) collective-permute-start(f32[8,2176]{1,0:T(8,128)S(1)} %combine_0.1.refs_0_.refs_4_), channel_id=1, source_target_pairs={{0,16},{4,20},{8,24},{12,28},{16,0},{20,4},{24,8},{28,12},{1,17},{... | collective-permute-start | bytes 208904 | tf_op jit(solution)/shard_map/ppermute | solution.py:474
  101.6 6.1 %collective-permute-start.17 = (f32[8,2176]{1,0:T(8,128)S(1)}, f32[8,2176]{1,0:T(8,128)S(1)}, u32[]{:S(2)}, u32[]{:S(2)}) collective-permute-start(f32[8,2176]{1,0:T(8,128)S(1)} %combine_0.1.refs_0_.refs_4_), channel_id=1, source_target_pairs={{0,24},{4,28},{8,16},{12,20},{16,8},{20,12},{24,0},{28,4},{1,25},{... | collective-permute-start | bytes 208904 | tf_op jit(solution)/shard_map/ppermute | solution.py:474
  103.5 7.5 %collective-permute-start.20 = (f32[2,8,2176]{2,1,0:T(8,128)S(1)}, f32[2,8,2176]{2,1,0:T(8,128)S(1)}, u32[]{:S(2)}, u32[]{:S(2)}) collective-permute-start(f32[2,8,2176]{2,1,0:T(8,128)S(1)} %pad_maximum_fusion.1), channel_id=1, source_target_pairs={{0,4},{4,0},{8,12},{12,8},{16,20},{20,16},{24,28},{28,24},{1,5},{5... | collective-permute-start | bytes 417800 | tf_op jit(solution)/shard_map/ppermute | solution.py:474
  107.7 5.1 %collective-permute-start.18 = (f32[2,8,2176]{2,1,0:T(8,128)S(1)}, f32[2,8,2176]{2,1,0:T(8,128)S(1)}, u32[]{:S(2)}, u32[]{:S(2)}) collective-permute-start(f32[2,8,2176]{2,1,0:T(8,128)S(1)} %pad_maximum_fusion), channel_id=1, source_target_pairs={{0,4},{4,0},{8,12},{12,8},{16,20},{20,16},{24,28},{28,24},{1,5},{5... | collective-permute-start | bytes 417800 | tf_op jit(solution)/shard_map/ppermute | solution.py:474
  120.5 6.5 %collective-permute-start.23 = (f32[2,8,2176]{2,1,0:T(8,128)S(1)}, f32[2,8,2176]{2,1,0:T(8,128)S(1)}, u32[]{:S(2)}, u32[]{:S(2)}) collective-permute-start(f32[2,8,2176]{2,1,0:T(8,128)S(1)} %get-tuple-element.47), channel_id=1, source_target_pairs={{0,4},{4,0},{8,12},{12,8},{16,20},{20,16},{24,28},{28,24},{1,5},{5... | collective-permute-start | bytes 417800 | tf_op jit(solution)/shard_map/ppermute | solution.py:474
  121.9 7.7 %collective-permute-start.21 = (f32[2,8,2176]{2,1,0:T(8,128)S(1)}, f32[2,8,2176]{2,1,0:T(8,128)S(1)}, u32[]{:S(2)}, u32[]{:S(2)}) collective-permute-start(f32[2,8,2176]{2,1,0:T(8,128)S(1)} %near_across_1.1), channel_id=1, source_target_pairs={{0,4},{4,0},{8,12},{12,8},{16,20},{20,16},{24,28},{28,24},{1,5},{5... | collective-permute-start | bytes 417800 | tf_op jit(solution)/shard_map/ppermute | solution.py:474
  127.1 7.3 %collective-permute-start.24 = (f32[8,2176]{1,0:T(8,128)S(1)}, f32[8,2176]{1,0:T(8,128)S(1)}, u32[]{:S(2)}, u32[]{:S(2)}) collective-permute-start(f32[8,2176]{1,0:T(8,128)S(1)} %get-tuple-element.48), channel_id=1, source_target_pairs={{0,16},{4,20},{8,24},{12,28},{16,0},{20,4},{24,8},{28,12},{1,17},{... | collective-permute-start | bytes 208904 | tf_op jit(solution)/shard_map/ppermute | solution.py:474
  127.1 7.2 %collective-permute-start.25 = (f32[8,2176]{1,0:T(8,128)S(1)}, f32[8,2176]{1,0:T(8,128)S(1)}, u32[]{:S(2)}, u32[]{:S(2)}) collective-permute-start(f32[8,2176]{1,0:T(8,128)S(1)} %get-tuple-element.49), channel_id=1, source_target_pairs={{0,24},{4,28},{8,16},{12,20},{16,8},{20,12},{24,0},{28,4},{1,25},{... | collective-permute-start | bytes 208904 | tf_op jit(solution)/shard_map/ppermute | solution.py:474
  135.0 7.6 %collective-permute-start.27 = (f32[8,2176]{1,0:T(8,128)S(1)}, f32[8,2176]{1,0:T(8,128)S(1)}, u32[]{:S(2)}, u32[]{:S(2)}) collective-permute-start(f32[8,2176]{1,0:T(8,128)S(1)} %combine_1.1.refs_0_), channel_id=1, source_target_pairs={{0,16},{4,20},{8,24},{12,28},{16,0},{20,4},{24,8},{28,12},{1,17},{... | collective-permute-start | bytes 208904 | tf_op jit(solution)/shard_map/ppermute | solution.py:474
  136.1 6.5 %collective-permute-start.28 = (f32[8,2176]{1,0:T(8,128)S(1)}, f32[8,2176]{1,0:T(8,128)S(1)}, u32[]{:S(2)}, u32[]{:S(2)}) collective-permute-start(f32[8,2176]{1,0:T(8,128)S(1)} %combine_1.1.refs_0_), channel_id=1, source_target_pairs={{0,24},{4,28},{8,16},{12,20},{16,8},{20,12},{24,0},{28,4},{1,25},{... | collective-permute-start | bytes 208904 | tf_op jit(solution)/shard_map/ppermute | solution.py:474
  138.3 5.9 %collective-permute-start.26 = (f32[8,2176]{1,0:T(8,128)S(1)}, f32[8,2176]{1,0:T(8,128)S(1)}, u32[]{:S(2)}, u32[]{:S(2)}) collective-permute-start(f32[8,2176]{1,0:T(8,128)S(1)} %combine_1.1.refs_0_), channel_id=1, source_target_pairs={{0,8},{4,12},{8,0},{12,4},{16,24},{20,28},{24,16},{28,20},{1,9},{5... | collective-permute-start | bytes 208904 | tf_op jit(solution)/shard_map/ppermute | solution.py:474
  142.7 5.1 %collective-permute-start.30 = (f32[2,8,2176]{2,1,0:T(8,128)S(1)}, f32[2,8,2176]{2,1,0:T(8,128)S(1)}, u32[]{:S(2)}, u32[]{:S(2)}) collective-permute-start(f32[2,8,2176]{2,1,0:T(8,128)S(1)} %pad_maximum_fusion.3), channel_id=1, source_target_pairs={{0,4},{4,0},{8,12},{12,8},{16,20},{20,16},{24,28},{28,24},{1,5},{5... | collective-permute-start | bytes 417800 | tf_op jit(solution)/shard_map/ppermute | solution.py:474
  144.2 5.1 %collective-permute-start.29 = (f32[2,8,2176]{2,1,0:T(8,128)S(1)}, f32[2,8,2176]{2,1,0:T(8,128)S(1)}, u32[]{:S(2)}, u32[]{:S(2)}) collective-permute-start(f32[2,8,2176]{2,1,0:T(8,128)S(1)} %pad_maximum_fusion.2), channel_id=1, source_target_pairs={{0,4},{4,0},{8,12},{12,8},{16,20},{20,16},{24,28},{28,24},{1,5},{5... | collective-permute-start | bytes 417800 | tf_op jit(solution)/shard_map/ppermute | solution.py:474
  (14 other events, 85.6 us)

commit v5 on v4

--- a/solution.py
+++ b/solution.py
@@ -103,11 +103,10 @@
         return total + jnp.dot(off.astype(bf16), e_vmem[at, :], preferred_element_type=f32)
 
     total = lax.fori_loop(0, CHUNKS, step, jnp.zeros((8, e_hbm.shape[1]), f32))
-    for k in range(copies.shape[0]):
-        copies[k] = total
-
-
-def load_project(queries, mean, basis, levels, row_count):
+    copies[...] = total
+
+
+def load_project(queries, mean, basis, levels):
     pixels, comps = basis.shape
     queries, mean, basis, levels = [
         pltpu.with_memory_space_constraint(x, pltpu.HBM) for x in (queries, mean, basis, levels)
@@ -115,7 +114,7 @@
     return call(
         load_project_kernel,
         [
-            shape((row_count, 8, comps)),
+            shape((8, comps)),
             shape((8, pixels)),
             pltpu.VMEM((pixels, comps), bf16),
             shape((8, PAD)),
@@ -142,7 +141,9 @@
     elif part == "theirs":
         start = (1 - core) * span
     else:
-        start = (2 * core + (upper if part == "keep" else 1 - upper)) * span
+        whose, which = part
+        side = core if whose == "mine" else 1 - core
+        start = (2 * side + (upper if which == "keep" else 1 - upper)) * span
     now = sigma[:, step : step + 1]
     coeff = jnp.sum(parts[...], axis=0)
     ev = eigenvalues[...]
@@ -159,13 +160,13 @@
 
 def back(step, part, parts, eigenvalues, sigma, e_vmem):
     pixels, comps = e_vmem.shape
-    span = pixels // (2 if part in ("mine", "theirs") else 4)
+    span = pixels // (2 if isinstance(part, str) else 4)
     return call(
         functools.partial(back_kernel, step, part),
         shape((8, span)),
         (parts, eigenvalues, sigma, in_vmem(e_vmem)),
         flops=16 * span * comps,
-        name=f"back_{step}_{part}",
+        name=f"back_{step}_" + (part if isinstance(part, str) else "_".join(part)),
     )
 
 
@@ -194,8 +195,7 @@
         return total + jnp.dot(part, e_vmem[at, :], preferred_element_type=f32)
 
     total = lax.fori_loop(0, half // tile, step, own[...])
-    for k in range(copies.shape[0]):
-        copies[k] = total
+    copies[...] = total
 
 
 def first_update_kernel(mine, theirs, offset, sigma, out):
@@ -206,19 +206,13 @@
     out[...] = image + ratio * (offset[:, rows_at(core * half, half, half)] - image)
 
 
-def give_kernel(image, other, out):
-    span = image.shape[1]
-    upper = lax.div(lax.axis_index("px"), 2)
-    out[...] = image[...] + other[:, rows_at((1 - upper) * span, span, span)]
-
-
 def second_update_kernel(image, other, given, offset, mean, sigma, out):
     span = image.shape[1]
     place = lax.axis_index("px")
     core, upper = lax.rem(place, 2), lax.div(place, 2)
     ratio = sigma[:, 2:3] / sigma[:, 1:2]
     at = rows_at(upper * span, span, span)
-    total = image[...] + other[:, at] + given[...]
+    total = image[...] + other[...] + given[...]
     average = mean[:, rows_at((2 * core + upper) * span, span, span)]
     out[...] = average + total + ratio * (offset[:, at] - total)
 
@@ -247,7 +241,9 @@
     px = lax.axis_size("px")
     per = lax.axis_size("rows") // px
     other = lax.bitwise_xor(lax.axis_index("rows"), k)
-    return rows_at((lax.rem(other, per) * px + lax.div(other, per)) * span, span, span)
+    place = lax.div(other, per)
+    place = lax.rem(place, 2) * (px // 2) + lax.div(place, 2)
+    return rows_at((lax.rem(other, per) * px + place) * span, span, span)
 
 
 def dots_kernel(offsets, fresh, *refs):
@@ -309,8 +305,8 @@
         out[i, :, span:] = tail
 
 
-def scores_kernel(step, ks, gathered, norms, classes, targets, sigma, slab, out, kept, tails, aside):
-    both = jnp.sum(gathered[...], axis=0)
+def scores_kernel(step, ks, g0, g1, g2, g3, norms, classes, targets, sigma, slab, out, kept, tails, aside):
+    both = (g0[...] + g1[...]) + (g2[...] + g3[...])
     inner = both[:8]
     if step == 0:
         norm = both[8:9]
@@ -434,7 +430,7 @@
             shape((8, PAD)),
             shape((8, slab_rows)),
         ],
-        (gathered, norms, classes, targets, sigma, in_vmem(slab)),
+        (*gathered, norms, classes, targets, sigma, in_vmem(slab)),
         flops=unit * len(ks),
         name=f"scores_{step}",
     )
@@ -474,8 +470,10 @@
     return lax.ppermute(x, axis, [(i, i ^ flip) for i in range(lax.axis_size(axis))])
 
 
-def swap_rows(x):
-    return lax.all_to_all(x, "rows", 0, 0, tiled=True)
+def sum_rows(x):
+    rows = lax.axis_size("rows")
+    mine = sum([exchange("rows", x, k) for k in range(2, rows, 2)], x)
+    return jnp.stack([mine, exchange("rows", mine, 1)])
 
 
 def to_readers(x, turn):
@@ -485,7 +483,7 @@
     for r in range(rows):
         for p in range(px):
             upper, core = divmod(p, 2)
-            place = (2 * core + upper) ^ turn
+            place = (2 * upper + core) ^ turn
             pairs.append((r * px + p, (place * per + r % per) * px + r // per))
     return lax.ppermute(x, ("rows", "px"), pairs)
 
@@ -503,9 +501,9 @@
     gauss_flops = 8 * pixels * comps
 
     copies, offset, basis, sigma, mean = load_project(
-        queries, pixel_mean[None, :], eigenbasis, level_ids, rows
-    )
-    parts = swap_rows(copies)
+        queries, pixel_mean[None, :], eigenbasis, level_ids
+    )
+    parts = sum_rows(copies)
     sent = exchange("px", back(0, "theirs", parts, values, sigma, basis), 1)
     image = back(0, "mine", parts, values, sigma, basis) + sent
     across = exchange("px", image, 2)
@@ -534,30 +532,29 @@
     )
     copies = call(
         project_rest_kernel,
-        shape((rows, 8, comps)),
+        shape((8, comps)),
         (other, own, in_vmem(basis)),
         flops=gauss_flops,
         name="project_rest",
     )
-    parts = swap_rows(copies)
-    sent = exchange("px", back(1, "theirs", parts, values, sigma, basis), 1)
-    given = call(
-        give_kernel,
-        shape((8, pixels // 4)),
-        (back(1, "give", parts, values, sigma, basis), sent),
-        name="give",
-    )
+    parts = sum_rows(copies)
+    def quarter(which, parts):
+        other = back(1, ("theirs", which), parts, values, sigma, basis)
+        other = exchange("px", other, 1)
+        return back(1, ("mine", which), parts, values, sigma, basis), other
+
+    given, parts = lax.optimization_barrier((sum(quarter("give", parts)), parts))
     given = exchange("px", given, 2)
     piece = call(
         second_update_kernel,
         shape((8, pixels // 4)),
-        (back(1, "keep", parts, values, sigma, basis), sent, given, offset, mean, sigma),
+        (*quarter("keep", parts), given, offset, mean, sigma),
         name="second_update",
     )
     state, products = read_slices(piece, norms, slab)
     scale = norms
     for step in range(2):
-        gathered = lax.all_gather(products, "px")
+        gathered = [products] + [exchange("px", products, k) for k in (2, 3, 1)]
         parts, aside = reduce_rows(step, gathered, norms, classes, targets, sigma, slab)
         if step == 0:
             norms = aside
@@ -573,7 +570,7 @@
             products = gather_dots(state, slab, "dots_1")
     pieces, offsets = gather_rows(state)
     squares = call(squares_kernel, shape((8, PAD)), pieces, name="squares")
-    squares = lax.all_gather(squares, "px")
+    squares = jnp.stack([squares] + [exchange("px", squares, k) for k in (2, 3, 1)])
     return call(
         functools.partial(finish_kernel, offsets),
         shape((8, slab_pixels)),

time: 156 us -> 150 us (0.962)
  blocking collectives: 45.7 us -> 0 us
  starting transfers between devices: 38.3 us -> 60.1 us
  waiting for transfers between devices: 30.6 us -> 48.7 us
    all_to_all x2 -> x0, blocking collectives: 28.8 us -> none  [swap_rows(): return lax.all_to_all(x, 'rows', 0, 0, tiled=True)]
    ppermute x27 -> x45, starting transfers between devices: 29.4 us -> 52.2 us  [exchange(): lax.ppermute(x, axis, [(i, i ^ flip) for i in range(lax.axis_size(axis))])]
    ppermute x27 -> x45, waiting for transfers between devices: 29 us -> 48.1 us  [exchange(): lax.ppermute(x, axis, [(i, i ^ flip) for i in range(lax.axis_size(axis))])]
    all_gather x3 -> x0, blocking collectives: 16.9 us -> none  [the longest x2 11.8 us: shards(): gathered = lax.all_gather(products, 'px')]
  transfers between devices with their start and end apart: 31 -> 49, of which waited for: 17 -> 28; matrix products, arithmetic and copies ran while one was open for 0% -> 0% of each run, Pallas kernels for 14% -> 15%
where the time goes in v5:
time: 150 us
  starting transfers between devices  60.1 us (40%)
  waiting for transfers between devices  48.7 us (32%)
  Pallas kernels  40.6 us (27%)
    ppermute x45, starting transfers between devices, exchange(): lax.ppermute(x, axis, [(i, i ^ flip) for i in range(lax.axis_size(axis))])  52.2 us
    ppermute x45, waiting for transfers between devices, exchange(): lax.ppermute(x, axis, [(i, i ^ flip) for i in range(lax.axis_size(axis))])  48.1 us
    pallas_call x37, Pallas kernels, call(): pl.pallas_call(kernel, in_specs=in_specs or [vmem()] * len(args), out_spe...  40.6 us
    ppermute x4, starting transfers between devices, to_readers(): return lax.ppermute(x, ('rows', 'px'), pairs)  7.9 us
  transfers between devices with their start and end apart: 49, of which 28 were waited for; matrix products, arithmetic and copies ran while one was open for 0% of the time, Pallas kernels for 15%

profile of v5, /device:TPU:0, one launch (start us, length us, event | category | flops | bytes accessed | tf_op | source)
XLA Modules:
  0.0 149.8 jit_solution(382672828906068156)
XLA Ops:
  0.0 6.7 %load_project.1 = (f32[8,1024]{1,0:T(8,128)S(1)}, f32[8,8192]{1,0:T(8,128)S(1)}, bf16[8192,1024]{1,0:T(8,128)(2,1)S(1)}, f32[8,128]{1,0:T(8,128)S(1)}, f32[1,8192]{1,0:T(1,128)S(1)}) custom-call(f32[8,8192]{1,0:T(8,128)} %q_hbm.1, f32[1,8192]{1,0:T(1,128)} %bitcast.53, bf16[8192,1024]{1,0:T(8,128)(2,1)} %e_hbm.1, s32[5,8]{1,0:T(8,128)} %levels_hbm.1), custom_call_target="tpu_custom_call" | custom-call | flops 134217728 | bytes 16777216 | tf_op jit(solution)/shard_map/load_project/pallas_call | solution.py:42
  6.7 3.1 %collective-permute-start = (f32[8,1024]{1,0:T(8,128)S(1)}, f32[8,1024]{1,0:T(8,128)S(1)}, u32[]{:S(2)}, u32[]{:S(2)}) collective-permute-start(f32[8,1024]{1,0:T(8,128)S(1)} %get-tuple-element.30), channel_id=1, source_target_pairs={{0,8},{4,12},{8,0},{12,4},{16,24},{20,28},{24,16},{28,20},{1,9},{5... | collective-permute-start | bytes 98312 | tf_op jit(solution)/shard_map/ppermute | solution.py:470
  9.8 2.6 %collective-permute-start.1 = (f32[8,1024]{1,0:T(8,128)S(1)}, f32[8,1024]{1,0:T(8,128)S(1)}, u32[]{:S(2)}, u32[]{:S(2)}) collective-permute-start(f32[8,1024]{1,0:T(8,128)S(1)} %get-tuple-element.30), channel_id=1, source_target_pairs={{0,16},{4,20},{8,24},{12,28},{16,0},{20,4},{24,8},{28,12},{1,17},{... | collective-permute-start | bytes 98312 | tf_op jit(solution)/shard_map/ppermute | solution.py:470
  12.4 2.8 %collective-permute-done.1 = f32[8,1024]{1,0:T(8,128)S(1)} collective-permute-done((f32[8,1024]{1,0:T(8,128)S(1)}, f32[8,1024]{1,0:T(8,128)S(1)}, u32[]{:S(2)}, u32[]{:S(2)}) %collective-permute-start.1) | collective-permute-done | bytes 32800 | tf_op jit(solution)/shard_map/ppermute | solution.py:470
  15.2 2.9 %collective-permute-done.2 = f32[8,1024]{1,0:T(8,128)S(1)} collective-permute-done((f32[8,1024]{1,0:T(8,128)S(1)}, f32[8,1024]{1,0:T(8,128)S(1)}, u32[]{:S(2)}, u32[]{:S(2)}) %collective-permute-start.2) | collective-permute-done | bytes 32800 | tf_op jit(solution)/shard_map/ppermute | solution.py:470
  19.7 2.4 %collective-permute-done.3 = f32[8,1024]{1,0:T(8,128)S(1)} collective-permute-done((f32[8,1024]{1,0:T(8,128)S(1)}, f32[8,1024]{1,0:T(8,128)S(1)}, u32[]{:S(2)}, u32[]{:S(2)}) %collective-permute-start.3) | collective-permute-done | bytes 32800 | tf_op jit(solution)/shard_map/ppermute | solution.py:470
  22.2 2.3 %back_0_theirs.1 = f32[8,4096]{1,0:T(8,128)S(1)} custom-call(f32[2,8,1024]{2,1,0:T(8,128)S(1)} %pad_maximum_fusion.6.parts, f32[1,1024]{1,0:T(1,128)S(1)} %bitcast.39, f32[8,128]{1,0:T(8,128)S(1)} %get-tuple-element.31.sigma.refs_6_, bf16[8192,1024]{1,0:T(8,128)(2,1)S(1)} %get-tuple-element.32.e_vmem), custom_call_target="tpu_custom_call" | custom-call | flops 67108864 | bytes 16777216 | tf_op jit(solution)/shard_map/back_0_theirs/pallas_call | solution.py:42
  24.5 2.3 %back_0_mine.1 = f32[8,4096]{1,0:T(8,128)S(1)} custom-call(f32[2,8,1024]{2,1,0:T(8,128)S(1)} %pad_maximum_fusion.6.parts, f32[1,1024]{1,0:T(1,128)S(1)} %bitcast.40, f32[8,128]{1,0:T(8,128)S(1)} %get-tuple-element.31.sigma.refs_6_, bf16[8192,1024]{1,0:T(8,128)(2,1)S(1)} %get-tuple-element.32.e_vmem), custom_call_target="tpu_custom_call" | custom-call | flops 67108864 | bytes 16777216 | tf_op jit(solution)/shard_map/back_0_mine/pallas_call | solution.py:42
  28.4 4.6 %norms.1.refs_5_ = f32[1,512]{1,0:T(1,128)S(1)} custom-call(bf16[512,16384]{1,0:T(8,128)(2,1)S(1)} %bitcast.26), custom_call_target="tpu_custom_call" | custom-call | flops 16777216 | bytes 16777216 | tf_op jit(solution)/shard_map/norms/pallas_call | solution.py:42
  36.8 3.5 %collective-permute-start.9 = (f32[8,1024]{1,0:T(8,128)S(1)}, f32[8,1024]{1,0:T(8,128)S(1)}, u32[]{:S(2)}, u32[]{:S(2)}) collective-permute-start(f32[8,1024]{1,0:T(8,128)S(1)} %project_rest.1), channel_id=1, source_target_pairs={{0,24},{4,28},{8,16},{12,20},{16,8},{20,12},{24,0},{28,4},{1,25},{... | collective-permute-start | bytes 98312 | tf_op jit(solution)/shard_map/ppermute | solution.py:470
  44.2 2.4 %collective-permute-done.10 = f32[8,1024]{1,0:T(8,128)S(1)} collective-permute-done((f32[8,1024]{1,0:T(8,128)S(1)}, f32[8,1024]{1,0:T(8,128)S(1)}, u32[]{:S(2)}, u32[]{:S(2)}) %collective-permute-start.10) | collective-permute-done | bytes 32800 | tf_op jit(solution)/shard_map/ppermute | solution.py:470
  57.7 3.1 %collective-permute-start.14 = (f32[8,2048]{1,0:T(8,128)S(1)}, f32[8,2048]{1,0:T(8,128)S(1)}, u32[]{:S(2)}, u32[]{:S(2)}) collective-permute-start(f32[8,2048]{1,0:T(8,128)S(1)} %second_update.1), channel_id=1, source_target_pairs={{0,16},{1,24},{2,0},{3,8},{4,20},{5,28},{6,4},{7,12},{8,17},{9,25}... | collective-permute-start | bytes 196616 | tf_op jit(solution)/shard_map/ppermute | solution.py:488
  60.8 2.2 %collective-permute-start.15 = (f32[8,2048]{1,0:T(8,128)S(1)}, f32[8,2048]{1,0:T(8,128)S(1)}, u32[]{:S(2)}, u32[]{:S(2)}) collective-permute-start(f32[8,2048]{1,0:T(8,128)S(1)} %second_update.1), channel_id=1, source_target_pairs={{0,24},{1,16},{2,8},{3,0},{4,28},{5,20},{6,12},{7,4},{8,25},{9,17}... | collective-permute-start | bytes 196616 | tf_op jit(solution)/shard_map/ppermute | solution.py:488
  71.6 4.4 %collective-permute-start.20 = (f32[16,512]{1,0:T(8,128)S(1)}, f32[16,512]{1,0:T(8,128)S(1)}, u32[]{:S(2)}, u32[]{:S(2)}) collective-permute-start(f32[16,512]{1,0:T(8,128)S(1)} %dots_0_3.1.g0), channel_id=1, source_target_pairs={{0,2},{1,3},{2,0},{3,1},{4,6},{5,7},{6,4},{7,5},{8,10},{9,11},{10,... | collective-permute-start | bytes 98312 | tf_op jit(solution)/shard_map/ppermute | solution.py:470
  84.2 2.2 %collective-permute-done.25.theirs = f32[2,8,2176]{2,1,0:T(8,128)S(1)} collective-permute-done((f32[2,8,2176]{2,1,0:T(8,128)S(1)}, f32[2,8,2176]{2,1,0:T(8,128)S(1)}, u32[]{:S(2)}, u32[]{:S(2)}) %collective-permute-start.25) | collective-permute-done | bytes 139296 | tf_op jit(solution)/shard_map/ppermute | solution.py:470
  90.6 2.6 %collective-permute-done.26.refs_2_ = f32[8,2176]{1,0:T(8,128)S(1)} collective-permute-done((f32[8,2176]{1,0:T(8,128)S(1)}, f32[8,2176]{1,0:T(8,128)S(1)}, u32[]{:S(2)}, u32[]{:S(2)}) %collective-permute-start.26) | collective-permute-done | bytes 69664 | tf_op jit(solution)/shard_map/ppermute | solution.py:470
  94.9 2.1 %collective-permute-done.24.refs_1_ = f32[8,2176]{1,0:T(8,128)S(1)} collective-permute-done((f32[8,2176]{1,0:T(8,128)S(1)}, f32[8,2176]{1,0:T(8,128)S(1)}, u32[]{:S(2)}, u32[]{:S(2)}) %collective-permute-start.24) | collective-permute-done | bytes 69664 | tf_op jit(solution)/shard_map/ppermute | solution.py:470
  98.9 2.7 %collective-permute-start.29 = (f32[8,2176]{1,0:T(8,128)S(1)}, f32[8,2176]{1,0:T(8,128)S(1)}, u32[]{:S(2)}, u32[]{:S(2)}) collective-permute-start(f32[8,2176]{1,0:T(8,128)S(1)} %combine_0.1.refs_0_.refs_4_), channel_id=1, source_target_pairs={{0,24},{4,28},{8,16},{12,20},{16,8},{20,12},{24,0},{28,4},{1,25},{... | collective-permute-start | bytes 208904 | tf_op jit(solution)/shard_map/ppermute | solution.py:470
  102.8 2.2 %collective-permute-done.29.refs_1_ = f32[8,2176]{1,0:T(8,128)S(1)} collective-permute-done((f32[8,2176]{1,0:T(8,128)S(1)}, f32[8,2176]{1,0:T(8,128)S(1)}, u32[]{:S(2)}, u32[]{:S(2)}) %collective-permute-start.29) | collective-permute-done | bytes 69664 | tf_op jit(solution)/shard_map/ppermute | solution.py:470
  120.7 2.5 %collective-permute-done.38.theirs = f32[2,8,2176]{2,1,0:T(8,128)S(1)} collective-permute-done((f32[2,8,2176]{2,1,0:T(8,128)S(1)}, f32[2,8,2176]{2,1,0:T(8,128)S(1)}, u32[]{:S(2)}, u32[]{:S(2)}) %collective-permute-start.38) | collective-permute-done | bytes 139296 | tf_op jit(solution)/shard_map/ppermute | solution.py:470
  123.4 2.2 %collective-permute-start.40 = (f32[8,2176]{1,0:T(8,128)S(1)}, f32[8,2176]{1,0:T(8,128)S(1)}, u32[]{:S(2)}, u32[]{:S(2)}) collective-permute-start(f32[8,2176]{1,0:T(8,128)S(1)} %get-tuple-element.53), channel_id=1, source_target_pairs={{0,24},{4,28},{8,16},{12,20},{16,8},{20,12},{24,0},{28,4},{1,25},{... | collective-permute-start | bytes 208904 | tf_op jit(solution)/shard_map/ppermute | solution.py:470
  127.0 3.1 %collective-permute-done.39.refs_2_ = f32[8,2176]{1,0:T(8,128)S(1)} collective-permute-done((f32[8,2176]{1,0:T(8,128)S(1)}, f32[8,2176]{1,0:T(8,128)S(1)}, u32[]{:S(2)}, u32[]{:S(2)}) %collective-permute-start.39) | collective-permute-done | bytes 69664 | tf_op jit(solution)/shard_map/ppermute | solution.py:470
  134.4 2.8 %collective-permute-done.42.refs_2_ = f32[8,2176]{1,0:T(8,128)S(1)} collective-permute-done((f32[8,2176]{1,0:T(8,128)S(1)}, f32[8,2176]{1,0:T(8,128)S(1)}, u32[]{:S(2)}, u32[]{:S(2)}) %collective-permute-start.42) | collective-permute-done | bytes 69664 | tf_op jit(solution)/shard_map/ppermute | solution.py:470
  140.7 2.9 %collective-permute-done.45.refs_5_ = f32[2,8,2176]{2,1,0:T(8,128)S(1)} collective-permute-done((f32[2,8,2176]{2,1,0:T(8,128)S(1)}, f32[2,8,2176]{2,1,0:T(8,128)S(1)}, u32[]{:S(2)}, u32[]{:S(2)}) %collective-permute-start.45) | collective-permute-done | bytes 139296 | tf_op jit(solution)/shard_map/ppermute | solution.py:470
  (140 shorter events, 78.8 us)
Async XLA Ops:
  6.7 5.7 %collective-permute-start = (f32[8,1024]{1,0:T(8,128)S(1)}, f32[8,1024]{1,0:T(8,128)S(1)}, u32[]{:S(2)}, u32[]{:S(2)}) collective-permute-start(f32[8,1024]{1,0:T(8,128)S(1)} %get-tuple-element.30), channel_id=1, source_target_pairs={{0,8},{4,12},{8,0},{12,4},{16,24},{20,28},{24,16},{28,20},{1,9},{5... | collective-permute-start | bytes 98312 | tf_op jit(solution)/shard_map/ppermute | solution.py:470
  12.4 5.7 %collective-permute-start.2 = (f32[8,1024]{1,0:T(8,128)S(1)}, f32[8,1024]{1,0:T(8,128)S(1)}, u32[]{:S(2)}, u32[]{:S(2)}) collective-permute-start(f32[8,1024]{1,0:T(8,128)S(1)} %get-tuple-element.30), channel_id=1, source_target_pairs={{0,24},{4,28},{8,16},{12,20},{16,8},{20,12},{24,0},{28,4},{1,25},{... | collective-permute-start | bytes 98312 | tf_op jit(solution)/shard_map/ppermute | solution.py:470
  26.8 6.2 %collective-permute-start.5 = (f32[8,4096]{1,0:T(8,128)S(1)}, f32[8,4096]{1,0:T(8,128)S(1)}, u32[]{:S(2)}, u32[]{:S(2)}) collective-permute-start(f32[8,4096]{1,0:T(8,128)S(1)} %add.27.mine), channel_id=1, source_target_pairs={{0,2},{1,3},{2,0},{3,1},{4,6},{5,7},{6,4},{7,5},{8,10},{9,11},{10,... | collective-permute-start | bytes 393224 | tf_op jit(solution)/shard_map/ppermute | solution.py:470
  36.8 5.8 %collective-permute-start.9 = (f32[8,1024]{1,0:T(8,128)S(1)}, f32[8,1024]{1,0:T(8,128)S(1)}, u32[]{:S(2)}, u32[]{:S(2)}) collective-permute-start(f32[8,1024]{1,0:T(8,128)S(1)} %project_rest.1), channel_id=1, source_target_pairs={{0,24},{4,28},{8,16},{12,20},{16,8},{20,12},{24,0},{28,4},{1,25},{... | collective-permute-start | bytes 98312 | tf_op jit(solution)/shard_map/ppermute | solution.py:470
  55.2 7.9 %collective-permute-start.17 = (f32[8,2048]{1,0:T(8,128)S(1)}, f32[8,2048]{1,0:T(8,128)S(1)}, u32[]{:S(2)}, u32[]{:S(2)}) collective-permute-start(f32[8,2048]{1,0:T(8,128)S(1)} %second_update.1), channel_id=1, source_target_pairs={{0,0},{1,8},{2,16},{3,24},{4,4},{5,12},{6,20},{7,28},{8,1},{9,9},{... | collective-permute-start | bytes 196616 | tf_op jit(solution)/shard_map/ppermute | solution.py:488
  55.8 7.3 %collective-permute-start.18 = (f32[8,2048]{1,0:T(8,128)S(1)}, f32[8,2048]{1,0:T(8,128)S(1)}, u32[]{:S(2)}, u32[]{:S(2)}) collective-permute-start(f32[8,2048]{1,0:T(8,128)S(1)} %second_update.1), channel_id=1, source_target_pairs={{0,8},{1,0},{2,24},{3,16},{4,12},{5,4},{6,28},{7,20},{8,9},{9,1},{... | collective-permute-start | bytes 196616 | tf_op jit(solution)/shard_map/ppermute | solution.py:488
  57.7 7.0 %collective-permute-start.14 = (f32[8,2048]{1,0:T(8,128)S(1)}, f32[8,2048]{1,0:T(8,128)S(1)}, u32[]{:S(2)}, u32[]{:S(2)}) collective-permute-start(f32[8,2048]{1,0:T(8,128)S(1)} %second_update.1), channel_id=1, source_target_pairs={{0,16},{1,24},{2,0},{3,8},{4,20},{5,28},{6,4},{7,12},{8,17},{9,25}... | collective-permute-start | bytes 196616 | tf_op jit(solution)/shard_map/ppermute | solution.py:488
  63.1 6.1 %collective-permute-start.19 = (f32[2,8,2048]{2,1,0:T(8,128)S(1)}, f32[2,8,2048]{2,1,0:T(8,128)S(1)}, u32[]{:S(2)}, u32[]{:S(2)}) collective-permute-start(f32[2,8,2048]{2,1,0:T(8,128)S(1)} %pad_maximum_fusion.5), channel_id=1, source_target_pairs={{0,4},{4,0},{8,12},{12,8},{16,20},{20,16},{24,28},{28,24},{1,5},{5... | collective-permute-start | bytes 393224 | tf_op jit(solution)/shard_map/ppermute | solution.py:470
  71.6 6.3 %collective-permute-start.20 = (f32[16,512]{1,0:T(8,128)S(1)}, f32[16,512]{1,0:T(8,128)S(1)}, u32[]{:S(2)}, u32[]{:S(2)}) collective-permute-start(f32[16,512]{1,0:T(8,128)S(1)} %dots_0_3.1.g0), channel_id=1, source_target_pairs={{0,2},{1,3},{2,0},{3,1},{4,6},{5,7},{6,4},{7,5},{8,10},{9,11},{10,... | collective-permute-start | bytes 98312 | tf_op jit(solution)/shard_map/ppermute | solution.py:470
  80.2 6.2 %collective-permute-start.25 = (f32[2,8,2176]{2,1,0:T(8,128)S(1)}, f32[2,8,2176]{2,1,0:T(8,128)S(1)}, u32[]{:S(2)}, u32[]{:S(2)}) collective-permute-start(f32[2,8,2176]{2,1,0:T(8,128)S(1)} %get-tuple-element.43), channel_id=1, source_target_pairs={{0,4},{4,0},{8,12},{12,8},{16,20},{20,16},{24,28},{28,24},{1,5},{5... | collective-permute-start | bytes 417800 | tf_op jit(solution)/shard_map/ppermute | solution.py:470
  82.4 8.0 %collective-permute-start.23 = (f32[2,8,2176]{2,1,0:T(8,128)S(1)}, f32[2,8,2176]{2,1,0:T(8,128)S(1)}, u32[]{:S(2)}, u32[]{:S(2)}) collective-permute-start(f32[2,8,2176]{2,1,0:T(8,128)S(1)} %near_across_0.1), channel_id=1, source_target_pairs={{0,4},{4,0},{8,12},{12,8},{16,20},{20,16},{24,28},{28,24},{1,5},{5... | collective-permute-start | bytes 417800 | tf_op jit(solution)/shard_map/ppermute | solution.py:470
  86.6 6.7 %collective-permute-start.26 = (f32[8,2176]{1,0:T(8,128)S(1)}, f32[8,2176]{1,0:T(8,128)S(1)}, u32[]{:S(2)}, u32[]{:S(2)}) collective-permute-start(f32[8,2176]{1,0:T(8,128)S(1)} %get-tuple-element.44), channel_id=1, source_target_pairs={{0,16},{4,20},{8,24},{12,28},{16,0},{20,4},{24,8},{28,12},{1,17},{... | collective-permute-start | bytes 208904 | tf_op jit(solution)/shard_map/ppermute | solution.py:470
  88.6 6.3 %collective-permute-start.27 = (f32[8,2176]{1,0:T(8,128)S(1)}, f32[8,2176]{1,0:T(8,128)S(1)}, u32[]{:S(2)}, u32[]{:S(2)}) collective-permute-start(f32[8,2176]{1,0:T(8,128)S(1)} %get-tuple-element.45), channel_id=1, source_target_pairs={{0,24},{4,28},{8,16},{12,20},{16,8},{20,12},{24,0},{28,4},{1,25},{... | collective-permute-start | bytes 208904 | tf_op jit(solution)/shard_map/ppermute | solution.py:470
  90.6 6.4 %collective-permute-start.24 = (f32[8,2176]{1,0:T(8,128)S(1)}, f32[8,2176]{1,0:T(8,128)S(1)}, u32[]{:S(2)}, u32[]{:S(2)}) collective-permute-start(f32[8,2176]{1,0:T(8,128)S(1)} %get-tuple-element.42), channel_id=1, source_target_pairs={{0,8},{4,12},{8,0},{12,4},{16,24},{20,28},{24,16},{28,20},{1,9},{5... | collective-permute-start | bytes 208904 | tf_op jit(solution)/shard_map/ppermute | solution.py:470
  97.2 5.6 %collective-permute-start.28 = (f32[8,2176]{1,0:T(8,128)S(1)}, f32[8,2176]{1,0:T(8,128)S(1)}, u32[]{:S(2)}, u32[]{:S(2)}) collective-permute-start(f32[8,2176]{1,0:T(8,128)S(1)} %combine_0.1.refs_0_.refs_4_), channel_id=1, source_target_pairs={{0,16},{4,20},{8,24},{12,28},{16,0},{20,4},{24,8},{28,12},{1,17},{... | collective-permute-start | bytes 208904 | tf_op jit(solution)/shard_map/ppermute | solution.py:470
  98.9 6.1 %collective-permute-start.29 = (f32[8,2176]{1,0:T(8,128)S(1)}, f32[8,2176]{1,0:T(8,128)S(1)}, u32[]{:S(2)}, u32[]{:S(2)}) collective-permute-start(f32[8,2176]{1,0:T(8,128)S(1)} %combine_0.1.refs_0_.refs_4_), channel_id=1, source_target_pairs={{0,24},{4,28},{8,16},{12,20},{16,8},{20,12},{24,0},{28,4},{1,25},{... | collective-permute-start | bytes 208904 | tf_op jit(solution)/shard_map/ppermute | solution.py:470
  101.6 6.4 %collective-permute-start.32 = (f32[2,8,2176]{2,1,0:T(8,128)S(1)}, f32[2,8,2176]{2,1,0:T(8,128)S(1)}, u32[]{:S(2)}, u32[]{:S(2)}) collective-permute-start(f32[2,8,2176]{2,1,0:T(8,128)S(1)} %pad_maximum_fusion.1), channel_id=1, source_target_pairs={{0,4},{4,0},{8,12},{12,8},{16,20},{20,16},{24,28},{28,24},{1,5},{5... | collective-permute-start | bytes 417800 | tf_op jit(solution)/shard_map/ppermute | solution.py:470
  116.7 6.5 %collective-permute-start.38 = (f32[2,8,2176]{2,1,0:T(8,128)S(1)}, f32[2,8,2176]{2,1,0:T(8,128)S(1)}, u32[]{:S(2)}, u32[]{:S(2)}) collective-permute-start(f32[2,8,2176]{2,1,0:T(8,128)S(1)} %get-tuple-element.51), channel_id=1, source_target_pairs={{0,4},{4,0},{8,12},{12,8},{16,20},{20,16},{24,28},{28,24},{1,5},{5... | collective-permute-start | bytes 417800 | tf_op jit(solution)/shard_map/ppermute | solution.py:470
  118.3 7.3 %collective-permute-start.36 = (f32[2,8,2176]{2,1,0:T(8,128)S(1)}, f32[2,8,2176]{2,1,0:T(8,128)S(1)}, u32[]{:S(2)}, u32[]{:S(2)}) collective-permute-start(f32[2,8,2176]{2,1,0:T(8,128)S(1)} %near_across_1.1), channel_id=1, source_target_pairs={{0,4},{4,0},{8,12},{12,8},{16,20},{20,16},{24,28},{28,24},{1,5},{5... | collective-permute-start | bytes 417800 | tf_op jit(solution)/shard_map/ppermute | solution.py:470
  123.3 6.8 %collective-permute-start.39 = (f32[8,2176]{1,0:T(8,128)S(1)}, f32[8,2176]{1,0:T(8,128)S(1)}, u32[]{:S(2)}, u32[]{:S(2)}) collective-permute-start(f32[8,2176]{1,0:T(8,128)S(1)} %get-tuple-element.52), channel_id=1, source_target_pairs={{0,16},{4,20},{8,24},{12,28},{16,0},{20,4},{24,8},{28,12},{1,17},{... | collective-permute-start | bytes 208904 | tf_op jit(solution)/shard_map/ppermute | solution.py:470
  123.4 6.8 %collective-permute-start.40 = (f32[8,2176]{1,0:T(8,128)S(1)}, f32[8,2176]{1,0:T(8,128)S(1)}, u32[]{:S(2)}, u32[]{:S(2)}) collective-permute-start(f32[8,2176]{1,0:T(8,128)S(1)} %get-tuple-element.53), channel_id=1, source_target_pairs={{0,24},{4,28},{8,16},{12,20},{16,8},{20,12},{24,0},{28,4},{1,25},{... | collective-permute-start | bytes 208904 | tf_op jit(solution)/shard_map/ppermute | solution.py:470
  130.9 6.3 %collective-permute-start.42 = (f32[8,2176]{1,0:T(8,128)S(1)}, f32[8,2176]{1,0:T(8,128)S(1)}, u32[]{:S(2)}, u32[]{:S(2)}) collective-permute-start(f32[8,2176]{1,0:T(8,128)S(1)} %combine_1.1.refs_0_), channel_id=1, source_target_pairs={{0,16},{4,20},{8,24},{12,28},{16,0},{20,4},{24,8},{28,12},{1,17},{... | collective-permute-start | bytes 208904 | tf_op jit(solution)/shard_map/ppermute | solution.py:470
  132.2 6.3 %collective-permute-start.43 = (f32[8,2176]{1,0:T(8,128)S(1)}, f32[8,2176]{1,0:T(8,128)S(1)}, u32[]{:S(2)}, u32[]{:S(2)}) collective-permute-start(f32[8,2176]{1,0:T(8,128)S(1)} %combine_1.1.refs_0_), channel_id=1, source_target_pairs={{0,24},{4,28},{8,16},{12,20},{16,8},{20,12},{24,0},{28,4},{1,25},{... | collective-permute-start | bytes 208904 | tf_op jit(solution)/shard_map/ppermute | solution.py:470
  139.4 5.8 %collective-permute-start.44 = (f32[2,8,2176]{2,1,0:T(8,128)S(1)}, f32[2,8,2176]{2,1,0:T(8,128)S(1)}, u32[]{:S(2)}, u32[]{:S(2)}) collective-permute-start(f32[2,8,2176]{2,1,0:T(8,128)S(1)} %pad_maximum_fusion.2), channel_id=1, source_target_pairs={{0,4},{4,0},{8,12},{12,8},{16,20},{20,16},{24,28},{28,24},{1,5},{5... | collective-permute-start | bytes 417800 | tf_op jit(solution)/shard_map/ppermute | solution.py:470
  (32 other events, 160.1 us)

commit v6 on v5

--- a/solution.py
+++ b/solution.py
@@ -284,7 +284,7 @@
     rows, px = lax.axis_size("rows"), lax.axis_size("px")
     per = rows // px
     got = [to_readers(piece, turn) for turn in range(px)]
-    halves = [range(px // 2), range(px // 2, px)]
+    halves = [range(1, px, 2), range(0, px, 2)]
     packs = [jnp.stack([got[t] for t in half]) for half in halves]
     groups = [([got[t] for t in half], [(t * per,) for t in half]) for half in halves]
     for k in range(1, per):
@@ -381,11 +381,12 @@
     rows = lax.axis_size("rows")
     near, far = spread(rows)
     got = {k: exchange("rows", state, k) if k else state for k in near + far}
-    first = exchange("rows", jnp.stack([got[k] for k in near]), 1)
-    second = exchange("rows", jnp.stack([got[k] for k in far]), 1)
+    one, two = near[:1] + far[:-1], near[1:] + far[-1:]
+    first = exchange("rows", jnp.stack([got[k] for k in one]), 1)
+    second = exchange("rows", jnp.stack([got[k] for k in two]), 1)
     pieces = [got[k] for k in near + far] + [first, second]
     offsets = [(k,) for k in near + far]
-    offsets += [tuple(k ^ 1 for k in near), tuple(k ^ 1 for k in far)]
+    offsets += [tuple(k ^ 1 for k in one), tuple(k ^ 1 for k in two)]
     return pieces, offsets
 
 

time: 150 us -> 148 us (0.987)
  waiting for transfers between devices: 48.7 us -> 46.1 us
    ppermute x45, waiting for transfers between devices: 48.1 us -> 45.7 us  [exchange(): lax.ppermute(x, axis, [(i, i ^ flip) for i in range(lax.axis_size(axis))])]
    ppermute x4, starting transfers between devices: 7.9 us -> 9.4 us  [to_readers(): return lax.ppermute(x, ('rows', 'px'), pairs)]
  transfers between devices with their start and end apart: 49 -> 49, of which waited for: 28 -> 32; matrix products, arithmetic and copies ran while one was open for 0% -> 0% of each run, Pallas kernels for 15% -> 15%
where the time goes in v6:
time: 148 us
  starting transfers between devices  60.6 us (41%)
  waiting for transfers between devices  46.1 us (31%)
  Pallas kernels  40.6 us (27%)
    ppermute x45, starting transfers between devices, exchange(): lax.ppermute(x, axis, [(i, i ^ flip) for i in range(lax.axis_size(axis))])  51.2 us
    ppermute x45, waiting for transfers between devices, exchange(): lax.ppermute(x, axis, [(i, i ^ flip) for i in range(lax.axis_size(axis))])  45.7 us
    pallas_call x37, Pallas kernels, call(): pl.pallas_call(kernel, in_specs=in_specs or [vmem()] * len(args), out_spe...  40.6 us
    ppermute x4, starting transfers between devices, to_readers(): return lax.ppermute(x, ('rows', 'px'), pairs)  9.4 us
  transfers between devices with their start and end apart: 49, of which 32 were waited for; matrix products, arithmetic and copies ran while one was open for 0% of the time, Pallas kernels for 15%

profile of v6, /device:TPU:0, one launch (start us, length us, event | category | flops | bytes accessed | tf_op | source)
XLA Modules:
  0.0 147.7 jit_solution(561774130289687150)
XLA Ops:
  0.0 6.7 %load_project.1 = (f32[8,1024]{1,0:T(8,128)S(1)}, f32[8,8192]{1,0:T(8,128)S(1)}, bf16[8192,1024]{1,0:T(8,128)(2,1)S(1)}, f32[8,128]{1,0:T(8,128)S(1)}, f32[1,8192]{1,0:T(1,128)S(1)}) custom-call(f32[8,8192]{1,0:T(8,128)} %q_hbm.1, f32[1,8192]{1,0:T(1,128)} %bitcast.53, bf16[8192,1024]{1,0:T(8,128)(2,1)} %e_hbm.1, s32[5,8]{1,0:T(8,128)} %levels_hbm.1), custom_call_target="tpu_custom_call" | custom-call | flops 134217728 | bytes 16777216 | tf_op jit(solution)/shard_map/load_project/pallas_call | solution.py:42
  6.7 3.1 %collective-permute-start = (f32[8,1024]{1,0:T(8,128)S(1)}, f32[8,1024]{1,0:T(8,128)S(1)}, u32[]{:S(2)}, u32[]{:S(2)}) collective-permute-start(f32[8,1024]{1,0:T(8,128)S(1)} %get-tuple-element.30), channel_id=1, source_target_pairs={{0,8},{4,12},{8,0},{12,4},{16,24},{20,28},{24,16},{28,20},{1,9},{5... | collective-permute-start | bytes 98312 | tf_op jit(solution)/shard_map/ppermute | solution.py:471
  9.8 2.6 %collective-permute-start.1 = (f32[8,1024]{1,0:T(8,128)S(1)}, f32[8,1024]{1,0:T(8,128)S(1)}, u32[]{:S(2)}, u32[]{:S(2)}) collective-permute-start(f32[8,1024]{1,0:T(8,128)S(1)} %get-tuple-element.30), channel_id=1, source_target_pairs={{0,16},{4,20},{8,24},{12,28},{16,0},{20,4},{24,8},{28,12},{1,17},{... | collective-permute-start | bytes 98312 | tf_op jit(solution)/shard_map/ppermute | solution.py:471
  12.4 2.8 %collective-permute-done.1 = f32[8,1024]{1,0:T(8,128)S(1)} collective-permute-done((f32[8,1024]{1,0:T(8,128)S(1)}, f32[8,1024]{1,0:T(8,128)S(1)}, u32[]{:S(2)}, u32[]{:S(2)}) %collective-permute-start.1) | collective-permute-done | bytes 32800 | tf_op jit(solution)/shard_map/ppermute | solution.py:471
  15.2 2.9 %collective-permute-done.2 = f32[8,1024]{1,0:T(8,128)S(1)} collective-permute-done((f32[8,1024]{1,0:T(8,128)S(1)}, f32[8,1024]{1,0:T(8,128)S(1)}, u32[]{:S(2)}, u32[]{:S(2)}) %collective-permute-start.2) | collective-permute-done | bytes 32800 | tf_op jit(solution)/shard_map/ppermute | solution.py:471
  19.7 2.4 %collective-permute-done.3 = f32[8,1024]{1,0:T(8,128)S(1)} collective-permute-done((f32[8,1024]{1,0:T(8,128)S(1)}, f32[8,1024]{1,0:T(8,128)S(1)}, u32[]{:S(2)}, u32[]{:S(2)}) %collective-permute-start.3) | collective-permute-done | bytes 32800 | tf_op jit(solution)/shard_map/ppermute | solution.py:471
  22.2 2.3 %back_0_theirs.1 = f32[8,4096]{1,0:T(8,128)S(1)} custom-call(f32[2,8,1024]{2,1,0:T(8,128)S(1)} %pad_maximum_fusion.6.parts, f32[1,1024]{1,0:T(1,128)S(1)} %bitcast.39, f32[8,128]{1,0:T(8,128)S(1)} %get-tuple-element.31.sigma.refs_6_, bf16[8192,1024]{1,0:T(8,128)(2,1)S(1)} %get-tuple-element.32.e_vmem), custom_call_target="tpu_custom_call" | custom-call | flops 67108864 | bytes 16777216 | tf_op jit(solution)/shard_map/back_0_theirs/pallas_call | solution.py:42
  24.5 2.3 %back_0_mine.1 = f32[8,4096]{1,0:T(8,128)S(1)} custom-call(f32[2,8,1024]{2,1,0:T(8,128)S(1)} %pad_maximum_fusion.6.parts, f32[1,1024]{1,0:T(1,128)S(1)} %bitcast.40, f32[8,128]{1,0:T(8,128)S(1)} %get-tuple-element.31.sigma.refs_6_, bf16[8192,1024]{1,0:T(8,128)(2,1)S(1)} %get-tuple-element.32.e_vmem), custom_call_target="tpu_custom_call" | custom-call | flops 67108864 | bytes 16777216 | tf_op jit(solution)/shard_map/back_0_mine/pallas_call | solution.py:42
  28.4 4.6 %norms.1.refs_5_ = f32[1,512]{1,0:T(1,128)S(1)} custom-call(bf16[512,16384]{1,0:T(8,128)(2,1)S(1)} %bitcast.26), custom_call_target="tpu_custom_call" | custom-call | flops 16777216 | bytes 16777216 | tf_op jit(solution)/shard_map/norms/pallas_call | solution.py:42
  36.8 3.5 %collective-permute-start.9 = (f32[8,1024]{1,0:T(8,128)S(1)}, f32[8,1024]{1,0:T(8,128)S(1)}, u32[]{:S(2)}, u32[]{:S(2)}) collective-permute-start(f32[8,1024]{1,0:T(8,128)S(1)} %project_rest.1), channel_id=1, source_target_pairs={{0,24},{4,28},{8,16},{12,20},{16,8},{20,12},{24,0},{28,4},{1,25},{... | collective-permute-start | bytes 98312 | tf_op jit(solution)/shard_map/ppermute | solution.py:471
  40.8 1.8 %collective-permute-done.9 = f32[8,1024]{1,0:T(8,128)S(1)} collective-permute-done((f32[8,1024]{1,0:T(8,128)S(1)}, f32[8,1024]{1,0:T(8,128)S(1)}, u32[]{:S(2)}, u32[]{:S(2)}) %collective-permute-start.9) | collective-permute-done | bytes 32800 | tf_op jit(solution)/shard_map/ppermute | solution.py:471
  44.2 2.4 %collective-permute-done.10 = f32[8,1024]{1,0:T(8,128)S(1)} collective-permute-done((f32[8,1024]{1,0:T(8,128)S(1)}, f32[8,1024]{1,0:T(8,128)S(1)}, u32[]{:S(2)}, u32[]{:S(2)}) %collective-permute-start.10) | collective-permute-done | bytes 32800 | tf_op jit(solution)/shard_map/ppermute | solution.py:471
  53.2 1.8 %collective-permute-done.13.given = f32[8,2048]{1,0:T(8,128)S(1)} collective-permute-done((f32[8,2048]{1,0:T(8,128)S(1)}, f32[8,2048]{1,0:T(8,128)S(1)}, u32[]{:S(2)}, u32[]{:S(2)}) %collective-permute-start.13) | collective-permute-done | bytes 65568 | tf_op jit(solution)/shard_map/ppermute | solution.py:471
  55.8 2.9 %collective-permute-start.18 = (f32[8,2048]{1,0:T(8,128)S(1)}, f32[8,2048]{1,0:T(8,128)S(1)}, u32[]{:S(2)}, u32[]{:S(2)}) collective-permute-start(f32[8,2048]{1,0:T(8,128)S(1)} %second_update.1), channel_id=1, source_target_pairs={{0,24},{1,16},{2,8},{3,0},{4,28},{5,20},{6,12},{7,4},{8,25},{9,17}... | collective-permute-start | bytes 196616 | tf_op jit(solution)/shard_map/ppermute | solution.py:489
  59.3 5.2 %collective-permute-start.15 = (f32[8,2048]{1,0:T(8,128)S(1)}, f32[8,2048]{1,0:T(8,128)S(1)}, u32[]{:S(2)}, u32[]{:S(2)}) collective-permute-start(f32[8,2048]{1,0:T(8,128)S(1)} %second_update.1), channel_id=1, source_target_pairs={{0,16},{1,24},{2,0},{3,8},{4,20},{5,28},{6,4},{7,12},{8,17},{9,25}... | collective-permute-start | bytes 196616 | tf_op jit(solution)/shard_map/ppermute | solution.py:489
  73.6 2.2 %collective-permute-start.20 = (f32[16,512]{1,0:T(8,128)S(1)}, f32[16,512]{1,0:T(8,128)S(1)}, u32[]{:S(2)}, u32[]{:S(2)}) collective-permute-start(f32[16,512]{1,0:T(8,128)S(1)} %dots_0_3.1.g0), channel_id=1, source_target_pairs={{0,2},{1,3},{2,0},{3,1},{4,6},{5,7},{6,4},{7,5},{8,10},{9,11},{10,... | collective-permute-start | bytes 98312 | tf_op jit(solution)/shard_map/ppermute | solution.py:471
  84.0 2.0 %collective-permute-done.25.theirs = f32[2,8,2176]{2,1,0:T(8,128)S(1)} collective-permute-done((f32[2,8,2176]{2,1,0:T(8,128)S(1)}, f32[2,8,2176]{2,1,0:T(8,128)S(1)}, u32[]{:S(2)}, u32[]{:S(2)}) %collective-permute-start.25) | collective-permute-done | bytes 139296 | tf_op jit(solution)/shard_map/ppermute | solution.py:471
  87.9 2.0 %collective-permute-start.24 = (f32[8,2176]{1,0:T(8,128)S(1)}, f32[8,2176]{1,0:T(8,128)S(1)}, u32[]{:S(2)}, u32[]{:S(2)}) collective-permute-start(f32[8,2176]{1,0:T(8,128)S(1)} %get-tuple-element.42), channel_id=1, source_target_pairs={{0,8},{4,12},{8,0},{12,4},{16,24},{20,28},{24,16},{28,20},{1,9},{5... | collective-permute-start | bytes 208904 | tf_op jit(solution)/shard_map/ppermute | solution.py:471
  89.9 2.1 %collective-permute-done.26.refs_2_ = f32[8,2176]{1,0:T(8,128)S(1)} collective-permute-done((f32[8,2176]{1,0:T(8,128)S(1)}, f32[8,2176]{1,0:T(8,128)S(1)}, u32[]{:S(2)}, u32[]{:S(2)}) %collective-permute-start.26) | collective-permute-done | bytes 69664 | tf_op jit(solution)/shard_map/ppermute | solution.py:471
  91.9 1.9 %collective-permute-done.27.refs_3_ = f32[8,2176]{1,0:T(8,128)S(1)} collective-permute-done((f32[8,2176]{1,0:T(8,128)S(1)}, f32[8,2176]{1,0:T(8,128)S(1)}, u32[]{:S(2)}, u32[]{:S(2)}) %collective-permute-start.27) | collective-permute-done | bytes 69664 | tf_op jit(solution)/shard_map/ppermute | solution.py:471
  98.5 1.9 %collective-permute-done.31.refs_0_ = f32[8,2176]{1,0:T(8,128)S(1)} collective-permute-done((f32[8,2176]{1,0:T(8,128)S(1)}, f32[8,2176]{1,0:T(8,128)S(1)}, u32[]{:S(2)}, u32[]{:S(2)}) %collective-permute-start.31) | collective-permute-done | bytes 69664 | tf_op jit(solution)/shard_map/ppermute | solution.py:471
  119.0 2.5 %collective-permute-done.38.theirs = f32[2,8,2176]{2,1,0:T(8,128)S(1)} collective-permute-done((f32[2,8,2176]{2,1,0:T(8,128)S(1)}, f32[2,8,2176]{2,1,0:T(8,128)S(1)}, u32[]{:S(2)}, u32[]{:S(2)}) %collective-permute-start.38) | collective-permute-done | bytes 139296 | tf_op jit(solution)/shard_map/ppermute | solution.py:471
  134.0 2.0 %collective-permute-done.43.refs_3_ = f32[8,2176]{1,0:T(8,128)S(1)} collective-permute-done((f32[8,2176]{1,0:T(8,128)S(1)}, f32[8,2176]{1,0:T(8,128)S(1)}, u32[]{:S(2)}, u32[]{:S(2)}) %collective-permute-start.43) | collective-permute-done | bytes 69664 | tf_op jit(solution)/shard_map/ppermute | solution.py:471
  138.8 2.3 %collective-permute-done.45.refs_5_ = f32[2,8,2176]{2,1,0:T(8,128)S(1)} collective-permute-done((f32[2,8,2176]{2,1,0:T(8,128)S(1)}, f32[2,8,2176]{2,1,0:T(8,128)S(1)}, u32[]{:S(2)}, u32[]{:S(2)}) %collective-permute-start.45) | collective-permute-done | bytes 139296 | tf_op jit(solution)/shard_map/ppermute | solution.py:471
  (140 shorter events, 81.2 us)
Async XLA Ops:
  6.7 5.7 %collective-permute-start = (f32[8,1024]{1,0:T(8,128)S(1)}, f32[8,1024]{1,0:T(8,128)S(1)}, u32[]{:S(2)}, u32[]{:S(2)}) collective-permute-start(f32[8,1024]{1,0:T(8,128)S(1)} %get-tuple-element.30), channel_id=1, source_target_pairs={{0,8},{4,12},{8,0},{12,4},{16,24},{20,28},{24,16},{28,20},{1,9},{5... | collective-permute-start | bytes 98312 | tf_op jit(solution)/shard_map/ppermute | solution.py:471
  12.4 5.7 %collective-permute-start.2 = (f32[8,1024]{1,0:T(8,128)S(1)}, f32[8,1024]{1,0:T(8,128)S(1)}, u32[]{:S(2)}, u32[]{:S(2)}) collective-permute-start(f32[8,1024]{1,0:T(8,128)S(1)} %get-tuple-element.30), channel_id=1, source_target_pairs={{0,24},{4,28},{8,16},{12,20},{16,8},{20,12},{24,0},{28,4},{1,25},{... | collective-permute-start | bytes 98312 | tf_op jit(solution)/shard_map/ppermute | solution.py:471
  26.8 6.2 %collective-permute-start.5 = (f32[8,4096]{1,0:T(8,128)S(1)}, f32[8,4096]{1,0:T(8,128)S(1)}, u32[]{:S(2)}, u32[]{:S(2)}) collective-permute-start(f32[8,4096]{1,0:T(8,128)S(1)} %add.27.mine), channel_id=1, source_target_pairs={{0,2},{1,3},{2,0},{3,1},{4,6},{5,7},{6,4},{7,5},{8,10},{9,11},{10,... | collective-permute-start | bytes 393224 | tf_op jit(solution)/shard_map/ppermute | solution.py:471
  36.8 5.8 %collective-permute-start.9 = (f32[8,1024]{1,0:T(8,128)S(1)}, f32[8,1024]{1,0:T(8,128)S(1)}, u32[]{:S(2)}, u32[]{:S(2)}) collective-permute-start(f32[8,1024]{1,0:T(8,128)S(1)} %project_rest.1), channel_id=1, source_target_pairs={{0,24},{4,28},{8,16},{12,20},{16,8},{20,12},{24,0},{28,4},{1,25},{... | collective-permute-start | bytes 98312 | tf_op jit(solution)/shard_map/ppermute | solution.py:471
  55.2 9.4 %collective-permute-start.17 = (f32[8,2048]{1,0:T(8,128)S(1)}, f32[8,2048]{1,0:T(8,128)S(1)}, u32[]{:S(2)}, u32[]{:S(2)}) collective-permute-start(f32[8,2048]{1,0:T(8,128)S(1)} %second_update.1), channel_id=1, source_target_pairs={{0,8},{1,0},{2,24},{3,16},{4,12},{5,4},{6,28},{7,20},{8,9},{9,1},{... | collective-permute-start | bytes 196616 | tf_op jit(solution)/shard_map/ppermute | solution.py:489
  55.8 8.8 %collective-permute-start.18 = (f32[8,2048]{1,0:T(8,128)S(1)}, f32[8,2048]{1,0:T(8,128)S(1)}, u32[]{:S(2)}, u32[]{:S(2)}) collective-permute-start(f32[8,2048]{1,0:T(8,128)S(1)} %second_update.1), channel_id=1, source_target_pairs={{0,24},{1,16},{2,8},{3,0},{4,28},{5,20},{6,12},{7,4},{8,25},{9,17}... | collective-permute-start | bytes 196616 | tf_op jit(solution)/shard_map/ppermute | solution.py:489
  58.7 7.5 %collective-permute-start.14 = (f32[8,2048]{1,0:T(8,128)S(1)}, f32[8,2048]{1,0:T(8,128)S(1)}, u32[]{:S(2)}, u32[]{:S(2)}) collective-permute-start(f32[8,2048]{1,0:T(8,128)S(1)} %second_update.1), channel_id=1, source_target_pairs={{0,0},{1,8},{2,16},{3,24},{4,4},{5,12},{6,20},{7,28},{8,1},{9,9},{... | collective-permute-start | bytes 196616 | tf_op jit(solution)/shard_map/ppermute | solution.py:489
  59.3 7.2 %collective-permute-start.15 = (f32[8,2048]{1,0:T(8,128)S(1)}, f32[8,2048]{1,0:T(8,128)S(1)}, u32[]{:S(2)}, u32[]{:S(2)}) collective-permute-start(f32[8,2048]{1,0:T(8,128)S(1)} %second_update.1), channel_id=1, source_target_pairs={{0,16},{1,24},{2,0},{3,8},{4,20},{5,28},{6,4},{7,12},{8,17},{9,25}... | collective-permute-start | bytes 196616 | tf_op jit(solution)/shard_map/ppermute | solution.py:489
  64.6 6.1 %collective-permute-start.19 = (f32[2,8,2048]{2,1,0:T(8,128)S(1)}, f32[2,8,2048]{2,1,0:T(8,128)S(1)}, u32[]{:S(2)}, u32[]{:S(2)}) collective-permute-start(f32[2,8,2048]{2,1,0:T(8,128)S(1)} %pad_maximum_fusion.5), channel_id=1, source_target_pairs={{0,4},{4,0},{8,12},{12,8},{16,20},{20,16},{24,28},{28,24},{1,5},{5... | collective-permute-start | bytes 393224 | tf_op jit(solution)/shard_map/ppermute | solution.py:471
  66.5 5.9 %collective-permute-start.16 = (f32[2,8,2048]{2,1,0:T(8,128)S(1)}, f32[2,8,2048]{2,1,0:T(8,128)S(1)}, u32[]{:S(2)}, u32[]{:S(2)}) collective-permute-start(f32[2,8,2048]{2,1,0:T(8,128)S(1)} %pad_maximum_fusion.4), channel_id=1, source_target_pairs={{0,4},{4,0},{8,12},{12,8},{16,20},{20,16},{24,28},{28,24},{1,5},{5... | collective-permute-start | bytes 393224 | tf_op jit(solution)/shard_map/ppermute | solution.py:471
  80.0 6.0 %collective-permute-start.25 = (f32[2,8,2176]{2,1,0:T(8,128)S(1)}, f32[2,8,2176]{2,1,0:T(8,128)S(1)}, u32[]{:S(2)}, u32[]{:S(2)}) collective-permute-start(f32[2,8,2176]{2,1,0:T(8,128)S(1)} %get-tuple-element.43), channel_id=1, source_target_pairs={{0,4},{4,0},{8,12},{12,8},{16,20},{20,16},{24,28},{28,24},{1,5},{5... | collective-permute-start | bytes 417800 | tf_op jit(solution)/shard_map/ppermute | solution.py:471
  82.0 5.8 %collective-permute-start.23 = (f32[2,8,2176]{2,1,0:T(8,128)S(1)}, f32[2,8,2176]{2,1,0:T(8,128)S(1)}, u32[]{:S(2)}, u32[]{:S(2)}) collective-permute-start(f32[2,8,2176]{2,1,0:T(8,128)S(1)} %near_across_0.1), channel_id=1, source_target_pairs={{0,4},{4,0},{8,12},{12,8},{16,20},{20,16},{24,28},{28,24},{1,5},{5... | collective-permute-start | bytes 417800 | tf_op jit(solution)/shard_map/ppermute | solution.py:471
  86.2 5.8 %collective-permute-start.26 = (f32[8,2176]{1,0:T(8,128)S(1)}, f32[8,2176]{1,0:T(8,128)S(1)}, u32[]{:S(2)}, u32[]{:S(2)}) collective-permute-start(f32[8,2176]{1,0:T(8,128)S(1)} %get-tuple-element.44), channel_id=1, source_target_pairs={{0,16},{4,20},{8,24},{12,28},{16,0},{20,4},{24,8},{28,12},{1,17},{... | collective-permute-start | bytes 208904 | tf_op jit(solution)/shard_map/ppermute | solution.py:471
  87.7 6.1 %collective-permute-start.27 = (f32[8,2176]{1,0:T(8,128)S(1)}, f32[8,2176]{1,0:T(8,128)S(1)}, u32[]{:S(2)}, u32[]{:S(2)}) collective-permute-start(f32[8,2176]{1,0:T(8,128)S(1)} %get-tuple-element.45), channel_id=1, source_target_pairs={{0,24},{4,28},{8,16},{12,20},{16,8},{20,12},{24,0},{28,4},{1,25},{... | collective-permute-start | bytes 208904 | tf_op jit(solution)/shard_map/ppermute | solution.py:471
  87.9 5.9 %collective-permute-start.24 = (f32[8,2176]{1,0:T(8,128)S(1)}, f32[8,2176]{1,0:T(8,128)S(1)}, u32[]{:S(2)}, u32[]{:S(2)}) collective-permute-start(f32[8,2176]{1,0:T(8,128)S(1)} %get-tuple-element.42), channel_id=1, source_target_pairs={{0,8},{4,12},{8,0},{12,4},{16,24},{20,28},{24,16},{28,20},{1,9},{5... | collective-permute-start | bytes 208904 | tf_op jit(solution)/shard_map/ppermute | solution.py:471
  94.1 6.3 %collective-permute-start.31 = (f32[8,2176]{1,0:T(8,128)S(1)}, f32[8,2176]{1,0:T(8,128)S(1)}, u32[]{:S(2)}, u32[]{:S(2)}) collective-permute-start(f32[8,2176]{1,0:T(8,128)S(1)} %combine_0.1.refs_0_.refs_4_), channel_id=1, source_target_pairs={{0,16},{4,20},{8,24},{12,28},{16,0},{20,4},{24,8},{28,12},{1,17},{... | collective-permute-start | bytes 208904 | tf_op jit(solution)/shard_map/ppermute | solution.py:471
  95.4 6.4 %collective-permute-start.28 = (f32[8,2176]{1,0:T(8,128)S(1)}, f32[8,2176]{1,0:T(8,128)S(1)}, u32[]{:S(2)}, u32[]{:S(2)}) collective-permute-start(f32[8,2176]{1,0:T(8,128)S(1)} %combine_0.1.refs_0_.refs_4_), channel_id=1, source_target_pairs={{0,8},{4,12},{8,0},{12,4},{16,24},{20,28},{24,16},{28,20},{1,9},{5... | collective-permute-start | bytes 208904 | tf_op jit(solution)/shard_map/ppermute | solution.py:471
  96.9 6.1 %collective-permute-start.29 = (f32[8,2176]{1,0:T(8,128)S(1)}, f32[8,2176]{1,0:T(8,128)S(1)}, u32[]{:S(2)}, u32[]{:S(2)}) collective-permute-start(f32[8,2176]{1,0:T(8,128)S(1)} %combine_0.1.refs_0_.refs_4_), channel_id=1, source_target_pairs={{0,24},{4,28},{8,16},{12,20},{16,8},{20,12},{24,0},{28,4},{1,25},{... | collective-permute-start | bytes 208904 | tf_op jit(solution)/shard_map/ppermute | solution.py:471
  100.5 6.6 %collective-permute-start.32 = (f32[2,8,2176]{2,1,0:T(8,128)S(1)}, f32[2,8,2176]{2,1,0:T(8,128)S(1)}, u32[]{:S(2)}, u32[]{:S(2)}) collective-permute-start(f32[2,8,2176]{2,1,0:T(8,128)S(1)} %pad_maximum_fusion.1), channel_id=1, source_target_pairs={{0,4},{4,0},{8,12},{12,8},{16,20},{20,16},{24,28},{28,24},{1,5},{5... | collective-permute-start | bytes 417800 | tf_op jit(solution)/shard_map/ppermute | solution.py:471
  115.0 6.5 %collective-permute-start.38 = (f32[2,8,2176]{2,1,0:T(8,128)S(1)}, f32[2,8,2176]{2,1,0:T(8,128)S(1)}, u32[]{:S(2)}, u32[]{:S(2)}) collective-permute-start(f32[2,8,2176]{2,1,0:T(8,128)S(1)} %get-tuple-element.51), channel_id=1, source_target_pairs={{0,4},{4,0},{8,12},{12,8},{16,20},{20,16},{24,28},{28,24},{1,5},{5... | collective-permute-start | bytes 417800 | tf_op jit(solution)/shard_map/ppermute | solution.py:471
  116.9 6.7 %collective-permute-start.36 = (f32[2,8,2176]{2,1,0:T(8,128)S(1)}, f32[2,8,2176]{2,1,0:T(8,128)S(1)}, u32[]{:S(2)}, u32[]{:S(2)}) collective-permute-start(f32[2,8,2176]{2,1,0:T(8,128)S(1)} %near_across_1.1), channel_id=1, source_target_pairs={{0,4},{4,0},{8,12},{12,8},{16,20},{20,16},{24,28},{28,24},{1,5},{5... | collective-permute-start | bytes 417800 | tf_op jit(solution)/shard_map/ppermute | solution.py:471
  121.7 6.4 %collective-permute-start.40 = (f32[8,2176]{1,0:T(8,128)S(1)}, f32[8,2176]{1,0:T(8,128)S(1)}, u32[]{:S(2)}, u32[]{:S(2)}) collective-permute-start(f32[8,2176]{1,0:T(8,128)S(1)} %get-tuple-element.53), channel_id=1, source_target_pairs={{0,24},{4,28},{8,16},{12,20},{16,8},{20,12},{24,0},{28,4},{1,25},{... | collective-permute-start | bytes 208904 | tf_op jit(solution)/shard_map/ppermute | solution.py:471
  129.9 6.1 %collective-permute-start.43 = (f32[8,2176]{1,0:T(8,128)S(1)}, f32[8,2176]{1,0:T(8,128)S(1)}, u32[]{:S(2)}, u32[]{:S(2)}) collective-permute-start(f32[8,2176]{1,0:T(8,128)S(1)} %combine_1.1.refs_0_), channel_id=1, source_target_pairs={{0,24},{4,28},{8,16},{12,20},{16,8},{20,12},{24,0},{28,4},{1,25},{... | collective-permute-start | bytes 208904 | tf_op jit(solution)/shard_map/ppermute | solution.py:471
  131.5 6.0 %collective-permute-start.42 = (f32[8,2176]{1,0:T(8,128)S(1)}, f32[8,2176]{1,0:T(8,128)S(1)}, u32[]{:S(2)}, u32[]{:S(2)}) collective-permute-start(f32[8,2176]{1,0:T(8,128)S(1)} %combine_1.1.refs_0_), channel_id=1, source_target_pairs={{0,16},{4,20},{8,24},{12,28},{16,0},{20,4},{24,8},{28,12},{1,17},{... | collective-permute-start | bytes 208904 | tf_op jit(solution)/shard_map/ppermute | solution.py:471
  (32 other events, 157.2 us)

commit v7 on v6

--- a/solution.py
+++ b/solution.py
@@ -45,7 +45,7 @@
         out_specs=[vmem()] * len(out_shape) if many else vmem(),
         out_shape=out_shape,
         scratch_shapes=list(scratch),
-        compiler_params=pltpu.CompilerParams(vmem_limit_bytes=10 * MIB),
+        compiler_params=pltpu.CompilerParams(vmem_limit_bytes=4 * MIB),
         cost_estimate=pl.CostEstimate(
             flops=flops, bytes_accessed=16 * MIB if flops else MIB, transcendentals=0
         ),
@@ -65,28 +65,41 @@
 
 
 def load_project_kernel(
-    q_hbm, mean_hbm, e_hbm, levels_hbm, copies, offset, e_vmem, sigma, mean, q, levels, sems
+    q_hbm, mean_hbm, e_hbm, levels_hbm, copies, offset, mine, theirs, sigma, mean, q, levels, sems
 ):
     pixels = e_hbm.shape[0]
     chunk = pixels // CHUNKS
 
-    def moves(c):
-        at = rows_at(c * chunk, chunk, chunk)
-        return (
-            pltpu.make_async_copy(q_hbm.at[:, at], q.at[:, at], sems.at[c, 0]),
-            pltpu.make_async_copy(mean_hbm.at[:, at], mean.at[:, at], sems.at[c, 1]),
-            pltpu.make_async_copy(e_hbm.at[at], e_vmem.at[at], sems.at[c, 2]),
+    core = lax.rem(lax.axis_index("px"), 2)
+    sides = ((core, mine), (1 - core, theirs))
+
+    def source(side, c):
+        return rows_at(side * (pixels // 2) + c * chunk, chunk, chunk)
+
+    def move(i, c):
+        side, held = sides[i]
+        to = rows_at(c * chunk, chunk, chunk)
+        return pltpu.make_async_copy(
+            e_hbm.at[source(side, c)], held.at[to], sems.at[i * (CHUNKS // 2) + c]
         )
 
-    tables = pltpu.make_async_copy(levels_hbm, levels, sems.at[CHUNKS, 0])
-    tables.start()
-
-    @pl.loop(0, CHUNKS)
-    def _(c):
-        for move in moves(c):
-            move.start()
-
-    tables.wait()
+    small = [
+        pltpu.make_async_copy(source, held, sems.at[CHUNKS + i])
+        for i, (source, held) in enumerate(
+            ((levels_hbm, levels), (q_hbm, q), (mean_hbm, mean))
+        )
+    ]
+    small[1].start()
+    small[2].start()
+    small[0].start()
+
+    for i in range(2):
+
+        @pl.loop(0, CHUNKS // 2)
+        def _(c, i=i):
+            move(i, c).start()
+
+    small[0].wait()
     lane = lax.broadcasted_iota(jnp.int32, sigma.shape, 1)
     table = jnp.zeros(sigma.shape, f32)
     for t in range(levels.shape[0]):
@@ -94,15 +107,20 @@
         table = jnp.where(lane == t, 0.6 * jnp.exp2(fraction), table)
     sigma[...] = table
 
-    def step(c, total):
-        for move in moves(c):
-            move.wait()
-        at = rows_at(c * chunk, chunk, chunk)
+    def step(i, c, total):
+        side, held = sides[i]
+        move(i, c).wait()
+        at = source(side, c)
         off = q[:, at] - mean[:, at]
         offset[:, at] = off
-        return total + jnp.dot(off.astype(bf16), e_vmem[at, :], preferred_element_type=f32)
-
-    total = lax.fori_loop(0, CHUNKS, step, jnp.zeros((8, e_hbm.shape[1]), f32))
+        block = held[rows_at(c * chunk, chunk, chunk), :]
+        return total + jnp.dot(off.astype(bf16), block, preferred_element_type=f32)
+
+    small[1].wait()
+    small[2].wait()
+    total = jnp.zeros((8, e_hbm.shape[1]), f32)
+    for i in range(2):
+        total = lax.fori_loop(0, CHUNKS // 2, functools.partial(step, i), total)
     copies[...] = total
 
 
@@ -116,7 +134,8 @@
         [
             shape((8, comps)),
             shape((8, pixels)),
-            pltpu.VMEM((pixels, comps), bf16),
+            pltpu.VMEM((pixels // 2, comps), bf16),
+            pltpu.VMEM((pixels // 2, comps), bf16),
             shape((8, PAD)),
             shape((1, pixels)),
         ],
@@ -125,77 +144,69 @@
         scratch=[
             pltpu.VMEM((8, pixels), f32),
             pltpu.VMEM(levels.shape, jnp.int32),
-            pltpu.SemaphoreType.DMA((CHUNKS + 1, 3)),
+            pltpu.SemaphoreType.DMA((CHUNKS + 3,)),
         ],
         flops=16 * pixels * comps,
         name="load_project",
     )
 
 
-def back_kernel(step, part, parts, eigenvalues, sigma, e_vmem, image):
+def turn_kernel(anchor, half, out):
+    pixels = half.shape[0]
+    tile = min(1024, pixels)
+
+    @pl.loop(0, pixels // tile)
+    def _(i):
+        at = rows_at(i * tile, tile, tile)
+        for k in range(out.shape[0] // 128):
+            comps = slice(k * 128, (k + 1) * 128)
+            out[comps, at] = half[at, comps].T
+
+
+def turned(half, name, anchor):
+    pixels, comps = half.shape
+    return call(
+        turn_kernel,
+        pltpu.VMEM((comps, pixels), bf16),
+        (anchor, in_vmem(half)),
+        flops=pixels * comps,
+        name=f"turn_{name}",
+    )
+
+
+def back_kernel(step, part, parts, eigenvalues, sigma, half, image):
     span = image.shape[1]
-    place = lax.axis_index("px")
-    core, upper = lax.rem(place, 2), lax.div(place, 2)
-    if part == "mine":
-        start = core * span
-    elif part == "theirs":
-        start = (1 - core) * span
-    else:
-        whose, which = part
-        side = core if whose == "mine" else 1 - core
-        start = (2 * side + (upper if which == "keep" else 1 - upper)) * span
     now = sigma[:, step : step + 1]
     coeff = jnp.sum(parts[...], axis=0)
     ev = eigenvalues[...]
     shrunk = (coeff * (ev / (ev + now * now))).astype(bf16)
-    tile = min(4096, span)
-
-    @pl.loop(0, span // tile)
-    def _(i):
-        at = rows_at(start + i * tile, tile, tile)
-        image[:, rows_at(i * tile, tile, tile)] = lax.dot_general(
-            shrunk, e_vmem[at, :], NT, preferred_element_type=f32
-        )
-
-
-def back(step, part, parts, eigenvalues, sigma, e_vmem):
-    pixels, comps = e_vmem.shape
-    span = pixels // (2 if isinstance(part, str) else 4)
+    if part == "whole":
+        image[...] = jnp.dot(shrunk, half[...], preferred_element_type=f32)
+    else:
+        upper = lax.div(lax.axis_index("px"), 2)
+        at = rows_at((upper if part == "keep" else 1 - upper) * span, span, span)
+        image[...] = jnp.dot(shrunk, half[:, at], preferred_element_type=f32)
+
+
+def back(step, part, parts, eigenvalues, sigma, half, name):
+    comps, pixels = half.shape
+    span = pixels if part == "whole" else pixels // 2
     return call(
         functools.partial(back_kernel, step, part),
         shape((8, span)),
-        (parts, eigenvalues, sigma, in_vmem(e_vmem)),
+        (parts, eigenvalues, sigma, in_vmem(half)),
         flops=16 * span * comps,
-        name=f"back_{step}_" + (part if isinstance(part, str) else "_".join(part)),
-    )
-
-
-def project_half_kernel(flip, off, e_vmem, out):
-    half = off.shape[1]
-    core = lax.rem(lax.axis_index("px"), 2)
-    which = 1 - core if flip else core
-    tile = min(4096, half)
-
-    def step(i, total):
-        at = rows_at(which * half + i * tile, tile, tile)
-        part = off[:, rows_at(i * tile, tile, tile)].astype(bf16)
-        return total + jnp.dot(part, e_vmem[at, :], preferred_element_type=f32)
-
-    out[...] = lax.fori_loop(0, half // tile, step, jnp.zeros(out.shape, f32))
-
-
-def project_rest_kernel(off, own, e_vmem, copies):
-    half = off.shape[1]
-    which = 1 - lax.rem(lax.axis_index("px"), 2)
-    tile = min(4096, half)
-
-    def step(i, total):
-        at = rows_at(which * half + i * tile, tile, tile)
-        part = off[:, rows_at(i * tile, tile, tile)].astype(bf16)
-        return total + jnp.dot(part, e_vmem[at, :], preferred_element_type=f32)
-
-    total = lax.fori_loop(0, half // tile, step, own[...])
-    copies[...] = total
+        name=f"back_{step}_{name}",
+    )
+
+
+def project_kernel(off, half, out):
+    out[...] = jnp.dot(off[...].astype(bf16), half[...], preferred_element_type=f32)
+
+
+def project_rest_kernel(off, own, half, out):
+    part = lax.dot_general(off[...].astype(bf16), half[...], NT, preferred_element_type=f32)
+    out[...] = own[...] + part
 
 
 def first_update_kernel(mine, theirs, offset, sigma, out):
@@ -206,13 +217,19 @@
     out[...] = image + ratio * (offset[:, rows_at(core * half, half, half)] - image)
 
 
+def give_kernel(image, other, out):
+    span = image.shape[1]
+    upper = lax.div(lax.axis_index("px"), 2)
+    out[...] = image[...] + other[:, rows_at((1 - upper) * span, span, span)]
+
+
 def second_update_kernel(image, other, given, offset, mean, sigma, out):
     span = image.shape[1]
     place = lax.axis_index("px")
     core, upper = lax.rem(place, 2), lax.div(place, 2)
     ratio = sigma[:, 2:3] / sigma[:, 1:2]
     at = rows_at(upper * span, span, span)
-    total = image[...] + other[...] + given[...]
+    total = image[...] + other[:, at] + given[...]
     average = mean[:, rows_at((2 * core + upper) * span, span, span)]
     out[...] = average + total + ratio * (offset[:, at] - total)
 
@@ -471,10 +488,17 @@
     return lax.ppermute(x, axis, [(i, i ^ flip) for i in range(lax.axis_size(axis))])
 
 
-def sum_rows(x):
+def sum_rows(x, beside=()):
     rows = lax.axis_size("rows")
-    mine = sum([exchange("rows", x, k) for k in range(2, rows, 2)], x)
-    return jnp.stack([mine, exchange("rows", mine, 1)])
+    parts = [exchange("rows", x, k) for k in range(2, rows, 2)]
+    done = [work(x) for work in beside]
+    if done:
+        parts, done[0] = lax.optimization_barrier((parts, done[0]))
+    mine = sum(parts, x)
+    other = exchange("rows", mine, 1)
+    if done:
+        other, done[1] = lax.optimization_barrier((other, done[1]))
+    return jnp.stack([mine, other]), done
 
 
 def to_readers(x, turn):
@@ -501,12 +525,18 @@
     targets = target_categories[None, :]
     gauss_flops = 8 * pixels * comps
 
-    copies, offset, basis, sigma, mean = load_project(
+    copies, offset, *basis, sigma, mean = load_project(
         queries, pixel_mean[None, :], eigenbasis, level_ids
     )
-    parts = sum_rows(copies)
-    sent = exchange("px", back(0, "theirs", parts, values, sigma, basis), 1)
-    image = back(0, "mine", parts, values, sigma, basis) + sent
+    parts, (theirs, mine) = sum_rows(
+        copies,
+        [
+            functools.partial(turned, basis[1], "theirs"),
+            functools.partial(turned, basis[0], "mine"),
+        ],
+    )
+    sent = exchange("px", back(0, "whole", parts, values, sigma, theirs, "theirs"), 1)
+    image = back(0, "whole", parts, values, sigma, mine, "mine") + sent
     across = exchange("px", image, 2)
     norms = call(
         norms_kernel,
@@ -525,31 +555,32 @@
     )
     other = exchange("px", offset, 1)
     own = call(
-        functools.partial(project_half_kernel, False),
+        project_kernel,
         shape((8, comps)),
-        (offset, in_vmem(basis)),
+        (offset, in_vmem(basis[0])),
         flops=gauss_flops,
         name="project_own",
     )
     copies = call(
         project_rest_kernel,
         shape((8, comps)),
-        (other, own, in_vmem(basis)),
+        (other, own, in_vmem(theirs)),
         flops=gauss_flops,
         name="project_rest",
     )
-    parts = sum_rows(copies)
-    def quarter(which, parts):
-        other = back(1, ("theirs", which), parts, values, sigma, basis)
-        other = exchange("px", other, 1)
-        return back(1, ("mine", which), parts, values, sigma, basis), other
-
-    given, parts = lax.optimization_barrier((sum(quarter("give", parts)), parts))
+    parts, _ = sum_rows(copies)
+    sent = exchange("px", back(1, "whole", parts, values, sigma, theirs, "theirs"), 1)
+    given = call(
+        give_kernel,
+        shape((8, pixels // 4)),
+        (back(1, "give", parts, values, sigma, mine, "give"), sent),
+        name="give",
+    )
     given = exchange("px", given, 2)
     piece = call(
         second_update_kernel,
         shape((8, pixels // 4)),
-        (*quarter("keep", parts), given, offset, mean, sigma),
+        (back(1, "keep", parts, values, sigma, mine, "keep"), sent, given, offset, mean, sigma),
         name="second_update",
     )
     state, products = read_slices(piece, norms, slab)

time: 148 us -> 145 us (0.980)
  waiting for transfers between devices: 46.1 us -> 43.2 us
    ppermute x45 -> x44, waiting for transfers between devices: 45.7 us -> 42.8 us  [exchange(): lax.ppermute(x, axis, [(i, i ^ flip) for i in range(lax.axis_size(axis))])]
    pallas_call x37 -> x39, Pallas kernels: 40.6 us -> 41.9 us  [call(): pl.pallas_call(kernel, in_specs=in_specs or [vmem()] * len(args), out_spe...]
    ppermute x45 -> x44, starting transfers between devices: 51.2 us -> 50 us  [exchange(): lax.ppermute(x, axis, [(i, i ^ flip) for i in range(lax.axis_size(axis))])]
  transfers between devices with their start and end apart: 49 -> 48, of which waited for: 32 -> 32; matrix products, arithmetic and copies ran while one was open for 0% -> 0% of each run, Pallas kernels for 15% -> 17%
where the time goes in v7:
time: 145 us
  starting transfers between devices  59.3 us (41%)
  waiting for transfers between devices  43.2 us (30%)
  Pallas kernels  41.9 us (29%)
    ppermute x44, starting transfers between devices, exchange(): lax.ppermute(x, axis, [(i, i ^ flip) for i in range(lax.axis_size(axis))])  50 us
    ppermute x44, waiting for transfers between devices, exchange(): lax.ppermute(x, axis, [(i, i ^ flip) for i in range(lax.axis_size(axis))])  42.8 us
    pallas_call x39, Pallas kernels, call(): pl.pallas_call(kernel, in_specs=in_specs or [vmem()] * len(args), out_spe...  41.9 us
    ppermute x4, starting transfers between devices, to_readers(): return lax.ppermute(x, ('rows', 'px'), pairs)  9.27 us
  transfers between devices with their start and end apart: 48, of which 32 were waited for; matrix products, arithmetic and copies ran while one was open for 0% of the time, Pallas kernels for 17%

profile of v7, /device:TPU:0, one launch (start us, length us, event | category | flops | bytes accessed | tf_op | source)
XLA Modules:
  0.0 144.8 jit_solution(9305325311346885880)
XLA Ops:
  0.0 6.3 %load_project.1 = (f32[8,1024]{1,0:T(8,128)S(1)}, f32[8,8192]{1,0:T(8,128)S(1)}, bf16[4096,1024]{1,0:T(8,128)(2,1)S(1)}, bf16[4096,1024]{1,0:T(8,128)(2,1)S(1)},...) custom-call(f32[8,8192]{1,0:T(8,128)} %q_hbm.1, f32[1,8192]{1,0:T(1,128)} %bitcast.52, bf16[8192,1024]{1,0:T(8,128)(2,1)} %e_hbm.1, ...), custom_call_target="tpu_custom_call" | custom-call | flops 134217728 | bytes 16777216 | tf_op jit(solution)/shard_map/load_project/pallas_call | solution.py:42
  6.3 3.1 %collective-permute-start = (f32[8,1024]{1,0:T(8,128)S(1)}, f32[8,1024]{1,0:T(8,128)S(1)}, u32[]{:S(2)}, u32[]{:S(2)}) collective-permute-start(f32[8,1024]{1,0:T(8,128)S(1)} %get-tuple-element.35.anchor), channel_id=1, source_target_pairs={{0,8},{4,12},{8,0},{12,4},{16,24},{20,28},{24,16},{28,20},{1,9},{5... | collective-permute-start | bytes 98312 | tf_op jit(solution)/shard_map/ppermute | solution.py:488
  9.4 2.6 %collective-permute-start.1 = (f32[8,1024]{1,0:T(8,128)S(1)}, f32[8,1024]{1,0:T(8,128)S(1)}, u32[]{:S(2)}, u32[]{:S(2)}) collective-permute-start(f32[8,1024]{1,0:T(8,128)S(1)} %get-tuple-element.35.anchor), channel_id=1, source_target_pairs={{0,16},{4,20},{8,24},{12,28},{16,0},{20,4},{24,8},{28,12},{1,17},{... | collective-permute-start | bytes 98312 | tf_op jit(solution)/shard_map/ppermute | solution.py:488
  12.0 2.4 %turn_theirs.1.half = bf16[1024,4096]{1,0:T(8,128)(2,1)S(1)} custom-call(f32[8,1024]{1,0:T(8,128)S(1)} %get-tuple-element.35.anchor, bf16[4096,1024]{1,0:T(8,128)(2,1)S(1)} %get-tuple-element.36.half), custom_call_target="tpu_custom_call" | custom-call | flops 4194304 | bytes 16777216 | tf_op jit(solution)/shard_map/turn_theirs/pallas_call | solution.py:42
  14.8 2.9 %collective-permute-done.2 = f32[8,1024]{1,0:T(8,128)S(1)} collective-permute-done((f32[8,1024]{1,0:T(8,128)S(1)}, f32[8,1024]{1,0:T(8,128)S(1)}, u32[]{:S(2)}, u32[]{:S(2)}) %collective-permute-start.2) | collective-permute-done | bytes 32800 | tf_op jit(solution)/shard_map/ppermute | solution.py:488
  19.3 2.4 %turn_mine.1.half = bf16[1024,4096]{1,0:T(8,128)(2,1)S(1)} custom-call(f32[8,1024]{1,0:T(8,128)S(1)} %get-tuple-element.35.anchor, bf16[4096,1024]{1,0:T(8,128)(2,1)S(1)} %get-tuple-element.40.half), custom_call_target="tpu_custom_call" | custom-call | flops 4194304 | bytes 16777216 | tf_op jit(solution)/shard_map/turn_mine/pallas_call | solution.py:42
  26.0 4.6 %norms.1.refs_5_ = f32[1,512]{1,0:T(1,128)S(1)} custom-call(bf16[512,16384]{1,0:T(8,128)(2,1)S(1)} %bitcast.26), custom_call_target="tpu_custom_call" | custom-call | flops 16777216 | bytes 16777216 | tf_op jit(solution)/shard_map/norms/pallas_call | solution.py:42
  32.2 2.3 %project_rest.1 = f32[8,1024]{1,0:T(8,128)S(1)} custom-call(f32[8,4096]{1,0:T(8,128)S(1)} %collective-permute-done.6.off, f32[8,1024]{1,0:T(8,128)S(1)} %project_own.1.own, bf16[1024,4096]{1,0:T(8,128)(2,1)S(1)} %turn_theirs.1.half), custom_call_target="tpu_custom_call" | custom-call | flops 67108864 | bytes 16777216 | tf_op jit(solution)/shard_map/project_rest/pallas_call | solution.py:42
  35.7 3.3 %collective-permute-start.9 = (f32[8,1024]{1,0:T(8,128)S(1)}, f32[8,1024]{1,0:T(8,128)S(1)}, u32[]{:S(2)}, u32[]{:S(2)}) collective-permute-start(f32[8,1024]{1,0:T(8,128)S(1)} %project_rest.1), channel_id=1, source_target_pairs={{0,24},{4,28},{8,16},{12,20},{16,8},{20,12},{24,0},{28,4},{1,25},{... | collective-permute-start | bytes 98312 | tf_op jit(solution)/shard_map/ppermute | solution.py:488
  39.5 1.9 %collective-permute-done.9 = f32[8,1024]{1,0:T(8,128)S(1)} collective-permute-done((f32[8,1024]{1,0:T(8,128)S(1)}, f32[8,1024]{1,0:T(8,128)S(1)}, u32[]{:S(2)}, u32[]{:S(2)}) %collective-permute-start.9) | collective-permute-done | bytes 32800 | tf_op jit(solution)/shard_map/ppermute | solution.py:488
  42.9 2.5 %collective-permute-done.10 = f32[8,1024]{1,0:T(8,128)S(1)} collective-permute-done((f32[8,1024]{1,0:T(8,128)S(1)}, f32[8,1024]{1,0:T(8,128)S(1)}, u32[]{:S(2)}, u32[]{:S(2)}) %collective-permute-start.10) | collective-permute-done | bytes 32800 | tf_op jit(solution)/shard_map/ppermute | solution.py:488
  49.9 2.4 %collective-permute-done.12.given = f32[8,2048]{1,0:T(8,128)S(1)} collective-permute-done((f32[8,2048]{1,0:T(8,128)S(1)}, f32[8,2048]{1,0:T(8,128)S(1)}, u32[]{:S(2)}, u32[]{:S(2)}) %collective-permute-start.12) | collective-permute-done | bytes 65568 | tf_op jit(solution)/shard_map/ppermute | solution.py:488
  52.7 3.2 %collective-permute-start.17 = (f32[8,2048]{1,0:T(8,128)S(1)}, f32[8,2048]{1,0:T(8,128)S(1)}, u32[]{:S(2)}, u32[]{:S(2)}) collective-permute-start(f32[8,2048]{1,0:T(8,128)S(1)} %second_update.1), channel_id=1, source_target_pairs={{0,24},{1,16},{2,8},{3,0},{4,28},{5,20},{6,12},{7,4},{8,25},{9,17}... | collective-permute-start | bytes 196616 | tf_op jit(solution)/shard_map/ppermute | solution.py:513
  56.5 5.2 %collective-permute-start.14 = (f32[8,2048]{1,0:T(8,128)S(1)}, f32[8,2048]{1,0:T(8,128)S(1)}, u32[]{:S(2)}, u32[]{:S(2)}) collective-permute-start(f32[8,2048]{1,0:T(8,128)S(1)} %second_update.1), channel_id=1, source_target_pairs={{0,16},{1,24},{2,0},{3,8},{4,20},{5,28},{6,4},{7,12},{8,17},{9,25}... | collective-permute-start | bytes 196616 | tf_op jit(solution)/shard_map/ppermute | solution.py:513
  70.8 2.1 %collective-permute-start.19 = (f32[16,512]{1,0:T(8,128)S(1)}, f32[16,512]{1,0:T(8,128)S(1)}, u32[]{:S(2)}, u32[]{:S(2)}) collective-permute-start(f32[16,512]{1,0:T(8,128)S(1)} %dots_0_3.1.g0), channel_id=1, source_target_pairs={{0,2},{1,3},{2,0},{3,1},{4,6},{5,7},{6,4},{7,5},{8,10},{9,11},{10,... | collective-permute-start | bytes 98312 | tf_op jit(solution)/shard_map/ppermute | solution.py:488
  81.0 2.1 %collective-permute-done.24.theirs = f32[2,8,2176]{2,1,0:T(8,128)S(1)} collective-permute-done((f32[2,8,2176]{2,1,0:T(8,128)S(1)}, f32[2,8,2176]{2,1,0:T(8,128)S(1)}, u32[]{:S(2)}, u32[]{:S(2)}) %collective-permute-start.24) | collective-permute-done | bytes 139296 | tf_op jit(solution)/shard_map/ppermute | solution.py:488
  85.1 1.9 %collective-permute-start.23 = (f32[8,2176]{1,0:T(8,128)S(1)}, f32[8,2176]{1,0:T(8,128)S(1)}, u32[]{:S(2)}, u32[]{:S(2)}) collective-permute-start(f32[8,2176]{1,0:T(8,128)S(1)} %get-tuple-element.52), channel_id=1, source_target_pairs={{0,8},{4,12},{8,0},{12,4},{16,24},{20,28},{24,16},{28,20},{1,9},{5... | collective-permute-start | bytes 208904 | tf_op jit(solution)/shard_map/ppermute | solution.py:488
  87.0 2.2 %collective-permute-done.25.refs_2_ = f32[8,2176]{1,0:T(8,128)S(1)} collective-permute-done((f32[8,2176]{1,0:T(8,128)S(1)}, f32[8,2176]{1,0:T(8,128)S(1)}, u32[]{:S(2)}, u32[]{:S(2)}) %collective-permute-start.25) | collective-permute-done | bytes 69664 | tf_op jit(solution)/shard_map/ppermute | solution.py:488
  89.1 1.9 %collective-permute-done.26.refs_3_ = f32[8,2176]{1,0:T(8,128)S(1)} collective-permute-done((f32[8,2176]{1,0:T(8,128)S(1)}, f32[8,2176]{1,0:T(8,128)S(1)}, u32[]{:S(2)}, u32[]{:S(2)}) %collective-permute-start.26) | collective-permute-done | bytes 69664 | tf_op jit(solution)/shard_map/ppermute | solution.py:488
  95.7 1.9 %collective-permute-done.30.refs_0_ = f32[8,2176]{1,0:T(8,128)S(1)} collective-permute-done((f32[8,2176]{1,0:T(8,128)S(1)}, f32[8,2176]{1,0:T(8,128)S(1)}, u32[]{:S(2)}, u32[]{:S(2)}) %collective-permute-start.30) | collective-permute-done | bytes 69664 | tf_op jit(solution)/shard_map/ppermute | solution.py:488
  108.8 1.8 %collective-permute-done.32.g1 = f32[16,512]{1,0:T(8,128)S(1)} collective-permute-done((f32[16,512]{1,0:T(8,128)S(1)}, f32[16,512]{1,0:T(8,128)S(1)}, u32[]{:S(2)}, u32[]{:S(2)}) %collective-permute-start.32) | collective-permute-done | bytes 32800 | tf_op jit(solution)/shard_map/ppermute | solution.py:488
  116.1 2.5 %collective-permute-done.37.theirs = f32[2,8,2176]{2,1,0:T(8,128)S(1)} collective-permute-done((f32[2,8,2176]{2,1,0:T(8,128)S(1)}, f32[2,8,2176]{2,1,0:T(8,128)S(1)}, u32[]{:S(2)}, u32[]{:S(2)}) %collective-permute-start.37) | collective-permute-done | bytes 139296 | tf_op jit(solution)/shard_map/ppermute | solution.py:488
  131.1 2.0 %collective-permute-done.42.refs_3_ = f32[8,2176]{1,0:T(8,128)S(1)} collective-permute-done((f32[8,2176]{1,0:T(8,128)S(1)}, f32[8,2176]{1,0:T(8,128)S(1)}, u32[]{:S(2)}, u32[]{:S(2)}) %collective-permute-start.42) | collective-permute-done | bytes 69664 | tf_op jit(solution)/shard_map/ppermute | solution.py:488
  135.9 2.3 %collective-permute-done.44.refs_5_ = f32[2,8,2176]{2,1,0:T(8,128)S(1)} collective-permute-done((f32[2,8,2176]{2,1,0:T(8,128)S(1)}, f32[2,8,2176]{2,1,0:T(8,128)S(1)}, u32[]{:S(2)}, u32[]{:S(2)}) %collective-permute-start.44) | collective-permute-done | bytes 139296 | tf_op jit(solution)/shard_map/ppermute | solution.py:488
  (139 shorter events, 78.7 us)
Async XLA Ops:
  6.3 8.1 %collective-permute-start = (f32[8,1024]{1,0:T(8,128)S(1)}, f32[8,1024]{1,0:T(8,128)S(1)}, u32[]{:S(2)}, u32[]{:S(2)}) collective-permute-start(f32[8,1024]{1,0:T(8,128)S(1)} %get-tuple-element.35.anchor), channel_id=1, source_target_pairs={{0,8},{4,12},{8,0},{12,4},{16,24},{20,28},{24,16},{28,20},{1,9},{5... | collective-permute-start | bytes 98312 | tf_op jit(solution)/shard_map/ppermute | solution.py:488
  12.0 5.7 %collective-permute-start.2 = (f32[8,1024]{1,0:T(8,128)S(1)}, f32[8,1024]{1,0:T(8,128)S(1)}, u32[]{:S(2)}, u32[]{:S(2)}) collective-permute-start(f32[8,1024]{1,0:T(8,128)S(1)} %get-tuple-element.35.anchor), channel_id=1, source_target_pairs={{0,24},{4,28},{8,16},{12,20},{16,8},{20,12},{24,0},{28,4},{1,25},{... | collective-permute-start | bytes 98312 | tf_op jit(solution)/shard_map/ppermute | solution.py:488
  24.4 6.2 %collective-permute-start.5 = (f32[8,4096]{1,0:T(8,128)S(1)}, f32[8,4096]{1,0:T(8,128)S(1)}, u32[]{:S(2)}, u32[]{:S(2)}) collective-permute-start(f32[8,4096]{1,0:T(8,128)S(1)} %add.24.mine), channel_id=1, source_target_pairs={{0,2},{1,3},{2,0},{3,1},{4,6},{5,7},{6,4},{7,5},{8,10},{9,11},{10,... | collective-permute-start | bytes 393224 | tf_op jit(solution)/shard_map/ppermute | solution.py:488
  35.7 5.7 %collective-permute-start.9 = (f32[8,1024]{1,0:T(8,128)S(1)}, f32[8,1024]{1,0:T(8,128)S(1)}, u32[]{:S(2)}, u32[]{:S(2)}) collective-permute-start(f32[8,1024]{1,0:T(8,128)S(1)} %project_rest.1), channel_id=1, source_target_pairs={{0,24},{4,28},{8,16},{12,20},{16,8},{20,12},{24,0},{28,4},{1,25},{... | collective-permute-start | bytes 98312 | tf_op jit(solution)/shard_map/ppermute | solution.py:488
  52.5 9.3 %collective-permute-start.16 = (f32[8,2048]{1,0:T(8,128)S(1)}, f32[8,2048]{1,0:T(8,128)S(1)}, u32[]{:S(2)}, u32[]{:S(2)}) collective-permute-start(f32[8,2048]{1,0:T(8,128)S(1)} %second_update.1), channel_id=1, source_target_pairs={{0,8},{1,0},{2,24},{3,16},{4,12},{5,4},{6,28},{7,20},{8,9},{9,1},{... | collective-permute-start | bytes 196616 | tf_op jit(solution)/shard_map/ppermute | solution.py:513
  52.7 9.1 %collective-permute-start.17 = (f32[8,2048]{1,0:T(8,128)S(1)}, f32[8,2048]{1,0:T(8,128)S(1)}, u32[]{:S(2)}, u32[]{:S(2)}) collective-permute-start(f32[8,2048]{1,0:T(8,128)S(1)} %second_update.1), channel_id=1, source_target_pairs={{0,24},{1,16},{2,8},{3,0},{4,28},{5,20},{6,12},{7,4},{8,25},{9,17}... | collective-permute-start | bytes 196616 | tf_op jit(solution)/shard_map/ppermute | solution.py:513
  55.9 7.4 %collective-permute-start.13 = (f32[8,2048]{1,0:T(8,128)S(1)}, f32[8,2048]{1,0:T(8,128)S(1)}, u32[]{:S(2)}, u32[]{:S(2)}) collective-permute-start(f32[8,2048]{1,0:T(8,128)S(1)} %second_update.1), channel_id=1, source_target_pairs={{0,0},{1,8},{2,16},{3,24},{4,4},{5,12},{6,20},{7,28},{8,1},{9,9},{... | collective-permute-start | bytes 196616 | tf_op jit(solution)/shard_map/ppermute | solution.py:513
  56.5 7.1 %collective-permute-start.14 = (f32[8,2048]{1,0:T(8,128)S(1)}, f32[8,2048]{1,0:T(8,128)S(1)}, u32[]{:S(2)}, u32[]{:S(2)}) collective-permute-start(f32[8,2048]{1,0:T(8,128)S(1)} %second_update.1), channel_id=1, source_target_pairs={{0,16},{1,24},{2,0},{3,8},{4,20},{5,28},{6,4},{7,12},{8,17},{9,25}... | collective-permute-start | bytes 196616 | tf_op jit(solution)/shard_map/ppermute | solution.py:513
  61.8 6.2 %collective-permute-start.18 = (f32[2,8,2048]{2,1,0:T(8,128)S(1)}, f32[2,8,2048]{2,1,0:T(8,128)S(1)}, u32[]{:S(2)}, u32[]{:S(2)}) collective-permute-start(f32[2,8,2048]{2,1,0:T(8,128)S(1)} %pad_maximum_fusion.5), channel_id=1, source_target_pairs={{0,4},{4,0},{8,12},{12,8},{16,20},{20,16},{24,28},{28,24},{1,5},{5... | collective-permute-start | bytes 393224 | tf_op jit(solution)/shard_map/ppermute | solution.py:488
  63.7 5.9 %collective-permute-start.15 = (f32[2,8,2048]{2,1,0:T(8,128)S(1)}, f32[2,8,2048]{2,1,0:T(8,128)S(1)}, u32[]{:S(2)}, u32[]{:S(2)}) collective-permute-start(f32[2,8,2048]{2,1,0:T(8,128)S(1)} %pad_maximum_fusion.4), channel_id=1, source_target_pairs={{0,4},{4,0},{8,12},{12,8},{16,20},{20,16},{24,28},{28,24},{1,5},{5... | collective-permute-start | bytes 393224 | tf_op jit(solution)/shard_map/ppermute | solution.py:488
  77.0 6.1 %collective-permute-start.24 = (f32[2,8,2176]{2,1,0:T(8,128)S(1)}, f32[2,8,2176]{2,1,0:T(8,128)S(1)}, u32[]{:S(2)}, u32[]{:S(2)}) collective-permute-start(f32[2,8,2176]{2,1,0:T(8,128)S(1)} %get-tuple-element.53), channel_id=1, source_target_pairs={{0,4},{4,0},{8,12},{12,8},{16,20},{20,16},{24,28},{28,24},{1,5},{5... | collective-permute-start | bytes 417800 | tf_op jit(solution)/shard_map/ppermute | solution.py:488
  79.1 5.9 %collective-permute-start.22 = (f32[2,8,2176]{2,1,0:T(8,128)S(1)}, f32[2,8,2176]{2,1,0:T(8,128)S(1)}, u32[]{:S(2)}, u32[]{:S(2)}) collective-permute-start(f32[2,8,2176]{2,1,0:T(8,128)S(1)} %near_across_0.1), channel_id=1, source_target_pairs={{0,4},{4,0},{8,12},{12,8},{16,20},{20,16},{24,28},{28,24},{1,5},{5... | collective-permute-start | bytes 417800 | tf_op jit(solution)/shard_map/ppermute | solution.py:488
  83.3 5.8 %collective-permute-start.25 = (f32[8,2176]{1,0:T(8,128)S(1)}, f32[8,2176]{1,0:T(8,128)S(1)}, u32[]{:S(2)}, u32[]{:S(2)}) collective-permute-start(f32[8,2176]{1,0:T(8,128)S(1)} %get-tuple-element.54), channel_id=1, source_target_pairs={{0,16},{4,20},{8,24},{12,28},{16,0},{20,4},{24,8},{28,12},{1,17},{... | collective-permute-start | bytes 208904 | tf_op jit(solution)/shard_map/ppermute | solution.py:488
  84.9 6.1 %collective-permute-start.26 = (f32[8,2176]{1,0:T(8,128)S(1)}, f32[8,2176]{1,0:T(8,128)S(1)}, u32[]{:S(2)}, u32[]{:S(2)}) collective-permute-start(f32[8,2176]{1,0:T(8,128)S(1)} %get-tuple-element.55), channel_id=1, source_target_pairs={{0,24},{4,28},{8,16},{12,20},{16,8},{20,12},{24,0},{28,4},{1,25},{... | collective-permute-start | bytes 208904 | tf_op jit(solution)/shard_map/ppermute | solution.py:488
  85.1 6.0 %collective-permute-start.23 = (f32[8,2176]{1,0:T(8,128)S(1)}, f32[8,2176]{1,0:T(8,128)S(1)}, u32[]{:S(2)}, u32[]{:S(2)}) collective-permute-start(f32[8,2176]{1,0:T(8,128)S(1)} %get-tuple-element.52), channel_id=1, source_target_pairs={{0,8},{4,12},{8,0},{12,4},{16,24},{20,28},{24,16},{28,20},{1,9},{5... | collective-permute-start | bytes 208904 | tf_op jit(solution)/shard_map/ppermute | solution.py:488
  91.3 6.3 %collective-permute-start.30 = (f32[8,2176]{1,0:T(8,128)S(1)}, f32[8,2176]{1,0:T(8,128)S(1)}, u32[]{:S(2)}, u32[]{:S(2)}) collective-permute-start(f32[8,2176]{1,0:T(8,128)S(1)} %combine_0.1.refs_0_.refs_4_), channel_id=1, source_target_pairs={{0,16},{4,20},{8,24},{12,28},{16,0},{20,4},{24,8},{28,12},{1,17},{... | collective-permute-start | bytes 208904 | tf_op jit(solution)/shard_map/ppermute | solution.py:488
  92.6 6.3 %collective-permute-start.27 = (f32[8,2176]{1,0:T(8,128)S(1)}, f32[8,2176]{1,0:T(8,128)S(1)}, u32[]{:S(2)}, u32[]{:S(2)}) collective-permute-start(f32[8,2176]{1,0:T(8,128)S(1)} %combine_0.1.refs_0_.refs_4_), channel_id=1, source_target_pairs={{0,8},{4,12},{8,0},{12,4},{16,24},{20,28},{24,16},{28,20},{1,9},{5... | collective-permute-start | bytes 208904 | tf_op jit(solution)/shard_map/ppermute | solution.py:488
  94.1 6.1 %collective-permute-start.28 = (f32[8,2176]{1,0:T(8,128)S(1)}, f32[8,2176]{1,0:T(8,128)S(1)}, u32[]{:S(2)}, u32[]{:S(2)}) collective-permute-start(f32[8,2176]{1,0:T(8,128)S(1)} %combine_0.1.refs_0_.refs_4_), channel_id=1, source_target_pairs={{0,24},{4,28},{8,16},{12,20},{16,8},{20,12},{24,0},{28,4},{1,25},{... | collective-permute-start | bytes 208904 | tf_op jit(solution)/shard_map/ppermute | solution.py:488
  97.6 6.6 %collective-permute-start.31 = (f32[2,8,2176]{2,1,0:T(8,128)S(1)}, f32[2,8,2176]{2,1,0:T(8,128)S(1)}, u32[]{:S(2)}, u32[]{:S(2)}) collective-permute-start(f32[2,8,2176]{2,1,0:T(8,128)S(1)} %pad_maximum_fusion.1), channel_id=1, source_target_pairs={{0,4},{4,0},{8,12},{12,8},{16,20},{20,16},{24,28},{28,24},{1,5},{5... | collective-permute-start | bytes 417800 | tf_op jit(solution)/shard_map/ppermute | solution.py:488
  112.1 6.5 %collective-permute-start.37 = (f32[2,8,2176]{2,1,0:T(8,128)S(1)}, f32[2,8,2176]{2,1,0:T(8,128)S(1)}, u32[]{:S(2)}, u32[]{:S(2)}) collective-permute-start(f32[2,8,2176]{2,1,0:T(8,128)S(1)} %get-tuple-element.61), channel_id=1, source_target_pairs={{0,4},{4,0},{8,12},{12,8},{16,20},{20,16},{24,28},{28,24},{1,5},{5... | collective-permute-start | bytes 417800 | tf_op jit(solution)/shard_map/ppermute | solution.py:488
  114.0 6.7 %collective-permute-start.35 = (f32[2,8,2176]{2,1,0:T(8,128)S(1)}, f32[2,8,2176]{2,1,0:T(8,128)S(1)}, u32[]{:S(2)}, u32[]{:S(2)}) collective-permute-start(f32[2,8,2176]{2,1,0:T(8,128)S(1)} %near_across_1.1), channel_id=1, source_target_pairs={{0,4},{4,0},{8,12},{12,8},{16,20},{20,16},{24,28},{28,24},{1,5},{5... | collective-permute-start | bytes 417800 | tf_op jit(solution)/shard_map/ppermute | solution.py:488
  118.8 6.4 %collective-permute-start.39 = (f32[8,2176]{1,0:T(8,128)S(1)}, f32[8,2176]{1,0:T(8,128)S(1)}, u32[]{:S(2)}, u32[]{:S(2)}) collective-permute-start(f32[8,2176]{1,0:T(8,128)S(1)} %get-tuple-element.63), channel_id=1, source_target_pairs={{0,24},{4,28},{8,16},{12,20},{16,8},{20,12},{24,0},{28,4},{1,25},{... | collective-permute-start | bytes 208904 | tf_op jit(solution)/shard_map/ppermute | solution.py:488
  127.0 6.1 %collective-permute-start.42 = (f32[8,2176]{1,0:T(8,128)S(1)}, f32[8,2176]{1,0:T(8,128)S(1)}, u32[]{:S(2)}, u32[]{:S(2)}) collective-permute-start(f32[8,2176]{1,0:T(8,128)S(1)} %combine_1.1.refs_0_), channel_id=1, source_target_pairs={{0,24},{4,28},{8,16},{12,20},{16,8},{20,12},{24,0},{28,4},{1,25},{... | collective-permute-start | bytes 208904 | tf_op jit(solution)/shard_map/ppermute | solution.py:488
  128.6 6.0 %collective-permute-start.41 = (f32[8,2176]{1,0:T(8,128)S(1)}, f32[8,2176]{1,0:T(8,128)S(1)}, u32[]{:S(2)}, u32[]{:S(2)}) collective-permute-start(f32[8,2176]{1,0:T(8,128)S(1)} %combine_1.1.refs_0_), channel_id=1, source_target_pairs={{0,16},{4,20},{8,24},{12,28},{16,0},{20,4},{24,8},{28,12},{1,17},{... | collective-permute-start | bytes 208904 | tf_op jit(solution)/shard_map/ppermute | solution.py:488
  (31 other events, 130.6 us)

commit v8 on v7

--- a/solution.py
+++ b/solution.py
@@ -490,7 +490,7 @@
 
 def sum_rows(x, beside=()):
     rows = lax.axis_size("rows")
-    parts = [exchange("rows", x, k) for k in range(2, rows, 2)]
+    parts = [exchange("rows", x, k) for k in range(rows - 2, 0, -2)]
     done = [work(x) for work in beside]
     if done:
         parts, done[0] = lax.optimization_barrier((parts, done[0]))

time: 145 us -> 143 us (0.986)
    ppermute x44, waiting for transfers between devices: 42.8 us -> 41.4 us  [exchange(): lax.ppermute(x, axis, [(i, i ^ flip) for i in range(lax.axis_size(axis))])]
  transfers between devices with their start and end apart: 48 -> 48, of which waited for: 32 -> 30; matrix products, arithmetic and copies ran while one was open for 0% -> 0% of each run, Pallas kernels for 17% -> 18%
where the time goes in v8:
time: 143 us
  starting transfers between devices  58.3 us (41%)
  Pallas kernels  41.9 us (29%)
  waiting for transfers between devices  41.9 us (29%)
    ppermute x44, starting transfers between devices, exchange(): lax.ppermute(x, axis, [(i, i ^ flip) for i in range(lax.axis_size(axis))])  50.2 us
    pallas_call x39, Pallas kernels, call(): pl.pallas_call(kernel, in_specs=in_specs or [vmem()] * len(args), out_spe...  41.9 us
    ppermute x44, waiting for transfers between devices, exchange(): lax.ppermute(x, axis, [(i, i ^ flip) for i in range(lax.axis_size(axis))])  41.4 us
    ppermute x4, starting transfers between devices, to_readers(): return lax.ppermute(x, ('rows', 'px'), pairs)  8.11 us
  transfers between devices with their start and end apart: 48, of which 30 were waited for; matrix products, arithmetic and copies ran while one was open for 0% of the time, Pallas kernels for 18%

profile of v8, /device:TPU:0, one launch (start us, length us, event | category | flops | bytes accessed | tf_op | source)
XLA Modules:
  0.0 142.6 jit_solution(8594073410353595811)
XLA Ops:
  0.0 6.3 %load_project.1 = (f32[8,1024]{1,0:T(8,128)S(1)}, f32[8,8192]{1,0:T(8,128)S(1)}, bf16[4096,1024]{1,0:T(8,128)(2,1)S(1)}, bf16[4096,1024]{1,0:T(8,128)(2,1)S(1)},...) custom-call(f32[8,8192]{1,0:T(8,128)} %q_hbm.1, f32[1,8192]{1,0:T(1,128)} %bitcast.52, bf16[8192,1024]{1,0:T(8,128)(2,1)} %e_hbm.1, ...), custom_call_target="tpu_custom_call" | custom-call | flops 134217728 | bytes 16777216 | tf_op jit(solution)/shard_map/load_project/pallas_call | solution.py:42
  6.3 5.1 %collective-permute-start = (f32[8,1024]{1,0:T(8,128)S(1)}, f32[8,1024]{1,0:T(8,128)S(1)}, u32[]{:S(2)}, u32[]{:S(2)}) collective-permute-start(f32[8,1024]{1,0:T(8,128)S(1)} %get-tuple-element.35.anchor), channel_id=1, source_target_pairs={{0,24},{4,28},{8,16},{12,20},{16,8},{20,12},{24,0},{28,4},{1,25},{... | collective-permute-start | bytes 98312 | tf_op jit(solution)/shard_map/ppermute | solution.py:488
  12.1 2.4 %turn_theirs.1.half = bf16[1024,4096]{1,0:T(8,128)(2,1)S(1)} custom-call(f32[8,1024]{1,0:T(8,128)S(1)} %get-tuple-element.35.anchor, bf16[4096,1024]{1,0:T(8,128)(2,1)S(1)} %get-tuple-element.36.half), custom_call_target="tpu_custom_call" | custom-call | flops 4194304 | bytes 16777216 | tf_op jit(solution)/shard_map/turn_theirs/pallas_call | solution.py:42
  14.5 1.8 %collective-permute-done.1 = f32[8,1024]{1,0:T(8,128)S(1)} collective-permute-done((f32[8,1024]{1,0:T(8,128)S(1)}, f32[8,1024]{1,0:T(8,128)S(1)}, u32[]{:S(2)}, u32[]{:S(2)}) %collective-permute-start.1) | collective-permute-done | bytes 32800 | tf_op jit(solution)/shard_map/ppermute | solution.py:488
  17.9 2.4 %turn_mine.1.half = bf16[1024,4096]{1,0:T(8,128)(2,1)S(1)} custom-call(f32[8,1024]{1,0:T(8,128)S(1)} %get-tuple-element.35.anchor, bf16[4096,1024]{1,0:T(8,128)(2,1)S(1)} %get-tuple-element.40.half), custom_call_target="tpu_custom_call" | custom-call | flops 4194304 | bytes 16777216 | tf_op jit(solution)/shard_map/turn_mine/pallas_call | solution.py:42
  24.6 4.6 %norms.1.refs_5_ = f32[1,512]{1,0:T(1,128)S(1)} custom-call(bf16[512,16384]{1,0:T(8,128)(2,1)S(1)} %bitcast.26), custom_call_target="tpu_custom_call" | custom-call | flops 16777216 | bytes 16777216 | tf_op jit(solution)/shard_map/norms/pallas_call | solution.py:42
  30.8 2.3 %project_rest.1 = f32[8,1024]{1,0:T(8,128)S(1)} custom-call(f32[8,4096]{1,0:T(8,128)S(1)} %collective-permute-done.6.off, f32[8,1024]{1,0:T(8,128)S(1)} %project_own.1.own, bf16[1024,4096]{1,0:T(8,128)(2,1)S(1)} %turn_theirs.1.half), custom_call_target="tpu_custom_call" | custom-call | flops 67108864 | bytes 16777216 | tf_op jit(solution)/shard_map/project_rest/pallas_call | solution.py:42
  33.1 2.0 %collective-permute-start.7 = (f32[8,1024]{1,0:T(8,128)S(1)}, f32[8,1024]{1,0:T(8,128)S(1)}, u32[]{:S(2)}, u32[]{:S(2)}) collective-permute-start(f32[8,1024]{1,0:T(8,128)S(1)} %project_rest.1), channel_id=1, source_target_pairs={{0,24},{4,28},{8,16},{12,20},{16,8},{20,12},{24,0},{28,4},{1,25},{... | collective-permute-start | bytes 98312 | tf_op jit(solution)/shard_map/ppermute | solution.py:488
  35.2 2.3 %collective-permute-start.9 = (f32[8,1024]{1,0:T(8,128)S(1)}, f32[8,1024]{1,0:T(8,128)S(1)}, u32[]{:S(2)}, u32[]{:S(2)}) collective-permute-start(f32[8,1024]{1,0:T(8,128)S(1)} %project_rest.1), channel_id=1, source_target_pairs={{0,8},{4,12},{8,0},{12,4},{16,24},{20,28},{24,16},{28,20},{1,9},{5... | collective-permute-start | bytes 98312 | tf_op jit(solution)/shard_map/ppermute | solution.py:488
  41.8 2.5 %collective-permute-done.10 = f32[8,1024]{1,0:T(8,128)S(1)} collective-permute-done((f32[8,1024]{1,0:T(8,128)S(1)}, f32[8,1024]{1,0:T(8,128)S(1)}, u32[]{:S(2)}, u32[]{:S(2)}) %collective-permute-start.10) | collective-permute-done | bytes 32800 | tf_op jit(solution)/shard_map/ppermute | solution.py:488
  48.8 2.4 %collective-permute-done.12.given = f32[8,2048]{1,0:T(8,128)S(1)} collective-permute-done((f32[8,2048]{1,0:T(8,128)S(1)}, f32[8,2048]{1,0:T(8,128)S(1)}, u32[]{:S(2)}, u32[]{:S(2)}) %collective-permute-start.12) | collective-permute-done | bytes 65568 | tf_op jit(solution)/shard_map/ppermute | solution.py:488
  54.8 4.7 %collective-permute-start.14 = (f32[8,2048]{1,0:T(8,128)S(1)}, f32[8,2048]{1,0:T(8,128)S(1)}, u32[]{:S(2)}, u32[]{:S(2)}) collective-permute-start(f32[8,2048]{1,0:T(8,128)S(1)} %second_update.1), channel_id=1, source_target_pairs={{0,16},{1,24},{2,0},{3,8},{4,20},{5,28},{6,4},{7,12},{8,17},{9,25}... | collective-permute-start | bytes 196616 | tf_op jit(solution)/shard_map/ppermute | solution.py:513
  71.4 1.8 %collective-permute-done.19.g1 = f32[16,512]{1,0:T(8,128)S(1)} collective-permute-done((f32[16,512]{1,0:T(8,128)S(1)}, f32[16,512]{1,0:T(8,128)S(1)}, u32[]{:S(2)}, u32[]{:S(2)}) %collective-permute-start.19) | collective-permute-done | bytes 32800 | tf_op jit(solution)/shard_map/ppermute | solution.py:488
  79.0 2.4 %collective-permute-done.24.theirs = f32[2,8,2176]{2,1,0:T(8,128)S(1)} collective-permute-done((f32[2,8,2176]{2,1,0:T(8,128)S(1)}, f32[2,8,2176]{2,1,0:T(8,128)S(1)}, u32[]{:S(2)}, u32[]{:S(2)}) %collective-permute-start.24) | collective-permute-done | bytes 139296 | tf_op jit(solution)/shard_map/ppermute | solution.py:488
  85.2 2.4 %collective-permute-done.25.refs_2_ = f32[8,2176]{1,0:T(8,128)S(1)} collective-permute-done((f32[8,2176]{1,0:T(8,128)S(1)}, f32[8,2176]{1,0:T(8,128)S(1)}, u32[]{:S(2)}, u32[]{:S(2)}) %collective-permute-start.25) | collective-permute-done | bytes 69664 | tf_op jit(solution)/shard_map/ppermute | solution.py:488
  92.2 1.6 %collective-permute-start.28 = (f32[8,2176]{1,0:T(8,128)S(1)}, f32[8,2176]{1,0:T(8,128)S(1)}, u32[]{:S(2)}, u32[]{:S(2)}) collective-permute-start(f32[8,2176]{1,0:T(8,128)S(1)} %combine_0.1.refs_0_.refs_4_), channel_id=1, source_target_pairs={{0,24},{4,28},{8,16},{12,20},{16,8},{20,12},{24,0},{28,4},{1,25},{... | collective-permute-start | bytes 208904 | tf_op jit(solution)/shard_map/ppermute | solution.py:488
  93.8 2.6 %collective-permute-done.30.refs_0_ = f32[8,2176]{1,0:T(8,128)S(1)} collective-permute-done((f32[8,2176]{1,0:T(8,128)S(1)}, f32[8,2176]{1,0:T(8,128)S(1)}, u32[]{:S(2)}, u32[]{:S(2)}) %collective-permute-start.30) | collective-permute-done | bytes 69664 | tf_op jit(solution)/shard_map/ppermute | solution.py:488
  106.8 1.9 %collective-permute-done.32.g1 = f32[16,512]{1,0:T(8,128)S(1)} collective-permute-done((f32[16,512]{1,0:T(8,128)S(1)}, f32[16,512]{1,0:T(8,128)S(1)}, u32[]{:S(2)}, u32[]{:S(2)}) %collective-permute-start.32) | collective-permute-done | bytes 32800 | tf_op jit(solution)/shard_map/ppermute | solution.py:488
  114.0 2.5 %collective-permute-done.37.theirs = f32[2,8,2176]{2,1,0:T(8,128)S(1)} collective-permute-done((f32[2,8,2176]{2,1,0:T(8,128)S(1)}, f32[2,8,2176]{2,1,0:T(8,128)S(1)}, u32[]{:S(2)}, u32[]{:S(2)}) %collective-permute-start.37) | collective-permute-done | bytes 139296 | tf_op jit(solution)/shard_map/ppermute | solution.py:488
  116.7 2.1 %collective-permute-start.39 = (f32[8,2176]{1,0:T(8,128)S(1)}, f32[8,2176]{1,0:T(8,128)S(1)}, u32[]{:S(2)}, u32[]{:S(2)}) collective-permute-start(f32[8,2176]{1,0:T(8,128)S(1)} %get-tuple-element.63), channel_id=1, source_target_pairs={{0,24},{4,28},{8,16},{12,20},{16,8},{20,12},{24,0},{28,4},{1,25},{... | collective-permute-start | bytes 208904 | tf_op jit(solution)/shard_map/ppermute | solution.py:488
  120.3 2.9 %collective-permute-done.38.refs_2_ = f32[8,2176]{1,0:T(8,128)S(1)} collective-permute-done((f32[8,2176]{1,0:T(8,128)S(1)}, f32[8,2176]{1,0:T(8,128)S(1)}, u32[]{:S(2)}, u32[]{:S(2)}) %collective-permute-start.38) | collective-permute-done | bytes 69664 | tf_op jit(solution)/shard_map/ppermute | solution.py:488
  124.9 1.7 %collective-permute-start.42 = (f32[8,2176]{1,0:T(8,128)S(1)}, f32[8,2176]{1,0:T(8,128)S(1)}, u32[]{:S(2)}, u32[]{:S(2)}) collective-permute-start(f32[8,2176]{1,0:T(8,128)S(1)} %combine_1.1.refs_0_), channel_id=1, source_target_pairs={{0,24},{4,28},{8,16},{12,20},{16,8},{20,12},{24,0},{28,4},{1,25},{... | collective-permute-start | bytes 208904 | tf_op jit(solution)/shard_map/ppermute | solution.py:488
  129.2 1.8 %collective-permute-done.42.refs_3_ = f32[8,2176]{1,0:T(8,128)S(1)} collective-permute-done((f32[8,2176]{1,0:T(8,128)S(1)}, f32[8,2176]{1,0:T(8,128)S(1)}, u32[]{:S(2)}, u32[]{:S(2)}) %collective-permute-start.42) | collective-permute-done | bytes 69664 | tf_op jit(solution)/shard_map/ppermute | solution.py:488
  133.9 2.2 %collective-permute-done.44.refs_5_ = f32[2,8,2176]{2,1,0:T(8,128)S(1)} collective-permute-done((f32[2,8,2176]{2,1,0:T(8,128)S(1)}, f32[2,8,2176]{2,1,0:T(8,128)S(1)}, u32[]{:S(2)}, u32[]{:S(2)}) %collective-permute-start.44) | collective-permute-done | bytes 139296 | tf_op jit(solution)/shard_map/ppermute | solution.py:488
  (139 shorter events, 77.5 us)
Async XLA Ops:
  6.3 8.2 %collective-permute-start = (f32[8,1024]{1,0:T(8,128)S(1)}, f32[8,1024]{1,0:T(8,128)S(1)}, u32[]{:S(2)}, u32[]{:S(2)}) collective-permute-start(f32[8,1024]{1,0:T(8,128)S(1)} %get-tuple-element.35.anchor), channel_id=1, source_target_pairs={{0,24},{4,28},{8,16},{12,20},{16,8},{20,12},{24,0},{28,4},{1,25},{... | collective-permute-start | bytes 98312 | tf_op jit(solution)/shard_map/ppermute | solution.py:488
  23.0 6.2 %collective-permute-start.5 = (f32[8,4096]{1,0:T(8,128)S(1)}, f32[8,4096]{1,0:T(8,128)S(1)}, u32[]{:S(2)}, u32[]{:S(2)}) collective-permute-start(f32[8,4096]{1,0:T(8,128)S(1)} %add.24.mine), channel_id=1, source_target_pairs={{0,2},{1,3},{2,0},{3,1},{4,6},{5,7},{6,4},{7,5},{8,10},{9,11},{10,... | collective-permute-start | bytes 393224 | tf_op jit(solution)/shard_map/ppermute | solution.py:488
  33.1 5.9 %collective-permute-start.7 = (f32[8,1024]{1,0:T(8,128)S(1)}, f32[8,1024]{1,0:T(8,128)S(1)}, u32[]{:S(2)}, u32[]{:S(2)}) collective-permute-start(f32[8,1024]{1,0:T(8,128)S(1)} %project_rest.1), channel_id=1, source_target_pairs={{0,24},{4,28},{8,16},{12,20},{16,8},{20,12},{24,0},{28,4},{1,25},{... | collective-permute-start | bytes 98312 | tf_op jit(solution)/shard_map/ppermute | solution.py:488
  35.1 5.2 %collective-permute-start.8 = (f32[8,1024]{1,0:T(8,128)S(1)}, f32[8,1024]{1,0:T(8,128)S(1)}, u32[]{:S(2)}, u32[]{:S(2)}) collective-permute-start(f32[8,1024]{1,0:T(8,128)S(1)} %project_rest.1), channel_id=1, source_target_pairs={{0,16},{4,20},{8,24},{12,28},{16,0},{20,4},{24,8},{28,12},{1,17},{... | collective-permute-start | bytes 98312 | tf_op jit(solution)/shard_map/ppermute | solution.py:488
  51.4 8.1 %collective-permute-start.16 = (f32[8,2048]{1,0:T(8,128)S(1)}, f32[8,2048]{1,0:T(8,128)S(1)}, u32[]{:S(2)}, u32[]{:S(2)}) collective-permute-start(f32[8,2048]{1,0:T(8,128)S(1)} %second_update.1), channel_id=1, source_target_pairs={{0,8},{1,0},{2,24},{3,16},{4,12},{5,4},{6,28},{7,20},{8,9},{9,1},{... | collective-permute-start | bytes 196616 | tf_op jit(solution)/shard_map/ppermute | solution.py:513
  52.5 7.0 %collective-permute-start.17 = (f32[8,2048]{1,0:T(8,128)S(1)}, f32[8,2048]{1,0:T(8,128)S(1)}, u32[]{:S(2)}, u32[]{:S(2)}) collective-permute-start(f32[8,2048]{1,0:T(8,128)S(1)} %second_update.1), channel_id=1, source_target_pairs={{0,24},{1,16},{2,8},{3,0},{4,28},{5,20},{6,12},{7,4},{8,25},{9,17}... | collective-permute-start | bytes 196616 | tf_op jit(solution)/shard_map/ppermute | solution.py:513
  54.1 6.9 %collective-permute-start.13 = (f32[8,2048]{1,0:T(8,128)S(1)}, f32[8,2048]{1,0:T(8,128)S(1)}, u32[]{:S(2)}, u32[]{:S(2)}) collective-permute-start(f32[8,2048]{1,0:T(8,128)S(1)} %second_update.1), channel_id=1, source_target_pairs={{0,0},{1,8},{2,16},{3,24},{4,4},{5,12},{6,20},{7,28},{8,1},{9,9},{... | collective-permute-start | bytes 196616 | tf_op jit(solution)/shard_map/ppermute | solution.py:513
  54.8 6.8 %collective-permute-start.14 = (f32[8,2048]{1,0:T(8,128)S(1)}, f32[8,2048]{1,0:T(8,128)S(1)}, u32[]{:S(2)}, u32[]{:S(2)}) collective-permute-start(f32[8,2048]{1,0:T(8,128)S(1)} %second_update.1), channel_id=1, source_target_pairs={{0,16},{1,24},{2,0},{3,8},{4,20},{5,28},{6,4},{7,12},{8,17},{9,25}... | collective-permute-start | bytes 196616 | tf_op jit(solution)/shard_map/ppermute | solution.py:513
  59.5 6.4 %collective-permute-start.18 = (f32[2,8,2048]{2,1,0:T(8,128)S(1)}, f32[2,8,2048]{2,1,0:T(8,128)S(1)}, u32[]{:S(2)}, u32[]{:S(2)}) collective-permute-start(f32[2,8,2048]{2,1,0:T(8,128)S(1)} %pad_maximum_fusion.5), channel_id=1, source_target_pairs={{0,4},{4,0},{8,12},{12,8},{16,20},{20,16},{24,28},{28,24},{1,5},{5... | collective-permute-start | bytes 393224 | tf_op jit(solution)/shard_map/ppermute | solution.py:488
  61.6 6.5 %collective-permute-start.15 = (f32[2,8,2048]{2,1,0:T(8,128)S(1)}, f32[2,8,2048]{2,1,0:T(8,128)S(1)}, u32[]{:S(2)}, u32[]{:S(2)}) collective-permute-start(f32[2,8,2048]{2,1,0:T(8,128)S(1)} %pad_maximum_fusion.4), channel_id=1, source_target_pairs={{0,4},{4,0},{8,12},{12,8},{16,20},{20,16},{24,28},{28,24},{1,5},{5... | collective-permute-start | bytes 393224 | tf_op jit(solution)/shard_map/ppermute | solution.py:488
  75.0 6.5 %collective-permute-start.24 = (f32[2,8,2176]{2,1,0:T(8,128)S(1)}, f32[2,8,2176]{2,1,0:T(8,128)S(1)}, u32[]{:S(2)}, u32[]{:S(2)}) collective-permute-start(f32[2,8,2176]{2,1,0:T(8,128)S(1)} %get-tuple-element.53), channel_id=1, source_target_pairs={{0,4},{4,0},{8,12},{12,8},{16,20},{20,16},{24,28},{28,24},{1,5},{5... | collective-permute-start | bytes 417800 | tf_op jit(solution)/shard_map/ppermute | solution.py:488
  77.0 6.8 %collective-permute-start.22 = (f32[2,8,2176]{2,1,0:T(8,128)S(1)}, f32[2,8,2176]{2,1,0:T(8,128)S(1)}, u32[]{:S(2)}, u32[]{:S(2)}) collective-permute-start(f32[2,8,2176]{2,1,0:T(8,128)S(1)} %near_across_0.1), channel_id=1, source_target_pairs={{0,4},{4,0},{8,12},{12,8},{16,20},{20,16},{24,28},{28,24},{1,5},{5... | collective-permute-start | bytes 417800 | tf_op jit(solution)/shard_map/ppermute | solution.py:488
  81.6 6.1 %collective-permute-start.25 = (f32[8,2176]{1,0:T(8,128)S(1)}, f32[8,2176]{1,0:T(8,128)S(1)}, u32[]{:S(2)}, u32[]{:S(2)}) collective-permute-start(f32[8,2176]{1,0:T(8,128)S(1)} %get-tuple-element.54), channel_id=1, source_target_pairs={{0,16},{4,20},{8,24},{12,28},{16,0},{20,4},{24,8},{28,12},{1,17},{... | collective-permute-start | bytes 208904 | tf_op jit(solution)/shard_map/ppermute | solution.py:488
  82.8 6.3 %collective-permute-start.26 = (f32[8,2176]{1,0:T(8,128)S(1)}, f32[8,2176]{1,0:T(8,128)S(1)}, u32[]{:S(2)}, u32[]{:S(2)}) collective-permute-start(f32[8,2176]{1,0:T(8,128)S(1)} %get-tuple-element.55), channel_id=1, source_target_pairs={{0,24},{4,28},{8,16},{12,20},{16,8},{20,12},{24,0},{28,4},{1,25},{... | collective-permute-start | bytes 208904 | tf_op jit(solution)/shard_map/ppermute | solution.py:488
  89.4 7.0 %collective-permute-start.30 = (f32[8,2176]{1,0:T(8,128)S(1)}, f32[8,2176]{1,0:T(8,128)S(1)}, u32[]{:S(2)}, u32[]{:S(2)}) collective-permute-start(f32[8,2176]{1,0:T(8,128)S(1)} %combine_0.1.refs_0_.refs_4_), channel_id=1, source_target_pairs={{0,16},{4,20},{8,24},{12,28},{16,0},{20,4},{24,8},{28,12},{1,17},{... | collective-permute-start | bytes 208904 | tf_op jit(solution)/shard_map/ppermute | solution.py:488
  90.8 7.0 %collective-permute-start.27 = (f32[8,2176]{1,0:T(8,128)S(1)}, f32[8,2176]{1,0:T(8,128)S(1)}, u32[]{:S(2)}, u32[]{:S(2)}) collective-permute-start(f32[8,2176]{1,0:T(8,128)S(1)} %combine_0.1.refs_0_.refs_4_), channel_id=1, source_target_pairs={{0,8},{4,12},{8,0},{12,4},{16,24},{20,28},{24,16},{28,20},{1,9},{5... | collective-permute-start | bytes 208904 | tf_op jit(solution)/shard_map/ppermute | solution.py:488
  92.2 6.1 %collective-permute-start.28 = (f32[8,2176]{1,0:T(8,128)S(1)}, f32[8,2176]{1,0:T(8,128)S(1)}, u32[]{:S(2)}, u32[]{:S(2)}) collective-permute-start(f32[8,2176]{1,0:T(8,128)S(1)} %combine_0.1.refs_0_.refs_4_), channel_id=1, source_target_pairs={{0,24},{4,28},{8,16},{12,20},{16,8},{20,12},{24,0},{28,4},{1,25},{... | collective-permute-start | bytes 208904 | tf_op jit(solution)/shard_map/ppermute | solution.py:488
  96.4 5.8 %collective-permute-start.31 = (f32[2,8,2176]{2,1,0:T(8,128)S(1)}, f32[2,8,2176]{2,1,0:T(8,128)S(1)}, u32[]{:S(2)}, u32[]{:S(2)}) collective-permute-start(f32[2,8,2176]{2,1,0:T(8,128)S(1)} %pad_maximum_fusion.1), channel_id=1, source_target_pairs={{0,4},{4,0},{8,12},{12,8},{16,20},{20,16},{24,28},{28,24},{1,5},{5... | collective-permute-start | bytes 417800 | tf_op jit(solution)/shard_map/ppermute | solution.py:488
  110.0 6.5 %collective-permute-start.37 = (f32[2,8,2176]{2,1,0:T(8,128)S(1)}, f32[2,8,2176]{2,1,0:T(8,128)S(1)}, u32[]{:S(2)}, u32[]{:S(2)}) collective-permute-start(f32[2,8,2176]{2,1,0:T(8,128)S(1)} %get-tuple-element.61), channel_id=1, source_target_pairs={{0,4},{4,0},{8,12},{12,8},{16,20},{20,16},{24,28},{28,24},{1,5},{5... | collective-permute-start | bytes 417800 | tf_op jit(solution)/shard_map/ppermute | solution.py:488
  111.7 7.1 %collective-permute-start.35 = (f32[2,8,2176]{2,1,0:T(8,128)S(1)}, f32[2,8,2176]{2,1,0:T(8,128)S(1)}, u32[]{:S(2)}, u32[]{:S(2)}) collective-permute-start(f32[2,8,2176]{2,1,0:T(8,128)S(1)} %near_across_1.1), channel_id=1, source_target_pairs={{0,4},{4,0},{8,12},{12,8},{16,20},{20,16},{24,28},{28,24},{1,5},{5... | collective-permute-start | bytes 417800 | tf_op jit(solution)/shard_map/ppermute | solution.py:488
  116.6 6.6 %collective-permute-start.38 = (f32[8,2176]{1,0:T(8,128)S(1)}, f32[8,2176]{1,0:T(8,128)S(1)}, u32[]{:S(2)}, u32[]{:S(2)}) collective-permute-start(f32[8,2176]{1,0:T(8,128)S(1)} %get-tuple-element.62), channel_id=1, source_target_pairs={{0,16},{4,20},{8,24},{12,28},{16,0},{20,4},{24,8},{28,12},{1,17},{... | collective-permute-start | bytes 208904 | tf_op jit(solution)/shard_map/ppermute | solution.py:488
  116.7 6.5 %collective-permute-start.39 = (f32[8,2176]{1,0:T(8,128)S(1)}, f32[8,2176]{1,0:T(8,128)S(1)}, u32[]{:S(2)}, u32[]{:S(2)}) collective-permute-start(f32[8,2176]{1,0:T(8,128)S(1)} %get-tuple-element.63), channel_id=1, source_target_pairs={{0,24},{4,28},{8,16},{12,20},{16,8},{20,12},{24,0},{28,4},{1,25},{... | collective-permute-start | bytes 208904 | tf_op jit(solution)/shard_map/ppermute | solution.py:488
  124.9 6.1 %collective-permute-start.42 = (f32[8,2176]{1,0:T(8,128)S(1)}, f32[8,2176]{1,0:T(8,128)S(1)}, u32[]{:S(2)}, u32[]{:S(2)}) collective-permute-start(f32[8,2176]{1,0:T(8,128)S(1)} %combine_1.1.refs_0_), channel_id=1, source_target_pairs={{0,24},{4,28},{8,16},{12,20},{16,8},{20,12},{24,0},{28,4},{1,25},{... | collective-permute-start | bytes 208904 | tf_op jit(solution)/shard_map/ppermute | solution.py:488
  126.6 5.9 %collective-permute-start.41 = (f32[8,2176]{1,0:T(8,128)S(1)}, f32[8,2176]{1,0:T(8,128)S(1)}, u32[]{:S(2)}, u32[]{:S(2)}) collective-permute-start(f32[8,2176]{1,0:T(8,128)S(1)} %combine_1.1.refs_0_), channel_id=1, source_target_pairs={{0,16},{4,20},{8,24},{12,28},{16,0},{20,4},{24,8},{28,12},{1,17},{... | collective-permute-start | bytes 208904 | tf_op jit(solution)/shard_map/ppermute | solution.py:488
  (31 other events, 130.5 us)

commit v9 on v8

--- a/solution.py
+++ b/solution.py
@@ -301,7 +301,7 @@
     rows, px = lax.axis_size("rows"), lax.axis_size("px")
     per = rows // px
     got = [to_readers(piece, turn) for turn in range(px)]
-    halves = [range(1, px, 2), range(0, px, 2)]
+    halves = [range(1, px - 1), [0, px - 1]]
     packs = [jnp.stack([got[t] for t in half]) for half in halves]
     groups = [([got[t] for t in half], [(t * per,) for t in half]) for half in halves]
     for k in range(1, per):

time: 143 us -> 142 us (level)
  transfers between devices with their start and end apart: 48 -> 48, of which waited for: 30 -> 29; matrix products, arithmetic and copies ran while one was open for 0% -> 0% of each run, Pallas kernels for 18% -> 18%
where the time goes in v9:
time: 142 us
  starting transfers between devices  58.4 us (41%)
  Pallas kernels  41.9 us (30%)
  waiting for transfers between devices  41.6 us (29%)
    ppermute x44, starting transfers between devices, exchange(): lax.ppermute(x, axis, [(i, i ^ flip) for i in range(lax.axis_size(axis))])  50.1 us
    pallas_call x39, Pallas kernels, call(): pl.pallas_call(kernel, in_specs=in_specs or [vmem()] * len(args), out_spe...  41.9 us
    ppermute x44, waiting for transfers between devices, exchange(): lax.ppermute(x, axis, [(i, i ^ flip) for i in range(lax.axis_size(axis))])  41.2 us
    ppermute x4, starting transfers between devices, to_readers(): return lax.ppermute(x, ('rows', 'px'), pairs)  8.29 us
  transfers between devices with their start and end apart: 48, of which 29 were waited for; matrix products, arithmetic and copies ran while one was open for 0% of the time, Pallas kernels for 18%

profile of v9, /device:TPU:0, one launch (start us, length us, event | category | flops | bytes accessed | tf_op | source)
XLA Modules:
  0.0 142.3 jit_solution(1743847151048898109)
XLA Ops:
  0.0 6.3 %load_project.1 = (f32[8,1024]{1,0:T(8,128)S(1)}, f32[8,8192]{1,0:T(8,128)S(1)}, bf16[4096,1024]{1,0:T(8,128)(2,1)S(1)}, bf16[4096,1024]{1,0:T(8,128)(2,1)S(1)},...) custom-call(f32[8,8192]{1,0:T(8,128)} %q_hbm.1, f32[1,8192]{1,0:T(1,128)} %bitcast.52, bf16[8192,1024]{1,0:T(8,128)(2,1)} %e_hbm.1, ...), custom_call_target="tpu_custom_call" | custom-call | flops 134217728 | bytes 16777216 | tf_op jit(solution)/shard_map/load_project/pallas_call | solution.py:42
  6.3 5.1 %collective-permute-start = (f32[8,1024]{1,0:T(8,128)S(1)}, f32[8,1024]{1,0:T(8,128)S(1)}, u32[]{:S(2)}, u32[]{:S(2)}) collective-permute-start(f32[8,1024]{1,0:T(8,128)S(1)} %get-tuple-element.35.anchor), channel_id=1, source_target_pairs={{0,24},{4,28},{8,16},{12,20},{16,8},{20,12},{24,0},{28,4},{1,25},{... | collective-permute-start | bytes 98312 | tf_op jit(solution)/shard_map/ppermute | solution.py:488
  12.1 2.4 %turn_theirs.1.half = bf16[1024,4096]{1,0:T(8,128)(2,1)S(1)} custom-call(f32[8,1024]{1,0:T(8,128)S(1)} %get-tuple-element.35.anchor, bf16[4096,1024]{1,0:T(8,128)(2,1)S(1)} %get-tuple-element.36.half), custom_call_target="tpu_custom_call" | custom-call | flops 4194304 | bytes 16777216 | tf_op jit(solution)/shard_map/turn_theirs/pallas_call | solution.py:42
  17.9 2.4 %turn_mine.1.half = bf16[1024,4096]{1,0:T(8,128)(2,1)S(1)} custom-call(f32[8,1024]{1,0:T(8,128)S(1)} %get-tuple-element.35.anchor, bf16[4096,1024]{1,0:T(8,128)(2,1)S(1)} %get-tuple-element.40.half), custom_call_target="tpu_custom_call" | custom-call | flops 4194304 | bytes 16777216 | tf_op jit(solution)/shard_map/turn_mine/pallas_call | solution.py:42
  24.6 4.6 %norms.1.refs_5_ = f32[1,512]{1,0:T(1,128)S(1)} custom-call(bf16[512,16384]{1,0:T(8,128)(2,1)S(1)} %bitcast.26), custom_call_target="tpu_custom_call" | custom-call | flops 16777216 | bytes 16777216 | tf_op jit(solution)/shard_map/norms/pallas_call | solution.py:42
  30.8 2.3 %project_rest.1 = f32[8,1024]{1,0:T(8,128)S(1)} custom-call(f32[8,4096]{1,0:T(8,128)S(1)} %collective-permute-done.6.off, f32[8,1024]{1,0:T(8,128)S(1)} %project_own.1.own, bf16[1024,4096]{1,0:T(8,128)(2,1)S(1)} %turn_theirs.1.half), custom_call_target="tpu_custom_call" | custom-call | flops 67108864 | bytes 16777216 | tf_op jit(solution)/shard_map/project_rest/pallas_call | solution.py:42
  33.1 2.0 %collective-permute-start.7 = (f32[8,1024]{1,0:T(8,128)S(1)}, f32[8,1024]{1,0:T(8,128)S(1)}, u32[]{:S(2)}, u32[]{:S(2)}) collective-permute-start(f32[8,1024]{1,0:T(8,128)S(1)} %project_rest.1), channel_id=1, source_target_pairs={{0,24},{4,28},{8,16},{12,20},{16,8},{20,12},{24,0},{28,4},{1,25},{... | collective-permute-start | bytes 98312 | tf_op jit(solution)/shard_map/ppermute | solution.py:488
  35.2 2.3 %collective-permute-start.9 = (f32[8,1024]{1,0:T(8,128)S(1)}, f32[8,1024]{1,0:T(8,128)S(1)}, u32[]{:S(2)}, u32[]{:S(2)}) collective-permute-start(f32[8,1024]{1,0:T(8,128)S(1)} %project_rest.1), channel_id=1, source_target_pairs={{0,8},{4,12},{8,0},{12,4},{16,24},{20,28},{24,16},{28,20},{1,9},{5... | collective-permute-start | bytes 98312 | tf_op jit(solution)/shard_map/ppermute | solution.py:488
  41.8 2.5 %collective-permute-done.10 = f32[8,1024]{1,0:T(8,128)S(1)} collective-permute-done((f32[8,1024]{1,0:T(8,128)S(1)}, f32[8,1024]{1,0:T(8,128)S(1)}, u32[]{:S(2)}, u32[]{:S(2)}) %collective-permute-start.10) | collective-permute-done | bytes 32800 | tf_op jit(solution)/shard_map/ppermute | solution.py:488
  48.8 2.4 %collective-permute-done.12.given = f32[8,2048]{1,0:T(8,128)S(1)} collective-permute-done((f32[8,2048]{1,0:T(8,128)S(1)}, f32[8,2048]{1,0:T(8,128)S(1)}, u32[]{:S(2)}, u32[]{:S(2)}) %collective-permute-start.12) | collective-permute-done | bytes 65568 | tf_op jit(solution)/shard_map/ppermute | solution.py:488
  52.5 2.1 %collective-permute-start.17 = (f32[8,2048]{1,0:T(8,128)S(1)}, f32[8,2048]{1,0:T(8,128)S(1)}, u32[]{:S(2)}, u32[]{:S(2)}) collective-permute-start(f32[8,2048]{1,0:T(8,128)S(1)} %second_update.1), channel_id=1, source_target_pairs={{0,16},{1,24},{2,0},{3,8},{4,20},{5,28},{6,4},{7,12},{8,17},{9,25}... | collective-permute-start | bytes 196616 | tf_op jit(solution)/shard_map/ppermute | solution.py:513
  55.3 4.4 %collective-permute-start.14 = (f32[8,2048]{1,0:T(8,128)S(1)}, f32[8,2048]{1,0:T(8,128)S(1)}, u32[]{:S(2)}, u32[]{:S(2)}) collective-permute-start(f32[8,2048]{1,0:T(8,128)S(1)} %second_update.1), channel_id=1, source_target_pairs={{0,24},{1,16},{2,8},{3,0},{4,28},{5,20},{6,12},{7,4},{8,25},{9,17}... | collective-permute-start | bytes 196616 | tf_op jit(solution)/shard_map/ppermute | solution.py:513
  69.1 1.9 %collective-permute-start.19 = (f32[16,512]{1,0:T(8,128)S(1)}, f32[16,512]{1,0:T(8,128)S(1)}, u32[]{:S(2)}, u32[]{:S(2)}) collective-permute-start(f32[16,512]{1,0:T(8,128)S(1)} %dots_0_3.1.g0), channel_id=1, source_target_pairs={{0,2},{1,3},{2,0},{3,1},{4,6},{5,7},{6,4},{7,5},{8,10},{9,11},{10,... | collective-permute-start | bytes 98312 | tf_op jit(solution)/shard_map/ppermute | solution.py:488
  71.3 1.8 %collective-permute-done.19.g1 = f32[16,512]{1,0:T(8,128)S(1)} collective-permute-done((f32[16,512]{1,0:T(8,128)S(1)}, f32[16,512]{1,0:T(8,128)S(1)}, u32[]{:S(2)}, u32[]{:S(2)}) %collective-permute-start.19) | collective-permute-done | bytes 32800 | tf_op jit(solution)/shard_map/ppermute | solution.py:488
  79.2 2.3 %collective-permute-done.24.theirs = f32[2,8,2176]{2,1,0:T(8,128)S(1)} collective-permute-done((f32[2,8,2176]{2,1,0:T(8,128)S(1)}, f32[2,8,2176]{2,1,0:T(8,128)S(1)}, u32[]{:S(2)}, u32[]{:S(2)}) %collective-permute-start.24) | collective-permute-done | bytes 139296 | tf_op jit(solution)/shard_map/ppermute | solution.py:488
  81.9 2.4 %collective-permute-start.26 = (f32[8,2176]{1,0:T(8,128)S(1)}, f32[8,2176]{1,0:T(8,128)S(1)}, u32[]{:S(2)}, u32[]{:S(2)}) collective-permute-start(f32[8,2176]{1,0:T(8,128)S(1)} %get-tuple-element.55), channel_id=1, source_target_pairs={{0,24},{4,28},{8,16},{12,20},{16,8},{20,12},{24,0},{28,4},{1,25},{... | collective-permute-start | bytes 208904 | tf_op jit(solution)/shard_map/ppermute | solution.py:488
  85.3 2.9 %collective-permute-done.25.refs_2_ = f32[8,2176]{1,0:T(8,128)S(1)} collective-permute-done((f32[8,2176]{1,0:T(8,128)S(1)}, f32[8,2176]{1,0:T(8,128)S(1)}, u32[]{:S(2)}, u32[]{:S(2)}) %collective-permute-start.25) | collective-permute-done | bytes 69664 | tf_op jit(solution)/shard_map/ppermute | solution.py:488
  93.5 2.0 %collective-permute-done.30.refs_0_ = f32[8,2176]{1,0:T(8,128)S(1)} collective-permute-done((f32[8,2176]{1,0:T(8,128)S(1)}, f32[8,2176]{1,0:T(8,128)S(1)}, u32[]{:S(2)}, u32[]{:S(2)}) %collective-permute-start.30) | collective-permute-done | bytes 69664 | tf_op jit(solution)/shard_map/ppermute | solution.py:488
  113.6 2.5 %collective-permute-done.37.theirs = f32[2,8,2176]{2,1,0:T(8,128)S(1)} collective-permute-done((f32[2,8,2176]{2,1,0:T(8,128)S(1)}, f32[2,8,2176]{2,1,0:T(8,128)S(1)}, u32[]{:S(2)}, u32[]{:S(2)}) %collective-permute-start.37) | collective-permute-done | bytes 139296 | tf_op jit(solution)/shard_map/ppermute | solution.py:488
  116.3 2.0 %collective-permute-start.39 = (f32[8,2176]{1,0:T(8,128)S(1)}, f32[8,2176]{1,0:T(8,128)S(1)}, u32[]{:S(2)}, u32[]{:S(2)}) collective-permute-start(f32[8,2176]{1,0:T(8,128)S(1)} %get-tuple-element.63), channel_id=1, source_target_pairs={{0,24},{4,28},{8,16},{12,20},{16,8},{20,12},{24,0},{28,4},{1,25},{... | collective-permute-start | bytes 208904 | tf_op jit(solution)/shard_map/ppermute | solution.py:488
  119.9 2.8 %collective-permute-done.38.refs_2_ = f32[8,2176]{1,0:T(8,128)S(1)} collective-permute-done((f32[8,2176]{1,0:T(8,128)S(1)}, f32[8,2176]{1,0:T(8,128)S(1)}, u32[]{:S(2)}, u32[]{:S(2)}) %collective-permute-start.38) | collective-permute-done | bytes 69664 | tf_op jit(solution)/shard_map/ppermute | solution.py:488
  124.5 1.9 %collective-permute-start.42 = (f32[8,2176]{1,0:T(8,128)S(1)}, f32[8,2176]{1,0:T(8,128)S(1)}, u32[]{:S(2)}, u32[]{:S(2)}) collective-permute-start(f32[8,2176]{1,0:T(8,128)S(1)} %combine_1.1.refs_0_), channel_id=1, source_target_pairs={{0,24},{4,28},{8,16},{12,20},{16,8},{20,12},{24,0},{28,4},{1,25},{... | collective-permute-start | bytes 208904 | tf_op jit(solution)/shard_map/ppermute | solution.py:488
  128.7 1.9 %collective-permute-done.42.refs_3_ = f32[8,2176]{1,0:T(8,128)S(1)} collective-permute-done((f32[8,2176]{1,0:T(8,128)S(1)}, f32[8,2176]{1,0:T(8,128)S(1)}, u32[]{:S(2)}, u32[]{:S(2)}) %collective-permute-start.42) | collective-permute-done | bytes 69664 | tf_op jit(solution)/shard_map/ppermute | solution.py:488
  133.6 2.1 %collective-permute-done.44.refs_5_ = f32[2,8,2176]{2,1,0:T(8,128)S(1)} collective-permute-done((f32[2,8,2176]{2,1,0:T(8,128)S(1)}, f32[2,8,2176]{2,1,0:T(8,128)S(1)}, u32[]{:S(2)}, u32[]{:S(2)}) %collective-permute-start.44) | collective-permute-done | bytes 139296 | tf_op jit(solution)/shard_map/ppermute | solution.py:488
  (139 shorter events, 76.7 us)
Async XLA Ops:
  6.3 8.2 %collective-permute-start = (f32[8,1024]{1,0:T(8,128)S(1)}, f32[8,1024]{1,0:T(8,128)S(1)}, u32[]{:S(2)}, u32[]{:S(2)}) collective-permute-start(f32[8,1024]{1,0:T(8,128)S(1)} %get-tuple-element.35.anchor), channel_id=1, source_target_pairs={{0,24},{4,28},{8,16},{12,20},{16,8},{20,12},{24,0},{28,4},{1,25},{... | collective-permute-start | bytes 98312 | tf_op jit(solution)/shard_map/ppermute | solution.py:488
  23.0 6.2 %collective-permute-start.5 = (f32[8,4096]{1,0:T(8,128)S(1)}, f32[8,4096]{1,0:T(8,128)S(1)}, u32[]{:S(2)}, u32[]{:S(2)}) collective-permute-start(f32[8,4096]{1,0:T(8,128)S(1)} %add.24.mine), channel_id=1, source_target_pairs={{0,2},{1,3},{2,0},{3,1},{4,6},{5,7},{6,4},{7,5},{8,10},{9,11},{10,... | collective-permute-start | bytes 393224 | tf_op jit(solution)/shard_map/ppermute | solution.py:488
  33.1 5.9 %collective-permute-start.7 = (f32[8,1024]{1,0:T(8,128)S(1)}, f32[8,1024]{1,0:T(8,128)S(1)}, u32[]{:S(2)}, u32[]{:S(2)}) collective-permute-start(f32[8,1024]{1,0:T(8,128)S(1)} %project_rest.1), channel_id=1, source_target_pairs={{0,24},{4,28},{8,16},{12,20},{16,8},{20,12},{24,0},{28,4},{1,25},{... | collective-permute-start | bytes 98312 | tf_op jit(solution)/shard_map/ppermute | solution.py:488
  35.1 5.2 %collective-permute-start.8 = (f32[8,1024]{1,0:T(8,128)S(1)}, f32[8,1024]{1,0:T(8,128)S(1)}, u32[]{:S(2)}, u32[]{:S(2)}) collective-permute-start(f32[8,1024]{1,0:T(8,128)S(1)} %project_rest.1), channel_id=1, source_target_pairs={{0,16},{4,20},{8,24},{12,28},{16,0},{20,4},{24,8},{28,12},{1,17},{... | collective-permute-start | bytes 98312 | tf_op jit(solution)/shard_map/ppermute | solution.py:488
  51.4 8.3 %collective-permute-start.16 = (f32[8,2048]{1,0:T(8,128)S(1)}, f32[8,2048]{1,0:T(8,128)S(1)}, u32[]{:S(2)}, u32[]{:S(2)}) collective-permute-start(f32[8,2048]{1,0:T(8,128)S(1)} %second_update.1), channel_id=1, source_target_pairs={{0,8},{1,0},{2,24},{3,16},{4,12},{5,4},{6,28},{7,20},{8,9},{9,1},{... | collective-permute-start | bytes 196616 | tf_op jit(solution)/shard_map/ppermute | solution.py:513
  52.5 7.1 %collective-permute-start.17 = (f32[8,2048]{1,0:T(8,128)S(1)}, f32[8,2048]{1,0:T(8,128)S(1)}, u32[]{:S(2)}, u32[]{:S(2)}) collective-permute-start(f32[8,2048]{1,0:T(8,128)S(1)} %second_update.1), channel_id=1, source_target_pairs={{0,16},{1,24},{2,0},{3,8},{4,20},{5,28},{6,4},{7,12},{8,17},{9,25}... | collective-permute-start | bytes 196616 | tf_op jit(solution)/shard_map/ppermute | solution.py:513
  54.6 6.6 %collective-permute-start.13 = (f32[8,2048]{1,0:T(8,128)S(1)}, f32[8,2048]{1,0:T(8,128)S(1)}, u32[]{:S(2)}, u32[]{:S(2)}) collective-permute-start(f32[8,2048]{1,0:T(8,128)S(1)} %second_update.1), channel_id=1, source_target_pairs={{0,0},{1,8},{2,16},{3,24},{4,4},{5,12},{6,20},{7,28},{8,1},{9,9},{... | collective-permute-start | bytes 196616 | tf_op jit(solution)/shard_map/ppermute | solution.py:513
  55.3 6.3 %collective-permute-start.14 = (f32[8,2048]{1,0:T(8,128)S(1)}, f32[8,2048]{1,0:T(8,128)S(1)}, u32[]{:S(2)}, u32[]{:S(2)}) collective-permute-start(f32[8,2048]{1,0:T(8,128)S(1)} %second_update.1), channel_id=1, source_target_pairs={{0,24},{1,16},{2,8},{3,0},{4,28},{5,20},{6,12},{7,4},{8,25},{9,17}... | collective-permute-start | bytes 196616 | tf_op jit(solution)/shard_map/ppermute | solution.py:513
  59.7 6.4 %collective-permute-start.18 = (f32[2,8,2048]{2,1,0:T(8,128)S(1)}, f32[2,8,2048]{2,1,0:T(8,128)S(1)}, u32[]{:S(2)}, u32[]{:S(2)}) collective-permute-start(f32[2,8,2048]{2,1,0:T(8,128)S(1)} %pad_maximum_fusion.5), channel_id=1, source_target_pairs={{0,4},{4,0},{8,12},{12,8},{16,20},{20,16},{24,28},{28,24},{1,5},{5... | collective-permute-start | bytes 393224 | tf_op jit(solution)/shard_map/ppermute | solution.py:488
  61.6 6.3 %collective-permute-start.15 = (f32[2,8,2048]{2,1,0:T(8,128)S(1)}, f32[2,8,2048]{2,1,0:T(8,128)S(1)}, u32[]{:S(2)}, u32[]{:S(2)}) collective-permute-start(f32[2,8,2048]{2,1,0:T(8,128)S(1)} %pad_maximum_fusion.4), channel_id=1, source_target_pairs={{0,4},{4,0},{8,12},{12,8},{16,20},{20,16},{24,28},{28,24},{1,5},{5... | collective-permute-start | bytes 393224 | tf_op jit(solution)/shard_map/ppermute | solution.py:488
  75.2 6.3 %collective-permute-start.24 = (f32[2,8,2176]{2,1,0:T(8,128)S(1)}, f32[2,8,2176]{2,1,0:T(8,128)S(1)}, u32[]{:S(2)}, u32[]{:S(2)}) collective-permute-start(f32[2,8,2176]{2,1,0:T(8,128)S(1)} %get-tuple-element.53), channel_id=1, source_target_pairs={{0,4},{4,0},{8,12},{12,8},{16,20},{20,16},{24,28},{28,24},{1,5},{5... | collective-permute-start | bytes 417800 | tf_op jit(solution)/shard_map/ppermute | solution.py:488
  77.1 7.1 %collective-permute-start.22 = (f32[2,8,2176]{2,1,0:T(8,128)S(1)}, f32[2,8,2176]{2,1,0:T(8,128)S(1)}, u32[]{:S(2)}, u32[]{:S(2)}) collective-permute-start(f32[2,8,2176]{2,1,0:T(8,128)S(1)} %near_across_0.1), channel_id=1, source_target_pairs={{0,4},{4,0},{8,12},{12,8},{16,20},{20,16},{24,28},{28,24},{1,5},{5... | collective-permute-start | bytes 417800 | tf_op jit(solution)/shard_map/ppermute | solution.py:488
  81.6 6.6 %collective-permute-start.25 = (f32[8,2176]{1,0:T(8,128)S(1)}, f32[8,2176]{1,0:T(8,128)S(1)}, u32[]{:S(2)}, u32[]{:S(2)}) collective-permute-start(f32[8,2176]{1,0:T(8,128)S(1)} %get-tuple-element.54), channel_id=1, source_target_pairs={{0,16},{4,20},{8,24},{12,28},{16,0},{20,4},{24,8},{28,12},{1,17},{... | collective-permute-start | bytes 208904 | tf_op jit(solution)/shard_map/ppermute | solution.py:488
  81.9 6.3 %collective-permute-start.26 = (f32[8,2176]{1,0:T(8,128)S(1)}, f32[8,2176]{1,0:T(8,128)S(1)}, u32[]{:S(2)}, u32[]{:S(2)}) collective-permute-start(f32[8,2176]{1,0:T(8,128)S(1)} %get-tuple-element.55), channel_id=1, source_target_pairs={{0,24},{4,28},{8,16},{12,20},{16,8},{20,12},{24,0},{28,4},{1,25},{... | collective-permute-start | bytes 208904 | tf_op jit(solution)/shard_map/ppermute | solution.py:488
  89.1 6.4 %collective-permute-start.30 = (f32[8,2176]{1,0:T(8,128)S(1)}, f32[8,2176]{1,0:T(8,128)S(1)}, u32[]{:S(2)}, u32[]{:S(2)}) collective-permute-start(f32[8,2176]{1,0:T(8,128)S(1)} %combine_0.1.refs_0_.refs_4_), channel_id=1, source_target_pairs={{0,16},{4,20},{8,24},{12,28},{16,0},{20,4},{24,8},{28,12},{1,17},{... | collective-permute-start | bytes 208904 | tf_op jit(solution)/shard_map/ppermute | solution.py:488
  90.3 6.7 %collective-permute-start.27 = (f32[8,2176]{1,0:T(8,128)S(1)}, f32[8,2176]{1,0:T(8,128)S(1)}, u32[]{:S(2)}, u32[]{:S(2)}) collective-permute-start(f32[8,2176]{1,0:T(8,128)S(1)} %combine_0.1.refs_0_.refs_4_), channel_id=1, source_target_pairs={{0,8},{4,12},{8,0},{12,4},{16,24},{20,28},{24,16},{28,20},{1,9},{5... | collective-permute-start | bytes 208904 | tf_op jit(solution)/shard_map/ppermute | solution.py:488
  91.8 6.1 %collective-permute-start.28 = (f32[8,2176]{1,0:T(8,128)S(1)}, f32[8,2176]{1,0:T(8,128)S(1)}, u32[]{:S(2)}, u32[]{:S(2)}) collective-permute-start(f32[8,2176]{1,0:T(8,128)S(1)} %combine_0.1.refs_0_.refs_4_), channel_id=1, source_target_pairs={{0,24},{4,28},{8,16},{12,20},{16,8},{20,12},{24,0},{28,4},{1,25},{... | collective-permute-start | bytes 208904 | tf_op jit(solution)/shard_map/ppermute | solution.py:488
  95.6 6.2 %collective-permute-start.31 = (f32[2,8,2176]{2,1,0:T(8,128)S(1)}, f32[2,8,2176]{2,1,0:T(8,128)S(1)}, u32[]{:S(2)}, u32[]{:S(2)}) collective-permute-start(f32[2,8,2176]{2,1,0:T(8,128)S(1)} %pad_maximum_fusion.1), channel_id=1, source_target_pairs={{0,4},{4,0},{8,12},{12,8},{16,20},{20,16},{24,28},{28,24},{1,5},{5... | collective-permute-start | bytes 417800 | tf_op jit(solution)/shard_map/ppermute | solution.py:488
  109.6 6.5 %collective-permute-start.37 = (f32[2,8,2176]{2,1,0:T(8,128)S(1)}, f32[2,8,2176]{2,1,0:T(8,128)S(1)}, u32[]{:S(2)}, u32[]{:S(2)}) collective-permute-start(f32[2,8,2176]{2,1,0:T(8,128)S(1)} %get-tuple-element.61), channel_id=1, source_target_pairs={{0,4},{4,0},{8,12},{12,8},{16,20},{20,16},{24,28},{28,24},{1,5},{5... | collective-permute-start | bytes 417800 | tf_op jit(solution)/shard_map/ppermute | solution.py:488
  111.4 6.8 %collective-permute-start.35 = (f32[2,8,2176]{2,1,0:T(8,128)S(1)}, f32[2,8,2176]{2,1,0:T(8,128)S(1)}, u32[]{:S(2)}, u32[]{:S(2)}) collective-permute-start(f32[2,8,2176]{2,1,0:T(8,128)S(1)} %near_across_1.1), channel_id=1, source_target_pairs={{0,4},{4,0},{8,12},{12,8},{16,20},{20,16},{24,28},{28,24},{1,5},{5... | collective-permute-start | bytes 417800 | tf_op jit(solution)/shard_map/ppermute | solution.py:488
  116.2 6.5 %collective-permute-start.38 = (f32[8,2176]{1,0:T(8,128)S(1)}, f32[8,2176]{1,0:T(8,128)S(1)}, u32[]{:S(2)}, u32[]{:S(2)}) collective-permute-start(f32[8,2176]{1,0:T(8,128)S(1)} %get-tuple-element.62), channel_id=1, source_target_pairs={{0,16},{4,20},{8,24},{12,28},{16,0},{20,4},{24,8},{28,12},{1,17},{... | collective-permute-start | bytes 208904 | tf_op jit(solution)/shard_map/ppermute | solution.py:488
  116.3 6.5 %collective-permute-start.39 = (f32[8,2176]{1,0:T(8,128)S(1)}, f32[8,2176]{1,0:T(8,128)S(1)}, u32[]{:S(2)}, u32[]{:S(2)}) collective-permute-start(f32[8,2176]{1,0:T(8,128)S(1)} %get-tuple-element.63), channel_id=1, source_target_pairs={{0,24},{4,28},{8,16},{12,20},{16,8},{20,12},{24,0},{28,4},{1,25},{... | collective-permute-start | bytes 208904 | tf_op jit(solution)/shard_map/ppermute | solution.py:488
  124.5 6.1 %collective-permute-start.42 = (f32[8,2176]{1,0:T(8,128)S(1)}, f32[8,2176]{1,0:T(8,128)S(1)}, u32[]{:S(2)}, u32[]{:S(2)}) collective-permute-start(f32[8,2176]{1,0:T(8,128)S(1)} %combine_1.1.refs_0_), channel_id=1, source_target_pairs={{0,24},{4,28},{8,16},{12,20},{16,8},{20,12},{24,0},{28,4},{1,25},{... | collective-permute-start | bytes 208904 | tf_op jit(solution)/shard_map/ppermute | solution.py:488
  126.4 6.0 %collective-permute-start.41 = (f32[8,2176]{1,0:T(8,128)S(1)}, f32[8,2176]{1,0:T(8,128)S(1)}, u32[]{:S(2)}, u32[]{:S(2)}) collective-permute-start(f32[8,2176]{1,0:T(8,128)S(1)} %combine_1.1.refs_0_), channel_id=1, source_target_pairs={{0,16},{4,20},{8,24},{12,28},{16,0},{20,4},{24,8},{28,12},{1,17},{... | collective-permute-start | bytes 208904 | tf_op jit(solution)/shard_map/ppermute | solution.py:488
  (31 other events, 129.7 us)
